TPU v7x, 512 devices: a whole 4x8x8 slice. The times are simulated.
512 devices in a mesh: dp: 4 (over x), expert: 128 (over y, z, core).
Axes of the slice: x: 4, y: 8, z: 8, core: 2. Of those that a mesh axis runs over, the one named last changes fastest.
Arguments:
- tokens: bfloat16 [16384, 1024], P(('dp', 'expert')), may hold values from -6 to 6
- cotangent: bfloat16 [16384, 1024], P(('dp', 'expert')), may hold values from -3 to 3
- routes: int32 [16384, 8], P(('dp', 'expert')), may hold values from 0 to 127, as said below
- combine: bfloat16 [16384, 8], P(('dp', 'expert')), may hold values from 0.099609375 to 1
- hot_experts: int32 [4], replicated, may hold values from 0 to 63, as said below
- extra_slots: int32 [4], replicated, may hold values from 1 to 2, as said below
- w_gate: bfloat16 [128, 1024, 384], P('expert'), may hold values from -0.1875 to 0.1875
- w_up: bfloat16 [128, 1024, 384], P('expert'), may hold values from -0.1875 to 0.1875
- w_down: bfloat16 [128, 384, 1024], P('expert'), may hold values from -0.3125 to 0.3125
Outputs:
- token_grads: bfloat16 [16384, 1024], P(('dp', 'expert'))
- grad_gate: bfloat16 [128, 1024, 384], P('expert', 'dp')
- grad_up: bfloat16 [128, 1024, 384], P('expert', 'dp')
- grad_down: bfloat16 [128, 384, 1024], P('expert')
Inputs may be any that keep to these rules, and one draw needn't show every extreme that they name: `routes`: each row names 8 different experts. `hot_experts`: 4 different experts, all below 64. `extra_slots`: one of the entries equals 2.
All inputs are finite; a program needn't handle non-finite values.
Results may differ from a plain program's by a relative error of at most 0.0064.
Values may be sent and summed in bfloat16 or wider, within the bound.
No kernel may reach another device: no remote copies, remote signals or barrier semaphores. Data moves between devices by JAX's collectives and lax.ppermute only.
A program may use at most 64 MiB of HBM per device.

v0:
```python
import jax
import jax.numpy as jnp
from jax import lax
from jax.sharding import PartitionSpec as P


def forward_rows(weight_gate, weight_up, weight_down, row_tokens, row_cotan, row_weights):
    gate_pre = jnp.dot(row_tokens, weight_gate, preferred_element_type=jnp.float32)
    up_proj = jnp.dot(row_tokens, weight_up, preferred_element_type=jnp.float32)
    sigmoid_gate = jax.nn.sigmoid(gate_pre)
    gate_act = gate_pre * sigmoid_gate
    hidden = (gate_act * up_proj).astype(jnp.bfloat16)
    out_grad = (row_weights.astype(jnp.float32)[:, None] * row_cotan.astype(jnp.float32)).astype(
        jnp.bfloat16
    )
    hidden_grad = jnp.dot(out_grad, weight_down.T, preferred_element_type=jnp.float32)
    gate_grad = (
        hidden_grad * up_proj * sigmoid_gate * (1.0 + gate_pre * (1.0 - sigmoid_gate))
    ).astype(jnp.bfloat16)
    up_grad = (hidden_grad * gate_act).astype(jnp.bfloat16)
    row_grads = jnp.dot(gate_grad, weight_gate.T, preferred_element_type=jnp.float32)
    row_grads = row_grads + jnp.dot(up_grad, weight_up.T, preferred_element_type=jnp.float32)
    return (row_grads.astype(jnp.bfloat16), (row_tokens, gate_grad, up_grad, hidden, out_grad))


def weight_terms(pieces):
    row_tokens, gate_grad, up_grad, hidden, out_grad = pieces
    grad_gate = jnp.dot(row_tokens.T, gate_grad, preferred_element_type=jnp.float32)
    grad_up = jnp.dot(row_tokens.T, up_grad, preferred_element_type=jnp.float32)
    grad_down = jnp.dot(hidden.T, out_grad, preferred_element_type=jnp.float32)
    return (grad_gate, grad_up, grad_down)


def expert_pass(weight_gate, weight_up, weight_down, row_tokens, row_cotan, row_weights):
    row_grads, pieces = forward_rows(
        weight_gate, weight_up, weight_down, row_tokens, row_cotan, row_weights
    )
    return (row_grads, weight_terms(pieces))


def shards(tokens, cotangent, routes, combine, hot_experts, extra_slots, w_gate, w_up, w_down):
    expert_count = lax.axis_size("expert")
    token_count, features = tokens.shape
    route_count = routes.shape[1]
    capacity = max(2, min(token_count * route_count * 7 // (8 * expert_count), token_count // 2))
    spare_slots = 2 * max(1, capacity // 6)
    expert_ids = routes.reshape(-1)
    assign_count = expert_ids.shape[0]
    assign_order = jnp.arange(assign_count, dtype=jnp.int32)
    earlier = (expert_ids[:, None] == expert_ids[None, :]) & (
        assign_order[None, :] < assign_order[:, None]
    )
    slot_rank = jnp.sum(earlier.astype(jnp.int32), axis=1)
    hot_match = expert_ids[:, None] == hot_experts[None, :]
    slot_limit = capacity + jnp.sum(jnp.where(hot_match, extra_slots[None, :], 0), axis=1)
    is_kept = slot_rank < slot_limit
    slot_count = capacity + spare_slots
    total_slots = expert_count * slot_count
    flat_slot = jnp.where(is_kept, expert_ids * slot_count + slot_rank, total_slots)
    slot_ids = jnp.arange(total_slots, dtype=jnp.int32)
    assign_onehot = slot_ids[:, None] == flat_slot[None, :]
    token_onehot = jnp.any(
        assign_onehot.reshape(total_slots, token_count, route_count), axis=2
    ).astype(jnp.bfloat16)
    both_rows = jnp.concatenate([tokens, cotangent], axis=1)
    filled = jnp.dot(token_onehot, both_rows, preferred_element_type=jnp.float32).astype(
        jnp.bfloat16
    )
    token_send = filled[:, :features].reshape(expert_count, slot_count, features)
    cotan_send = filled[:, features:].reshape(expert_count, slot_count, features)
    weight_flat = jnp.sum(
        jnp.where(assign_onehot, combine.reshape(-1).astype(jnp.float32)[None, :], 0.0), axis=1
    )
    weight_send = weight_flat.astype(jnp.bfloat16).reshape(expert_count, slot_count)
    token_recv, cotan_recv, weight_recv = (
        lax.all_to_all(token_send, "expert", split_axis=0, concat_axis=0, tiled=True),
        lax.all_to_all(cotan_send, "expert", split_axis=0, concat_axis=0, tiled=True),
        lax.all_to_all(weight_send, "expert", split_axis=0, concat_axis=0, tiled=True),
    )
    own_weights = (w_gate[0], w_up[0], w_down[0])
    all_rows, grad_terms = expert_pass(
        own_weights[0],
        own_weights[1],
        own_weights[2],
        token_recv.reshape(-1, features),
        cotan_recv.reshape(-1, features),
        weight_recv.reshape(-1),
    )
    grad_rows = all_rows.reshape(expert_count, slot_count, features)
    returned_rows = lax.all_to_all(grad_rows, "expert", split_axis=0, concat_axis=0, tiled=True)
    token_grads = jnp.dot(
        token_onehot.T,
        returned_rows.reshape(total_slots, features),
        preferred_element_type=jnp.float32,
    ).astype(jnp.bfloat16)
    grad_gate, grad_up = (
        lax.psum_scatter(grad_terms[0][None], "dp", scatter_dimension=1, tiled=True),
        lax.psum_scatter(grad_terms[1][None], "dp", scatter_dimension=1, tiled=True),
    )
    grad_down = lax.psum(grad_terms[2][None], "dp")
    return (
        token_grads,
        grad_gate.astype(jnp.bfloat16),
        grad_up.astype(jnp.bfloat16),
        grad_down.astype(jnp.bfloat16),
    )


def solution(mesh):
    in_specs = (
        P(("dp", "expert"), None),
        P(("dp", "expert"), None),
        P(("dp", "expert"), None),
        P(("dp", "expert"), None),
        P(),
        P(),
        P("expert", None, None),
        P("expert", None, None),
        P("expert", None, None),
    )
    out_specs = (
        P(("dp", "expert"), None),
        P("expert", "dp", None),
        P("expert", "dp", None),
        P("expert", None, None),
    )
    return jax.shard_map(shards, mesh=mesh, in_specs=in_specs, out_specs=out_specs, check_vma=False)
```

profile of v0, /device:TPU:1, one launch (start us, length us, event | category | flops | bytes accessed | tf_op | source)
XLA Modules:
  0.0 198.6 jit_solution(6270113972711976536)
XLA Ops:
  10.8 18.4 %all-to-all-start = ((bf16[128,1,4]{2,1,0:T(2,128)(2,1)}), bf16[128,1,4]{2,1,0:T(2,128)(2,1)S(1)}, u32[]{:S(2)}, u32[]{:S(2)}) async-start(bf16[128,1,4]{2,1,0:T(2,128)(2,1)} %convert_element_type.116), calls=%async_computation | async-start | bytes 131072 | tf_op jit(solution)/shard_map/all_to_all | solution.py:78
  29.7 1.6 convolution_convert_fusion
  31.5 1.2 reshape.98
  32.8 8.0 %all-to-all-done = bf16[128,1,4]{2,1,0:T(2,128)(2,1)S(1)} async-done(((bf16[128,1,4]{2,1,0:T(2,128)(2,1)}), bf16[128,1,4]{2,1,0:T(2,128)(2,1)S(1)}, u32[]{:S(2)}, u32[]{:S(2)}) %all-to-all-start) | async-done | bytes 1056 | tf_op jit(solution)/shard_map/all_to_all | solution.py:78
  40.7 5.8 %all-to-all-start.1 = ((bf16[128,4,1024]{2,1,0:T(4,128)(2,1)}), bf16[128,4,1024]{2,1,0:T(4,128)(2,1)S(1)}, u32[]{:S(2)}, u32[]{:S(2)}) async-start(bf16[128,4,1024]{2,1,0:T(4,128)(2,1)} %reshape.98), calls=%async_computation.1 | async-start | bytes 2097152 | tf_op jit(solution)/shard_map/all_to_all | solution.py:77
  46.5 1.2 reshape.99
  47.7 29.1 %all-to-all-done.1 = bf16[128,4,1024]{2,1,0:T(4,128)(2,1)S(1)} async-done(((bf16[128,4,1024]{2,1,0:T(4,128)(2,1)}), bf16[128,4,1024]{2,1,0:T(4,128)(2,1)S(1)}, u32[]{:S(2)}, u32[]{:S(2)}) %all-to-all-start.1) | async-done | bytes 1048608 | tf_op jit(solution)/shard_map/all_to_all | solution.py:77
  76.9 7.9 %all-to-all-start.2 = ((bf16[128,4,1024]{2,1,0:T(4,128)(2,1)}), bf16[128,4,1024]{2,1,0:T(4,128)(2,1)}, u32[]{:S(2)}, u32[]{:S(2)}) async-start(bf16[128,4,1024]{2,1,0:T(4,128)(2,1)} %reshape.99), calls=%async_computation.2 | async-start | bytes 2097152 | tf_op jit(solution)/shard_map/all_to_all | solution.py:76
  85.4 1.2 convert_element_type.98
  86.6 28.3 %all-to-all-done.2 = bf16[128,4,1024]{2,1,0:T(4,128)(2,1)} async-done(((bf16[128,4,1024]{2,1,0:T(4,128)(2,1)}), bf16[128,4,1024]{2,1,0:T(4,128)(2,1)}, u32[]{:S(2)}, u32[]{:S(2)}) %all-to-all-start.2) | async-done | bytes 1048608 | tf_op jit(solution)/shard_map/all_to_all | solution.py:76
  114.8 1.3 reshape.100
  118.1 1.6 multiply_convert_fusion.4
  119.7 1.9 convolution_bitcast_fusion.1
  121.9 2.9 %convolution_bitcast_fusion.2 = f32[1,1024,384]{2,1,0:T(8,128)} fusion(bf16[512,1024]{1,0:T(8,128)(2,1)S(1)} %reshape.100, bf16[512,384]{1,0:T(8,128)(2,1)} %get-tuple-element.7), kind=kOutput, calls=%fused_computation.6 | convolution fusion | flops 402653184 | bytes 3014656 | tf_op jit(solution)/shard_map/dot_general | solution.py:28
  124.8 1.8 fusion.1
  127.4 1.2 reshape.101
  128.6 7.1 %all-to-all-start.3 = ((bf16[128,4,1024]{2,1,0:T(4,128)(2,1)}), bf16[128,4,1024]{2,1,0:T(4,128)(2,1)S(1)}, u32[]{:S(2)}, u32[]{:S(2)}) async-start(bf16[128,4,1024]{2,1,0:T(4,128)(2,1)} %reshape.101), calls=%async_computation.3 | async-start | bytes 2097152 | tf_op jit(solution)/shard_map/all_to_all | solution.py:90
  136.0 1.5 reshape.106
  137.4 4.0 %convolution_bitcast_fusion = f32[1,384,1024]{2,1,0:T(8,128)} fusion(f32[512,1024]{1,0:T(8,128)} %reshape.106, f32[512]{0:T(512)S(1)} %reshape.105, f32[512,384]{1,0:T(8,128)} %copy-done.5, f32[512,384]{1,0:T(8,128)} %copy-done.4), kind=kOutput, calls=%fused_computation.4 | convolution fusion | flops 404881408 | bytes 5244928 | tf_op jit(solution)/shard_map/dot_general | solution.py:30
  141.5 40.8 %all-reduce.1 = bf16[1,384,1024]{2,1,0:T(8,128)(2,1)} all-reduce(f32[1,384,1024]{2,1,0:T(8,128)} %convolution_bitcast_fusion), channel_id=1, replica_groups=mesh['dp'=4,'expert'=128] {'dp'}, use_global_device_ids=true, to_apply=%region_6.7 | all-reduce | flops 393216 | bytes 2359296 | tf_op jit(solution)/shard_map/psum | solution.py:100
  182.6 0.9 convolution_convert_fusion.1
  183.5 1.7 convert_element_type.104
  185.2 4.9 %reduce-scatter.3.cloned.1.call-done = f32[1,256,384]{2,1,0:T(8,128)} async-done(((f32[1,1024,384]{2,1,0:T(8,128)}), f32[1,256,384]{2,1,0:T(8,128)}) %reduce-scatter.3.cloned.1.call-update) | async-done | bytes 393232 | tf_op jit(solution)/shard_map/reduce_scatter | solution.py:97
  190.1 1.7 convert_element_type.103
  (42 shorter events, 8.2 us)
Async XLA Ops:
  7.2 109.0 %copy-start = (bf16[1,1024,384]{2,1,0:T(8,128)(2,1)S(1)}, bf16[1,1024,384]{2,1,0:T(8,128)(2,1)}, u32[]{:S(2)}) copy-start(bf16[1,1024,384]{2,1,0:T(8,128)(2,1)} %param.15) | copy-start | bytes 2359300
  10.8 29.9 %all-to-all-start = ((bf16[128,1,4]{2,1,0:T(2,128)(2,1)}), bf16[128,1,4]{2,1,0:T(2,128)(2,1)S(1)}, u32[]{:S(2)}, u32[]{:S(2)}) async-start(bf16[128,1,4]{2,1,0:T(2,128)(2,1)} %convert_element_type.116), calls=%async_computation | async-start | bytes 131072 | tf_op jit(solution)/shard_map/all_to_all | solution.py:78
  40.7 36.1 %all-to-all-start.1 = ((bf16[128,4,1024]{2,1,0:T(4,128)(2,1)}), bf16[128,4,1024]{2,1,0:T(4,128)(2,1)S(1)}, u32[]{:S(2)}, u32[]{:S(2)}) async-start(bf16[128,4,1024]{2,1,0:T(4,128)(2,1)} %reshape.98), calls=%async_computation.1 | async-start | bytes 2097152 | tf_op jit(solution)/shard_map/all_to_all | solution.py:77
  76.9 38.0 %all-to-all-start.2 = ((bf16[128,4,1024]{2,1,0:T(4,128)(2,1)}), bf16[128,4,1024]{2,1,0:T(4,128)(2,1)}, u32[]{:S(2)}, u32[]{:S(2)}) async-start(bf16[128,4,1024]{2,1,0:T(4,128)(2,1)} %reshape.99), calls=%async_computation.2 | async-start | bytes 2097152 | tf_op jit(solution)/shard_map/all_to_all | solution.py:76
  84.8 98.7 %reduce-scatter.5.cloned.1.call-start = ((), (), s32[]{:S(2)}) async-start(), calls=%async_computation.7 | async-start | bytes 1966080 | tf_op jit(solution)/shard_map/reduce_scatter | solution.py:98
  116.2 1.1 copy-start.1
  116.2 1.8 copy-start.3
  116.2 1.8 copy-start.6
  117.3 2.4 %copy-start.4 = (f32[512,384]{1,0:T(8,128)}, f32[512,384]{1,0:T(8,128)S(1)}, u32[]{:S(2)}) copy-start(f32[512,384]{1,0:T(8,128)S(1)} %fusion.3) | copy-start | bytes 2359300
  118.1 1.7 copy-start.5
  121.7 68.4 %reduce-scatter.3.cloned.1.call-start = ((), (), s32[]{:S(2)}) async-start(), calls=%async_computation.6 | async-start | bytes 1966080 | tf_op jit(solution)/shard_map/reduce_scatter | solution.py:97
  124.8 1.8 copy-start.2
  128.6 53.7 %all-to-all-start.3 = ((bf16[128,4,1024]{2,1,0:T(4,128)(2,1)}), bf16[128,4,1024]{2,1,0:T(4,128)(2,1)S(1)}, u32[]{:S(2)}, u32[]{:S(2)}) async-start(bf16[128,4,1024]{2,1,0:T(4,128)(2,1)} %reshape.101), calls=%async_computation.3 | async-start | bytes 2097152 | tf_op jit(solution)/shard_map/all_to_all | solution.py:90
Sparse Core Ops, SparseCore 0:
  121.8 24.1 reduce-scatter.4
  148.8 41.2 reduce-scatter.2
where the time goes:
time: 200 us; the launch traced here: 199 us
  waiting for transfers between devices  70.3 us (35%)
  blocking collectives  40.8 us (20%)
  starting transfers between devices  39.4 us (20%)
  matrix products  17 us (8%)
  between operations  14.3 us (7%)
  local copies, waits for them, and re-layouts  11.3 us (6%)
  other arithmetic  5.49 us (3%)
    psum x1, blocking collectives, shards(): grad_down = lax.psum(grad_terms[2][None], 'dp')  40.8 us
    all_to_all x1, waiting for transfers between devices, shards(): lax.all_to_all(cotan_send, 'expert', split_axis=0, concat_axis=0, tiled=T...  29.1 us
    all_to_all x1, waiting for transfers between devices, shards(): lax.all_to_all(token_send, 'expert', split_axis=0, concat_axis=0, tiled=T...  28.3 us
    all_to_all x1, starting transfers between devices, shards(): lax.all_to_all(weight_send, 'expert', split_axis=0, concat_axis=0, tiled=...  18.4 us
    all_to_all x1, waiting for transfers between devices, shards(): lax.all_to_all(weight_send, 'expert', split_axis=0, concat_axis=0, tiled=...  7.97 us
    all_to_all x1, starting transfers between devices, shards(): lax.all_to_all(token_send, 'expert', split_axis=0, concat_axis=0, tiled=T...  7.92 us
    all_to_all x1, starting transfers between devices, shards(): lax.all_to_all(grad_rows, 'expert', split_axis=0, concat_axis=0, tiled=True)  7.07 us
    all_to_all x1, starting transfers between devices, shards(): lax.all_to_all(cotan_send, 'expert', split_axis=0, concat_axis=0, tiled=T...  5.76 us
  transfers between devices with their start and end apart: 6, of which 4 were waited for; matrix products, arithmetic and copies ran while one was open for 11% of the time, Pallas kernels for 0%

commit v1 on v0

v1 whole, which is shorter than its diff:
```python
import functools

import jax
import jax.numpy as jnp
from jax import lax
from jax.experimental import pallas as pl
from jax.experimental.pallas import tpu as pltpu
from jax.sharding import PartitionSpec as P

BASE = 2
SLOTS = 4
MSG = 2 * SLOTS
LANES = 128
F32 = jnp.float32
BF16 = jnp.bfloat16
VMEM = pl.BlockSpec(memory_space=pltpu.VMEM)
SMEM = pl.BlockSpec(memory_space=pltpu.SMEM)
VMEM_BYTES = 48 * 1024 * 1024


def call(body, name, out_shape, in_specs, scratch=(), flops=0, bytes_accessed=0):
    return pl.pallas_call(
        body,
        name=name,
        out_shape=out_shape,
        in_specs=in_specs,
        out_specs=jax.tree.map(lambda _: VMEM, out_shape),
        scratch_shapes=list(scratch),
        compiler_params=pltpu.CompilerParams(vmem_limit_bytes=VMEM_BYTES),
        cost_estimate=pl.CostEstimate(
            flops=flops, bytes_accessed=bytes_accessed, transcendentals=0
        ),
    )


def dispatch_body(experts, routes, combine, hot, extra, tok, cot, send, pick, both):
    count, width = tok.shape
    both[:count, :] = tok[...]
    both[count:, :] = cot[...]
    lanes = 2 * count
    expert_id = lax.broadcasted_iota(jnp.int32, (experts, lanes), 0)
    lane = lax.broadcasted_iota(jnp.int32, (experts, lanes), 1)
    named = jnp.zeros((experts, lanes), F32)
    weight = jnp.zeros((experts, lanes), F32)
    for k in range(routes.shape[0]):
        match = expert_id == routes[k : k + 1, :]
        named = named + jnp.where(match, 1.0, 0.0)
        weight = weight + jnp.where(match, combine[k : k + 1, :], 0.0)
    src = lax.broadcasted_iota(jnp.int32, (lanes, lanes), 0)
    dst = lax.broadcasted_iota(jnp.int32, (lanes, lanes), 1)
    dst = jnp.where(dst >= count, dst - count, dst)
    before = jnp.where(src < dst, 1.0, 0.0)
    before = jnp.where(src < count, before, 0.0).astype(BF16)
    rank = jnp.dot(named.astype(BF16), before, preferred_element_type=F32)
    limit = jnp.full((experts, lanes), float(BASE), F32)
    for j in range(hot.shape[0]):
        limit = limit + jnp.where(expert_id == hot[j], extra[j].astype(F32), 0.0)
    place = jnp.where(lane >= count, rank + float(SLOTS), rank)
    place = jnp.where(named > 0.5, place, -1.0)
    place = jnp.where(rank < limit, place, -1.0)
    weight = jnp.where(lane >= count, weight, 1.0)
    slot = lax.broadcasted_iota(jnp.int32, (experts, MSG, lanes), 1).astype(F32)
    hit = jnp.broadcast_to(place[:, None, :], (experts, MSG, lanes)) == slot
    scaled = jnp.where(hit, jnp.broadcast_to(weight[:, None, :], hit.shape), 0.0)
    pick[...] = jnp.where(hit, 1.0, 0.0).reshape(experts * MSG, lanes).astype(BF16)
    scaled = scaled.reshape(experts * MSG, lanes).astype(BF16)
    send[...] = jnp.dot(scaled, both[...], preferred_element_type=F32).astype(BF16)


NN = (((1,), (0,)), ((), ()))
NT = (((1,), (1,)), ((), ()))
TN = (((0,), (0,)), ((), ()))


def dot(a, b, dims):
    return lax.dot_general(a, b, dims, preferred_element_type=F32)


def rows_body(recv, w_gate, w_up, w_down, back, tok, og, gu, hid, wide, narrow):
    total, features = recv.shape
    peers = total // MSG
    hidden = w_gate.shape[1]
    half = features // 2
    for c in range(features // LANES):
        wide[c] = recv[:, c * LANES : (c + 1) * LANES].astype(F32)
    for part in range(2):
        first = part * (SLOTS // 2)
        rows = pl.ds(first * peers, 2 * peers)
        for s in range(2):
            at = pl.ds((first + s) * peers, peers)
            for c in range(features // LANES):
                cols = slice(c * LANES, (c + 1) * LANES)
                tok[at, cols] = wide[c, pl.ds(first + s, peers, MSG), :].astype(BF16)
                og[at, cols] = wide[c, pl.ds(first + s + SLOTS, peers, MSG), :].astype(BF16)
        x, g = tok[rows, :], og[rows, :]
        gate_pre = dot(x, w_gate[...], NN)
        up_proj = dot(x, w_up[...], NN)
        hidden_grad = dot(g, w_down[...], NT)
        s = jax.nn.sigmoid(gate_pre)
        act = gate_pre * s
        hid[rows, :] = (act * up_proj).astype(BF16)
        gate_grad = (hidden_grad * up_proj * s * (1.0 + gate_pre * (1.0 - s))).astype(BF16)
        up_grad = (hidden_grad * act).astype(BF16)
        gu[rows, :hidden] = gate_grad
        gu[rows, hidden:] = up_grad
        grads = dot(gate_grad, w_gate[...], NT) + dot(up_grad, w_up[...], NT)
        for s in range(2):
            piece = grads[s * peers : (s + 1) * peers, :]
            for c in range(half // LANES):
                low = piece[:, c * LANES : (c + 1) * LANES]
                high = piece[:, half + c * LANES : half + (c + 1) * LANES]
                narrow[c, pl.ds(first + s, peers, MSG), :] = low
                narrow[c, pl.ds(first + s + SLOTS, peers, MSG), :] = high
    for c in range(half // LANES):
        back[:, c * LANES : (c + 1) * LANES] = narrow[c].astype(BF16)


def weights_body(ranks, me, left, right, own, *rest):
    sends, total = rest[:-1], rest[-1]
    total[...] = dot(left[...], right[...], TN)
    piece = own.shape[0]
    own[...] = total[pl.ds(pl.multiple_of(me[0] * piece, 8), piece), :]
    for i in range(1, ranks):
        at = lax.rem(me[0] + i, ranks) * piece
        sends[i - 1][...] = total[pl.ds(pl.multiple_of(at, 8), piece), :].astype(BF16)


def weight_pieces(name, ranks, me, left, right):
    rows, depth, width = left.shape[0], left.shape[1], right.shape[1]
    piece = depth // ranks
    out = [jax.ShapeDtypeStruct((piece, width), F32)]
    out += [jax.ShapeDtypeStruct((piece, width), BF16)] * (ranks - 1)
    return call(
        functools.partial(weights_body, ranks),
        name,
        out,
        [SMEM, VMEM, VMEM],
        [pltpu.VMEM((depth, width), F32)],
        2 * rows * depth * width,
        2 * (rows * (depth + width) + 2 * depth * width),
    )(me, left, right)


def sum_over(axis, ranks, pieces):
    total = pieces[0]
    for i in range(1, ranks):
        total = total + lax.ppermute(
            pieces[i], axis, [(s, (s + i) % ranks) for s in range(ranks)]
        ).astype(F32)
    return total.astype(BF16)


def shards(tokens, cotangent, routes, combine, hot_experts, extra_slots, w_gate, w_up, w_down):
    experts = lax.axis_size("expert")
    ranks = lax.axis_size("dp")
    count, features = tokens.shape
    hidden = w_gate.shape[2]
    total = experts * MSG
    rows = experts * SLOTS
    route_lanes = jnp.concatenate([routes, routes], axis=0).T
    combine_lanes = jnp.concatenate([combine, combine], axis=0).astype(F32).T
    send, pick = call(
        functools.partial(dispatch_body, experts),
        "dispatch",
        [
            jax.ShapeDtypeStruct((total, features), BF16),
            jax.ShapeDtypeStruct((total, 2 * count), BF16),
        ],
        [VMEM, VMEM, SMEM, SMEM, VMEM, VMEM],
        [pltpu.VMEM((2 * count, features), BF16)],
        2 * total * 2 * count * features,
        2 * total * features,
    )(route_lanes, combine_lanes, hot_experts, extra_slots, tokens, cotangent)
    recv = lax.all_to_all(send, "expert", split_axis=0, concat_axis=0, tiled=True)
    back, tok, og, gu, hid = call(
        rows_body,
        "rows",
        [
            jax.ShapeDtypeStruct((total, features // 2), BF16),
            jax.ShapeDtypeStruct((rows, features), BF16),
            jax.ShapeDtypeStruct((rows, features), BF16),
            jax.ShapeDtypeStruct((rows, 2 * hidden), BF16),
            jax.ShapeDtypeStruct((rows, hidden), BF16),
        ],
        [VMEM] * 4,
        [
            pltpu.VMEM((features // LANES, total, LANES), F32),
            pltpu.VMEM((features // 2 // LANES, total, LANES), F32),
        ],
        10 * rows * features * hidden,
        2 * (total * features * 2 + 3 * features * hidden),
    )(recv, w_gate[0], w_up[0], w_down[0])
    returned = lax.all_to_all(back, "expert", split_axis=0, concat_axis=0, tiled=True)
    me = lax.axis_index("dp").astype(jnp.int32).reshape(1)
    down = sum_over("dp", ranks, weight_pieces("down_grad", ranks, me, hid, og))
    grad_down = lax.all_gather(down, "dp", axis=0, tiled=True)
    gate_up = sum_over("dp", ranks, weight_pieces("gate_up_grad", ranks, me, tok, gu))
    halves = dot(pick, returned, TN)
    token_grads = jnp.concatenate([halves[:count], halves[count:]], axis=1).astype(BF16)
    return (
        token_grads,
        gate_up[None, :, :hidden],
        gate_up[None, :, hidden:],
        grad_down[None],
    )


def solution(mesh):
    in_specs = (
        P(("dp", "expert"), None),
        P(("dp", "expert"), None),
        P(("dp", "expert"), None),
        P(("dp", "expert"), None),
        P(),
        P(),
        P("expert", None, None),
        P("expert", None, None),
        P("expert", None, None),
    )
    out_specs = (
        P(("dp", "expert"), None),
        P("expert", "dp", None),
        P("expert", "dp", None),
        P("expert", None, None),
    )
    return jax.shard_map(shards, mesh=mesh, in_specs=in_specs, out_specs=out_specs, check_vma=False)
```

time: 200 us -> 144 us (0.72)
  waiting for transfers between devices: 70.3 us -> 0.02 us
  blocking collectives: 40.8 us -> 95.8 us
  matrix products: 17 us -> 1.54 us
  between operations: 14.3 us -> 0.81 us
  starting transfers between devices: 39.4 us -> 26.8 us
  Pallas kernels: 0 us -> 10.4 us
  local copies, waits for them, and re-layouts: 11.3 us -> 4.68 us
  other arithmetic: 5.49 us -> 2.58 us
    all_to_all x0 -> x1, blocking collectives: none -> 70.6 us  [shards(): lax.all_to_all(send, 'expert', split_axis=0, concat_axis=0, tiled=True)]
    all_to_all x4 -> x1, waiting for transfers between devices: 65.4 us -> 0.01 us  [shards(): lax.all_to_all(back, 'expert', split_axis=0, concat_axis=0, tiled=True)]
    psum x1 -> x0, blocking collectives: 40.8 us -> none  [shards(): grad_down = lax.psum(grad_terms[2][None], 'dp')]
    all_to_all x4 -> x1, starting transfers between devices: 39.2 us -> 8.37 us  [shards(): lax.all_to_all(back, 'expert', split_axis=0, concat_axis=0, tiled=True)]
    all_gather x0 -> x1, blocking collectives: none -> 25.2 us  [shards(): grad_down = lax.all_gather(down, 'dp', axis=0, tiled=True)]
    ppermute x0 -> x6, starting transfers between devices: none -> 18.4 us  [sum_over(): lax.ppermute(pieces[i], axis, [(s, (s + i) % ranks) for s in range(ranks)])]
    dot_general x10 -> x1, matrix products: 17 us -> 1.54 us  [dot(): return lax.dot_general(a, b, dims, preferred_element_type=F32)]
    pallas_call x0 -> x4, Pallas kernels: none -> 10.4 us  [the longest x1 6.88 us: shards(): call(rows_body, 'rows', [jax.ShapeDtypeStruct((total, features // 2), BF1...]
  transfers between devices with their start and end apart: 6 -> 7, of which waited for: 4 -> 0; matrix products, arithmetic and copies ran while one was open for 11% -> 1% of each run, Pallas kernels for 0% -> 2%
where the time goes in v1:
time: 144 us; the launch traced here: 143 us
  blocking collectives  95.8 us (67%)
  starting transfers between devices  26.8 us (19%)
  Pallas kernels  10.4 us (7%)
  local copies, waits for them, and re-layouts  4.68 us (3%)
  other arithmetic  2.58 us (2%)
  matrix products  1.54 us (1%)
    all_to_all x1, blocking collectives, shards(): lax.all_to_all(send, 'expert', split_axis=0, concat_axis=0, tiled=True)  70.6 us
    all_gather x1, blocking collectives, shards(): grad_down = lax.all_gather(down, 'dp', axis=0, tiled=True)  25.2 us
    ppermute x6, starting transfers between devices, sum_over(): lax.ppermute(pieces[i], axis, [(s, (s + i) % ranks) for s in range(ranks)])  18.4 us
    all_to_all x1, starting transfers between devices, shards(): lax.all_to_all(back, 'expert', split_axis=0, concat_axis=0, tiled=True)  8.37 us
    pallas_call x1, Pallas kernels, shards(): call(rows_body, 'rows', [jax.ShapeDtypeStruct((total, features // 2), BF1...  6.88 us
    unnamed x17, local copies, waits for them, and re-layouts  3.89 us
  transfers between devices with their start and end apart: 7, of which 0 were waited for; matrix products, arithmetic and copies ran while one was open for 1% of the time, Pallas kernels for 2%

profile of v1, /device:TPU:1, one launch (start us, length us, event | category | flops | bytes accessed | tf_op | source)
XLA Modules:
  0.0 142.6 jit_solution(7843730296328737979)
XLA Ops:
  0.6 0.8 add_bitcast_fusion.routes
  1.5 0.8 convert_bitcast_fusion.combine
  2.3 0.8 copy-done.3
  3.1 0.8 copy-done.4
  4.0 0.7 copy-done.5
  4.6 0.7 copy-done.6
  5.3 1.4 dispatch.1
  6.7 70.6 %all_to_all.23 = bf16[128,8,1024]{2,1,0:T(8,128)(2,1)} all-to-all(bf16[128,8,1024]{2,1,0:T(8,128)(2,1)S(1)} %bitcast.20), channel_id=1, replica_groups=mesh['dp'=4,'expert'=128] {'expert'}, dimensions={0} | all-to-all | bytes 4194304 | tf_op jit(solution)/shard_map/all_to_all | solution.py:174
  77.3 6.9 %rows.1 = (bf16[1024,512]{1,0:T(8,128)(2,1)}, bf16[512,1024]{1,0:T(8,128)(2,1)S(1)}, bf16[512,1024]{1,0:T(8,128)(2,1)}, bf16[512,768]{1,0:T(8,128)(2,1)S(1)}, bf16[512,384]{1,0:T(8,128)(2,1)S(1)}) custom-call(bf16[1024,1024]{1,0:T(8,128)(2,1)} %bitcast.25, bf16[1024,384]{1,0:T(8,128)(2,1)S(1)} %bitcast.21, bf16[1024,384]{1,0:T(8,128)(2,1)S(1)} %bitcast.22, ...), custom_call_target="tpu_custom_call" | custom-call | flops 2013265920 | bytes 6553600 | tf_op jit(solution)/shard_map/rows/pallas_call | solution.py:175
  84.2 8.4 %all-to-all-start.1 = ((bf16[128,8,512]{2,1,0:T(8,128)(2,1)}), bf16[128,8,512]{2,1,0:T(8,128)(2,1)}, u32[]{:S(2)}, u32[]{:S(2)}) async-start(bf16[128,8,512]{2,1,0:T(8,128)(2,1)} %bitcast.7), calls=%async_computation.1 | async-start | bytes 2097152 | tf_op jit(solution)/shard_map/all_to_all | solution.py:193
  92.6 0.8 down_grad.1
  93.4 4.4 %collective-permute-start.5 = (bf16[96,1024]{1,0:T(8,128)(2,1)S(1)}, bf16[96,1024]{1,0:T(8,128)(2,1)S(1)}, u32[]{:S(2)}, u32[]{:S(2)}) collective-permute-start(bf16[96,1024]{1,0:T(8,128)(2,1)S(1)} %get-tuple-element.33), channel_id=1, source_target_pairs={{0,384},{128,0},{256,128},{384,256},{1,385},{129,1},{257,129},{385... | collective-permute-start | bytes 589832 | tf_op jit(solution)/shard_map/ppermute | solution.py:147
  97.8 2.4 %collective-permute-start.4 = (bf16[96,1024]{1,0:T(8,128)(2,1)S(1)}, bf16[96,1024]{1,0:T(8,128)(2,1)S(1)}, u32[]{:S(2)}, u32[]{:S(2)}) collective-permute-start(bf16[96,1024]{1,0:T(8,128)(2,1)S(1)} %get-tuple-element.32), channel_id=1, source_target_pairs={{0,256},{128,384},{256,0},{384,128},{1,257},{129,385},{257,1},{385... | collective-permute-start | bytes 589832 | tf_op jit(solution)/shard_map/ppermute | solution.py:147
  100.2 2.5 %collective-permute-start.3 = (bf16[96,1024]{1,0:T(8,128)(2,1)S(1)}, bf16[96,1024]{1,0:T(8,128)(2,1)S(1)}, u32[]{:S(2)}, u32[]{:S(2)}) collective-permute-start(bf16[96,1024]{1,0:T(8,128)(2,1)S(1)} %get-tuple-element.31), channel_id=1, source_target_pairs={{0,128},{128,256},{256,384},{384,0},{1,129},{129,257},{257,385},{3... | collective-permute-start | bytes 589832 | tf_op jit(solution)/shard_map/ppermute | solution.py:147
  102.7 1.4 gate_up_grad.1
  104.1 4.0 %collective-permute-start.2 = (bf16[256,768]{1,0:T(8,128)(2,1)S(1)}, bf16[256,768]{1,0:T(8,128)(2,1)S(1)}, u32[]{:S(2)}, u32[]{:S(2)}) collective-permute-start(bf16[256,768]{1,0:T(8,128)(2,1)S(1)} %get-tuple-element.27), channel_id=1, source_target_pairs={{0,384},{128,0},{256,128},{384,256},{1,385},{129,1},{257,129},{385... | collective-permute-start | bytes 1179656 | tf_op jit(solution)/shard_map/ppermute | solution.py:147
  108.1 3.1 %collective-permute-start.1 = (bf16[256,768]{1,0:T(8,128)(2,1)S(1)}, bf16[256,768]{1,0:T(8,128)(2,1)S(1)}, u32[]{:S(2)}, u32[]{:S(2)}) collective-permute-start(bf16[256,768]{1,0:T(8,128)(2,1)S(1)} %get-tuple-element.26), channel_id=1, source_target_pairs={{0,256},{128,384},{256,0},{384,128},{1,257},{129,385},{257,1},{385... | collective-permute-start | bytes 1179656 | tf_op jit(solution)/shard_map/ppermute | solution.py:147
  111.3 1.9 %collective-permute-start = (bf16[256,768]{1,0:T(8,128)(2,1)S(1)}, bf16[256,768]{1,0:T(8,128)(2,1)S(1)}, u32[]{:S(2)}, u32[]{:S(2)}) collective-permute-start(bf16[256,768]{1,0:T(8,128)(2,1)S(1)} %get-tuple-element.25), channel_id=1, source_target_pairs={{0,128},{128,256},{256,384},{384,0},{1,129},{129,257},{257,385},{3... | collective-permute-start | bytes 1179656 | tf_op jit(solution)/shard_map/ppermute | solution.py:147
  113.3 25.2 %all_gather.3 = bf16[384,1024]{1,0:T(8,128)(2,1)S(1)} all-gather(bf16[96,1024]{1,0:T(8,128)(2,1)S(1)} %add_convert_fusion.1), channel_id=1, replica_groups=mesh['dp'=4,'expert'=128] {'dp'}, dimensions={0}, use_global_device_ids=true | all-gather | bytes 983040 | tf_op jit(solution)/shard_map/all_gather | solution.py:196
  138.6 0.2 add_convert_fusion
  138.8 0.8 slice_bitcast_fusion
  139.5 1.5 %convolution_convert_fusion = bf16[64,512]{1,0:T(8,128)(2,1)S(1)} fusion(bf16[1024,64]{1,0:T(8,128)(2,1)S(1)} %get-tuple-element.19, bf16[128,8,512]{2,1,0:T(8,128)(2,1)} %all-to-all-done.1), kind=kOutput, calls=%fused_computation | convolution fusion | flops 67141632 | bytes 1245184 | tf_op jit(solution)/shard_map/dot_general | solution.py:76
  141.1 0.6 pad_maximum_fusion
  141.7 0.9 copy.14
  (21 shorter events, 0.2 us)
Async XLA Ops:
  2.3 0.8 copy-start.3
  3.1 0.8 copy-start.4
  4.0 0.7 copy-start.5
  4.6 0.7 copy-start.6
  6.7 70.6 %copy-start = (bf16[1,1024,384]{2,1,0:T(8,128)(2,1)S(1)}, bf16[1,1024,384]{2,1,0:T(8,128)(2,1)}, u32[]{:S(2)}) copy-start(bf16[1,1024,384]{2,1,0:T(8,128)(2,1)} %param.15) | copy-start | bytes 2359300
  6.7 70.6 %copy-start.1 = (bf16[1,1024,384]{2,1,0:T(8,128)(2,1)S(1)}, bf16[1,1024,384]{2,1,0:T(8,128)(2,1)}, u32[]{:S(2)}) copy-start(bf16[1,1024,384]{2,1,0:T(8,128)(2,1)} %param.16) | copy-start | bytes 2359300
  6.7 70.6 %copy-start.2 = (bf16[1,384,1024]{2,1,0:T(8,128)(2,1)S(1)}, bf16[1,384,1024]{2,1,0:T(8,128)(2,1)}, u32[]{:S(2)}) copy-start(bf16[1,384,1024]{2,1,0:T(8,128)(2,1)} %param.17) | copy-start | bytes 2359300
  84.2 8.4 %copy-start.7 = (bf16[512,1024]{1,0:T(8,128)(2,1)S(1)}, bf16[512,1024]{1,0:T(8,128)(2,1)}, u32[]{:S(2)}) copy-start(bf16[512,1024]{1,0:T(8,128)(2,1)} %get-tuple-element.29.right) | copy-start | bytes 3145732
  84.2 55.3 %all-to-all-start.1 = ((bf16[128,8,512]{2,1,0:T(8,128)(2,1)}), bf16[128,8,512]{2,1,0:T(8,128)(2,1)}, u32[]{:S(2)}, u32[]{:S(2)}) async-start(bf16[128,8,512]{2,1,0:T(8,128)(2,1)} %bitcast.7), calls=%async_computation.1 | async-start | bytes 2097152 | tf_op jit(solution)/shard_map/all_to_all | solution.py:193
  93.4 17.9 %collective-permute-start.5 = (bf16[96,1024]{1,0:T(8,128)(2,1)S(1)}, bf16[96,1024]{1,0:T(8,128)(2,1)S(1)}, u32[]{:S(2)}, u32[]{:S(2)}) collective-permute-start(bf16[96,1024]{1,0:T(8,128)(2,1)S(1)} %get-tuple-element.33), channel_id=1, source_target_pairs={{0,384},{128,0},{256,128},{384,256},{1,385},{129,1},{257,129},{385... | collective-permute-start | bytes 589832 | tf_op jit(solution)/shard_map/ppermute | solution.py:147
  97.8 15.4 %collective-permute-start.4 = (bf16[96,1024]{1,0:T(8,128)(2,1)S(1)}, bf16[96,1024]{1,0:T(8,128)(2,1)S(1)}, u32[]{:S(2)}, u32[]{:S(2)}) collective-permute-start(bf16[96,1024]{1,0:T(8,128)(2,1)S(1)} %get-tuple-element.32), channel_id=1, source_target_pairs={{0,256},{128,384},{256,0},{384,128},{1,257},{129,385},{257,1},{385... | collective-permute-start | bytes 589832 | tf_op jit(solution)/shard_map/ppermute | solution.py:147
  100.2 13.0 %collective-permute-start.3 = (bf16[96,1024]{1,0:T(8,128)(2,1)S(1)}, bf16[96,1024]{1,0:T(8,128)(2,1)S(1)}, u32[]{:S(2)}, u32[]{:S(2)}) collective-permute-start(bf16[96,1024]{1,0:T(8,128)(2,1)S(1)} %get-tuple-element.31), channel_id=1, source_target_pairs={{0,128},{128,256},{256,384},{384,0},{1,129},{129,257},{257,385},{3... | collective-permute-start | bytes 589832 | tf_op jit(solution)/shard_map/ppermute | solution.py:147
  104.1 34.5 %collective-permute-start.2 = (bf16[256,768]{1,0:T(8,128)(2,1)S(1)}, bf16[256,768]{1,0:T(8,128)(2,1)S(1)}, u32[]{:S(2)}, u32[]{:S(2)}) collective-permute-start(bf16[256,768]{1,0:T(8,128)(2,1)S(1)} %get-tuple-element.27), channel_id=1, source_target_pairs={{0,384},{128,0},{256,128},{384,256},{1,385},{129,1},{257,129},{385... | collective-permute-start | bytes 1179656 | tf_op jit(solution)/shard_map/ppermute | solution.py:147
  108.1 30.5 %collective-permute-start.1 = (bf16[256,768]{1,0:T(8,128)(2,1)S(1)}, bf16[256,768]{1,0:T(8,128)(2,1)S(1)}, u32[]{:S(2)}, u32[]{:S(2)}) collective-permute-start(bf16[256,768]{1,0:T(8,128)(2,1)S(1)} %get-tuple-element.26), channel_id=1, source_target_pairs={{0,256},{128,384},{256,0},{384,128},{1,257},{129,385},{257,1},{385... | collective-permute-start | bytes 1179656 | tf_op jit(solution)/shard_map/ppermute | solution.py:147
  111.3 27.3 %collective-permute-start = (bf16[256,768]{1,0:T(8,128)(2,1)S(1)}, bf16[256,768]{1,0:T(8,128)(2,1)S(1)}, u32[]{:S(2)}, u32[]{:S(2)}) collective-permute-start(bf16[256,768]{1,0:T(8,128)(2,1)S(1)} %get-tuple-element.25), channel_id=1, source_target_pairs={{0,128},{128,256},{256,384},{384,0},{1,129},{129,257},{257,385},{3... | collective-permute-start | bytes 1179656 | tf_op jit(solution)/shard_map/ppermute | solution.py:147

commit v2 on v1

--- a/solution.py
+++ b/solution.py
@@ -15,10 +15,21 @@
 BF16 = jnp.bfloat16
 VMEM = pl.BlockSpec(memory_space=pltpu.VMEM)
 SMEM = pl.BlockSpec(memory_space=pltpu.SMEM)
-VMEM_BYTES = 48 * 1024 * 1024
-
-
-def call(body, name, out_shape, in_specs, scratch=(), flops=0, bytes_accessed=0):
+MIB = 1024 * 1024
+
+
+NN = (((1,), (0,)), ((), ()))
+NT = (((1,), (1,)), ((), ()))
+TN = (((0,), (0,)), ((), ()))
+
+
+def dot(a, b, dims):
+    return lax.dot_general(a, b, dims, preferred_element_type=F32)
+
+
+def call(
+    body, name, out_shape, in_specs, scratch=(), flops=0, bytes_accessed=0, vmem=16 * MIB
+):
     return pl.pallas_call(
         body,
         name=name,
@@ -26,32 +37,58 @@
         in_specs=in_specs,
         out_specs=jax.tree.map(lambda _: VMEM, out_shape),
         scratch_shapes=list(scratch),
-        compiler_params=pltpu.CompilerParams(vmem_limit_bytes=VMEM_BYTES),
+        compiler_params=pltpu.CompilerParams(vmem_limit_bytes=vmem),
         cost_estimate=pl.CostEstimate(
             flops=flops, bytes_accessed=bytes_accessed, transcendentals=0
         ),
     )
 
 
-def dispatch_body(experts, routes, combine, hot, extra, tok, cot, send, pick, both):
-    count, width = tok.shape
-    both[:count, :] = tok[...]
-    both[count:, :] = cot[...]
+def identity(n):
+    rows = lax.broadcasted_iota(jnp.int32, (n, n), 0)
+    return jnp.where(rows == lax.broadcasted_iota(jnp.int32, (n, n), 1), 1.0, 0.0).astype(BF16)
+
+
+def dispatch_body(
+    experts, tok_hbm, cot_hbm, routes_hbm, combine_hbm, hot_hbm, extra_hbm,
+    send, pick_t, both, routes_in, combine_in, hot, extra, sems,
+):
+    count = tok_hbm.shape[0]
+    copies = [
+        pltpu.make_async_copy(source, target, sems.at[i])
+        for i, (source, target) in enumerate(
+            [
+                (routes_hbm, routes_in),
+                (combine_hbm, combine_in),
+                (hot_hbm, hot),
+                (extra_hbm, extra),
+                (tok_hbm, both.at[pl.ds(0, count)]),
+                (cot_hbm, both.at[pl.ds(count, count)]),
+            ]
+        )
+    ]
+    for copy in copies:
+        copy.start()
+    for copy in copies[:4]:
+        copy.wait()
     lanes = 2 * count
+    src = lax.broadcasted_iota(jnp.int32, (count, lanes), 0)
+    dst = lax.broadcasted_iota(jnp.int32, (count, lanes), 1)
+    dst = jnp.where(dst >= count, dst - count, dst)
+    twice = jnp.where(src == dst, 1.0, 0.0).astype(BF16)
+    routes = dot(routes_in[...].astype(F32).astype(BF16), twice, NN)
+    combine = dot(combine_in[...], twice, NN)
     expert_id = lax.broadcasted_iota(jnp.int32, (experts, lanes), 0)
     lane = lax.broadcasted_iota(jnp.int32, (experts, lanes), 1)
     named = jnp.zeros((experts, lanes), F32)
     weight = jnp.zeros((experts, lanes), F32)
+    expert_number = expert_id.astype(F32)
     for k in range(routes.shape[0]):
-        match = expert_id == routes[k : k + 1, :]
+        match = expert_number == routes[k : k + 1, :]
         named = named + jnp.where(match, 1.0, 0.0)
         weight = weight + jnp.where(match, combine[k : k + 1, :], 0.0)
-    src = lax.broadcasted_iota(jnp.int32, (lanes, lanes), 0)
-    dst = lax.broadcasted_iota(jnp.int32, (lanes, lanes), 1)
-    dst = jnp.where(dst >= count, dst - count, dst)
-    before = jnp.where(src < dst, 1.0, 0.0)
-    before = jnp.where(src < count, before, 0.0).astype(BF16)
-    rank = jnp.dot(named.astype(BF16), before, preferred_element_type=F32)
+    before = jnp.where(src < dst, 1.0, 0.0).astype(BF16)
+    rank = dot(named[:, :count].astype(BF16), before, NN)
     limit = jnp.full((experts, lanes), float(BASE), F32)
     for j in range(hot.shape[0]):
         limit = limit + jnp.where(expert_id == hot[j], extra[j].astype(F32), 0.0)
@@ -62,18 +99,27 @@
     slot = lax.broadcasted_iota(jnp.int32, (experts, MSG, lanes), 1).astype(F32)
     hit = jnp.broadcast_to(place[:, None, :], (experts, MSG, lanes)) == slot
     scaled = jnp.where(hit, jnp.broadcast_to(weight[:, None, :], hit.shape), 0.0)
-    pick[...] = jnp.where(hit, 1.0, 0.0).reshape(experts * MSG, lanes).astype(BF16)
     scaled = scaled.reshape(experts * MSG, lanes).astype(BF16)
+    for copy in copies[4:]:
+        copy.wait()
     send[...] = jnp.dot(scaled, both[...], preferred_element_type=F32).astype(BF16)
-
-
-NN = (((1,), (0,)), ((), ()))
-NT = (((1,), (1,)), ((), ()))
-TN = (((0,), (0,)), ((), ()))
-
-
-def dot(a, b, dims):
-    return lax.dot_general(a, b, dims, preferred_element_type=F32)
+    pick = jnp.where(hit, 1.0, 0.0).reshape(experts * MSG, lanes).astype(BF16)
+    pick_t[...] = dot(identity(lanes), pick, NT).astype(BF16)
+
+
+def token_body(pick_t, returned, out):
+    count, half = out.shape[0], returned.shape[1]
+    both = dot(pick_t[...], returned[...], NN)
+    out[:, :half] = both[:count].astype(BF16)
+    out[:, half:] = both[count:].astype(BF16)
+
+
+def place_body(ranks, me, *refs):
+    pieces, out = refs[:-1], refs[-1]
+    piece = pieces[0].shape[0]
+    for i in range(ranks):
+        at = lax.rem(me[0] + ranks - i, ranks) * piece
+        out[pl.ds(pl.multiple_of(at, 16), piece), :] = pieces[i][...]
 
 
 def rows_body(recv, w_gate, w_up, w_down, back, tok, og, gu, hid, wide, narrow):
@@ -141,12 +187,14 @@
     )(me, left, right)
 
 
-def sum_over(axis, ranks, pieces):
+def shift(value, ranks, by):
+    return lax.ppermute(value, "dp", [(s, (s + by) % ranks) for s in range(ranks)])
+
+
+def sum_over(ranks, pieces):
     total = pieces[0]
     for i in range(1, ranks):
-        total = total + lax.ppermute(
-            pieces[i], axis, [(s, (s + i) % ranks) for s in range(ranks)]
-        ).astype(F32)
+        total = total + shift(pieces[i], ranks, i).astype(F32)
     return total.astype(BF16)
 
 
@@ -157,20 +205,26 @@
     hidden = w_gate.shape[2]
     total = experts * MSG
     rows = experts * SLOTS
-    route_lanes = jnp.concatenate([routes, routes], axis=0).T
-    combine_lanes = jnp.concatenate([combine, combine], axis=0).astype(F32).T
-    send, pick = call(
+    send, pick_t = call(
         functools.partial(dispatch_body, experts),
         "dispatch",
         [
             jax.ShapeDtypeStruct((total, features), BF16),
-            jax.ShapeDtypeStruct((total, 2 * count), BF16),
-        ],
-        [VMEM, VMEM, SMEM, SMEM, VMEM, VMEM],
-        [pltpu.VMEM((2 * count, features), BF16)],
+            jax.ShapeDtypeStruct((2 * count, total), BF16),
+        ],
+        [pl.BlockSpec(memory_space=pltpu.HBM)] * 6,
+        [
+            pltpu.VMEM((2 * count, features), BF16),
+            pltpu.VMEM(routes.shape[::-1], jnp.int32),
+            pltpu.VMEM(combine.shape[::-1], BF16),
+            pltpu.SMEM(hot_experts.shape, jnp.int32),
+            pltpu.SMEM(extra_slots.shape, jnp.int32),
+            pltpu.SemaphoreType.DMA((6,)),
+        ],
         2 * total * 2 * count * features,
         2 * total * features,
-    )(route_lanes, combine_lanes, hot_experts, extra_slots, tokens, cotangent)
+        64 * MIB - 65536,
+    )(tokens, cotangent, routes.T, combine.T, hot_experts, extra_slots)
     recv = lax.all_to_all(send, "expert", split_axis=0, concat_axis=0, tiled=True)
     back, tok, og, gu, hid = call(
         rows_body,
@@ -189,14 +243,30 @@
         ],
         10 * rows * features * hidden,
         2 * (total * features * 2 + 3 * features * hidden),
+        32 * MIB,
     )(recv, w_gate[0], w_up[0], w_down[0])
     returned = lax.all_to_all(back, "expert", split_axis=0, concat_axis=0, tiled=True)
     me = lax.axis_index("dp").astype(jnp.int32).reshape(1)
-    down = sum_over("dp", ranks, weight_pieces("down_grad", ranks, me, hid, og))
-    grad_down = lax.all_gather(down, "dp", axis=0, tiled=True)
-    gate_up = sum_over("dp", ranks, weight_pieces("gate_up_grad", ranks, me, tok, gu))
-    halves = dot(pick, returned, TN)
-    token_grads = jnp.concatenate([halves[:count], halves[count:]], axis=1).astype(BF16)
+    down = sum_over(ranks, weight_pieces("down_grad", ranks, me, hid, og))
+    grad_down = call(
+        functools.partial(place_body, ranks),
+        "place",
+        jax.ShapeDtypeStruct((hidden, features), BF16),
+        [SMEM] + [VMEM] * ranks,
+        (),
+        0,
+        4 * hidden * features,
+    )(me, down, *(shift(down, ranks, i) for i in range(1, ranks)))
+    gate_up = sum_over(ranks, weight_pieces("gate_up_grad", ranks, me, tok, gu))
+    token_grads = call(
+        token_body,
+        "token_grad",
+        jax.ShapeDtypeStruct((count, features), BF16),
+        [VMEM, VMEM],
+        (),
+        2 * total * count * features,
+        2 * total * features,
+    )(pick_t, returned)
     return (
         token_grads,
         gate_up[None, :, :hidden],

time: 144 us -> 144 us (level)
  blocking collectives: 95.8 us -> 70.7 us
  waiting for transfers between devices: 0.02 us -> 18 us
  starting transfers between devices: 26.8 us -> 36.4 us
  other arithmetic: 2.58 us -> 0.28 us
  Pallas kernels: 10.4 us -> 12.5 us
  local copies, waits for them, and re-layouts: 4.68 us -> 2.81 us
  matrix products: 1.54 us -> 0 us
    all_gather x1 -> x0, blocking collectives: 25.2 us -> none  [shards(): grad_down = lax.all_gather(down, 'dp', axis=0, tiled=True)]
    ppermute x6 -> x9, waiting for transfers between devices: 0.02 us -> 18 us  [shift(): lax.ppermute(value, 'dp', [(s, (s + by) % ranks) for s in range(ranks)])]
    ppermute x6 -> x9, starting transfers between devices: 18.4 us -> 28.6 us  [shift(): lax.ppermute(value, 'dp', [(s, (s + by) % ranks) for s in range(ranks)])]
    pallas_call x1, Pallas kernels: 1.38 us -> 3.34 us  [shards(): call(functools.partial(dispatch_body, experts), 'dispatch', [jax.ShapeDty...]
    pallas_call x0 -> x2, Pallas kernels: none -> 1.86 us  [the longest x1 0.94 us: shards(): call(functools.partial(place_body, ranks), 'place', jax.ShapeDtypeStruct(...]
    unnamed x17 -> x12, local copies, waits for them, and re-layouts: 3.89 us -> 2.03 us
    pallas_call x1, Pallas kernels: 6.88 us -> 5.18 us  [shards(): call(rows_body, 'rows', [jax.ShapeDtypeStruct((total, features // 2), BF1...]
    transpose x2 -> x0, other arithmetic: 1.67 us -> none  [the longest x1 0.84 us: shards(): route_lanes = jnp.concatenate([routes, routes], axis=0).T]
  transfers between devices with their start and end apart: 7 -> 10, of which waited for: 0 -> 3; matrix products, arithmetic and copies ran while one was open for 1% -> 1% of each run, Pallas kernels for 2% -> 2%
where the time goes in v2:
time: 144 us; the launch traced here: 142 us
  blocking collectives  70.7 us (49%)
  starting transfers between devices  36.4 us (25%)
  waiting for transfers between devices  18 us (12%)
  Pallas kernels  12.5 us (9%)
  local copies, waits for them, and re-layouts  2.81 us (2%)
    all_to_all x1, blocking collectives, shards(): lax.all_to_all(send, 'expert', split_axis=0, concat_axis=0, tiled=True)  70.7 us
    ppermute x9, starting transfers between devices, shift(): lax.ppermute(value, 'dp', [(s, (s + by) % ranks) for s in range(ranks)])  28.6 us
    ppermute x9, waiting for transfers between devices, shift(): lax.ppermute(value, 'dp', [(s, (s + by) % ranks) for s in range(ranks)])  18 us
    all_to_all x1, starting transfers between devices, shards(): lax.all_to_all(back, 'expert', split_axis=0, concat_axis=0, tiled=True)  7.79 us
    pallas_call x1, Pallas kernels, shards(): call(rows_body, 'rows', [jax.ShapeDtypeStruct((total, features // 2), BF1...  5.18 us
    pallas_call x1, Pallas kernels, shards(): call(functools.partial(dispatch_body, experts), 'dispatch', [jax.ShapeDty...  3.34 us
  transfers between devices with their start and end apart: 10, of which 3 were waited for; matrix products, arithmetic and copies ran while one was open for 1% of the time, Pallas kernels for 2%

profile of v2, /device:TPU:1, one launch (start us, length us, event | category | flops | bytes accessed | tf_op | source)
XLA Modules:
  0.0 141.5 jit_solution(2815528316905431007)
XLA Ops:
  0.6 3.3 %dispatch.1 = (bf16[1024,1024]{1,0:T(8,128)(2,1)}, bf16[64,1024]{1,0:T(8,128)(2,1)}) custom-call(bf16[32,1024]{1,0:T(8,128)(2,1)} %tok_hbm.1, bf16[32,1024]{1,0:T(8,128)(2,1)} %cot_hbm.1, s32[8,32]{1,0:T(8,128)} %bitcast.22, bf16[8,32]{1,0:T(8,128)(2,1)} %bitcast.23, s32[4]{0:T(128)} %hot_hbm.1, s32[4]{0:T(128)} %extra_hbm.1), custom_call_target="tpu_custom_call" | custom-call | flops 134217728 | bytes 2097152 | tf_op jit(solution)/shard_map/dispatch/pallas_call | solution.py:208
  4.0 70.7 %all_to_all.22 = bf16[128,8,1024]{2,1,0:T(8,128)(2,1)S(1)} all-to-all(bf16[128,8,1024]{2,1,0:T(8,128)(2,1)} %bitcast.20), channel_id=1, replica_groups=mesh['dp'=4,'expert'=128] {'expert'}, dimensions={0} | all-to-all | bytes 4194304 | tf_op jit(solution)/shard_map/all_to_all | solution.py:228
  74.7 5.2 %rows.1 = (bf16[1024,512]{1,0:T(8,128)(2,1)}, bf16[512,1024]{1,0:T(8,128)(2,1)S(1)}, bf16[512,1024]{1,0:T(8,128)(2,1)S(1)}, bf16[512,768]{1,0:T(8,128)(2,1)S(1)}, bf16[512,384]{1,0:T(8,128)(2,1)S(1)}) custom-call(bf16[1024,1024]{1,0:T(8,128)(2,1)S(1)} %bitcast.16, bf16[1024,384]{1,0:T(8,128)(2,1)S(1)} %bitcast.17, bf16[1024,384]{1,0:T(8,128)(2,1)S(1)} %bitcast.18, ...), custom_call_target="tpu_custom_call" | custom-call | flops 2013265920 | bytes 6553600 | tf_op jit(solution)/shard_map/rows/pallas_call | solution.py:229
  79.9 0.9 copy-done.4
  80.8 7.8 %all-to-all-start.1 = ((bf16[128,8,512]{2,1,0:T(8,128)(2,1)}), bf16[128,8,512]{2,1,0:T(8,128)(2,1)S(1)}, u32[]{:S(2)}, u32[]{:S(2)}) async-start(bf16[128,8,512]{2,1,0:T(8,128)(2,1)} %bitcast.7), calls=%async_computation.1 | async-start | bytes 2097152 | tf_op jit(solution)/shard_map/all_to_all | solution.py:248
  88.6 0.8 down_grad.1
  89.4 4.4 %collective-permute-start.5 = (bf16[96,1024]{1,0:T(8,128)(2,1)S(1)}, bf16[96,1024]{1,0:T(8,128)(2,1)S(1)}, u32[]{:S(2)}, u32[]{:S(2)}) collective-permute-start(bf16[96,1024]{1,0:T(8,128)(2,1)S(1)} %get-tuple-element.33), channel_id=1, source_target_pairs={{0,384},{128,0},{256,128},{384,256},{1,385},{129,1},{257,129},{385... | collective-permute-start | bytes 589832 | tf_op jit(solution)/shard_map/ppermute | solution.py:191
  93.8 2.4 %collective-permute-start.4 = (bf16[96,1024]{1,0:T(8,128)(2,1)S(1)}, bf16[96,1024]{1,0:T(8,128)(2,1)S(1)}, u32[]{:S(2)}, u32[]{:S(2)}) collective-permute-start(bf16[96,1024]{1,0:T(8,128)(2,1)S(1)} %get-tuple-element.32), channel_id=1, source_target_pairs={{0,256},{128,384},{256,0},{384,128},{1,257},{129,385},{257,1},{385... | collective-permute-start | bytes 589832 | tf_op jit(solution)/shard_map/ppermute | solution.py:191
  96.2 2.5 %collective-permute-start.3 = (bf16[96,1024]{1,0:T(8,128)(2,1)S(1)}, bf16[96,1024]{1,0:T(8,128)(2,1)S(1)}, u32[]{:S(2)}, u32[]{:S(2)}) collective-permute-start(bf16[96,1024]{1,0:T(8,128)(2,1)S(1)} %get-tuple-element.31), channel_id=1, source_target_pairs={{0,128},{128,256},{256,384},{384,0},{1,129},{129,257},{257,385},{3... | collective-permute-start | bytes 589832 | tf_op jit(solution)/shard_map/ppermute | solution.py:191
  98.7 1.1 copy-done.5
  99.8 1.4 gate_up_grad.1
  101.2 1.1 collective-permute-done.4
  102.4 5.1 %collective-permute-done.3 = bf16[96,1024]{1,0:T(8,128)(2,1)S(1)} collective-permute-done((bf16[96,1024]{1,0:T(8,128)(2,1)S(1)}, bf16[96,1024]{1,0:T(8,128)(2,1)S(1)}, u32[]{:S(2)}, u32[]{:S(2)}) %collective-permute-start.3) | collective-permute-done | bytes 196640 | tf_op jit(solution)/shard_map/ppermute | solution.py:191
  107.6 1.9 %collective-permute-start.6 = (bf16[96,1024]{1,0:T(8,128)(2,1)S(1)}, bf16[96,1024]{1,0:T(8,128)(2,1)S(1)}, u32[]{:S(2)}, u32[]{:S(2)}) collective-permute-start(bf16[96,1024]{1,0:T(8,128)(2,1)S(1)} %add_convert_fusion.1.refs_0_), channel_id=1, source_target_pairs={{0,128},{128,256},{256,384},{384,0},{1,129},{129,257},{257,385},{3... | collective-permute-start | bytes 589832 | tf_op jit(solution)/shard_map/ppermute | solution.py:191
  109.5 4.6 %collective-permute-start.2 = (bf16[256,768]{1,0:T(8,128)(2,1)S(1)}, bf16[256,768]{1,0:T(8,128)(2,1)S(1)}, u32[]{:S(2)}, u32[]{:S(2)}) collective-permute-start(bf16[256,768]{1,0:T(8,128)(2,1)S(1)} %get-tuple-element.27), channel_id=1, source_target_pairs={{0,384},{128,0},{256,128},{384,256},{1,385},{129,1},{257,129},{385... | collective-permute-start | bytes 1179656 | tf_op jit(solution)/shard_map/ppermute | solution.py:191
  114.1 1.9 %collective-permute-start.1 = (bf16[256,768]{1,0:T(8,128)(2,1)S(1)}, bf16[256,768]{1,0:T(8,128)(2,1)S(1)}, u32[]{:S(2)}, u32[]{:S(2)}) collective-permute-start(bf16[256,768]{1,0:T(8,128)(2,1)S(1)} %get-tuple-element.26), channel_id=1, source_target_pairs={{0,256},{128,384},{256,0},{384,128},{1,257},{129,385},{257,1},{385... | collective-permute-start | bytes 1179656 | tf_op jit(solution)/shard_map/ppermute | solution.py:191
  116.0 2.6 %collective-permute-start = (bf16[256,768]{1,0:T(8,128)(2,1)S(1)}, bf16[256,768]{1,0:T(8,128)(2,1)S(1)}, u32[]{:S(2)}, u32[]{:S(2)}) collective-permute-start(bf16[256,768]{1,0:T(8,128)(2,1)S(1)} %get-tuple-element.25), channel_id=1, source_target_pairs={{0,128},{128,256},{256,384},{384,0},{1,129},{129,257},{257,385},{3... | collective-permute-start | bytes 1179656 | tf_op jit(solution)/shard_map/ppermute | solution.py:191
  118.6 4.3 %collective-permute-start.7 = (bf16[96,1024]{1,0:T(8,128)(2,1)S(1)}, bf16[96,1024]{1,0:T(8,128)(2,1)S(1)}, u32[]{:S(2)}, u32[]{:S(2)}) collective-permute-start(bf16[96,1024]{1,0:T(8,128)(2,1)S(1)} %add_convert_fusion.1.refs_0_), channel_id=1, source_target_pairs={{0,256},{128,384},{256,0},{384,128},{1,257},{129,385},{257,1},{385... | collective-permute-start | bytes 589832 | tf_op jit(solution)/shard_map/ppermute | solution.py:191
  123.0 4.0 %collective-permute-start.8 = (bf16[96,1024]{1,0:T(8,128)(2,1)S(1)}, bf16[96,1024]{1,0:T(8,128)(2,1)S(1)}, u32[]{:S(2)}, u32[]{:S(2)}) collective-permute-start(bf16[96,1024]{1,0:T(8,128)(2,1)S(1)} %add_convert_fusion.1.refs_0_), channel_id=1, source_target_pairs={{0,384},{128,0},{256,128},{384,256},{1,385},{129,1},{257,129},{385... | collective-permute-start | bytes 589832 | tf_op jit(solution)/shard_map/ppermute | solution.py:191
  126.9 11.7 %collective-permute-done.7.refs_2_ = bf16[96,1024]{1,0:T(8,128)(2,1)S(1)} collective-permute-done((bf16[96,1024]{1,0:T(8,128)(2,1)S(1)}, bf16[96,1024]{1,0:T(8,128)(2,1)S(1)}, u32[]{:S(2)}, u32[]{:S(2)}) %collective-permute-start.7) | collective-permute-done | bytes 196640 | tf_op jit(solution)/shard_map/ppermute | solution.py:191
  138.7 0.9 place.1
  139.6 0.2 add_convert_fusion
  139.8 0.8 slice_bitcast_fusion
  140.6 0.9 token_grad.1
  (18 shorter events, 0.2 us)
Async XLA Ops:
  4.0 70.7 %copy-start.1 = (bf16[1,1024,384]{2,1,0:T(8,128)(2,1)S(1)}, bf16[1,1024,384]{2,1,0:T(8,128)(2,1)}, u32[]{:S(2)}) copy-start(bf16[1,1024,384]{2,1,0:T(8,128)(2,1)} %param.15) | copy-start | bytes 2359300
  4.0 70.7 %copy-start.2 = (bf16[1,1024,384]{2,1,0:T(8,128)(2,1)S(1)}, bf16[1,1024,384]{2,1,0:T(8,128)(2,1)}, u32[]{:S(2)}) copy-start(bf16[1,1024,384]{2,1,0:T(8,128)(2,1)} %param.16) | copy-start | bytes 2359300
  4.0 70.7 %copy-start.3 = (bf16[1,384,1024]{2,1,0:T(8,128)(2,1)S(1)}, bf16[1,384,1024]{2,1,0:T(8,128)(2,1)}, u32[]{:S(2)}) copy-start(bf16[1,384,1024]{2,1,0:T(8,128)(2,1)} %param.17) | copy-start | bytes 2359300
  79.9 0.9 copy-start.4
  80.8 59.8 %all-to-all-start.1 = ((bf16[128,8,512]{2,1,0:T(8,128)(2,1)}), bf16[128,8,512]{2,1,0:T(8,128)(2,1)S(1)}, u32[]{:S(2)}, u32[]{:S(2)}) async-start(bf16[128,8,512]{2,1,0:T(8,128)(2,1)} %bitcast.7), calls=%async_computation.1 | async-start | bytes 2097152 | tf_op jit(solution)/shard_map/all_to_all | solution.py:248
  89.4 11.9 %collective-permute-start.5 = (bf16[96,1024]{1,0:T(8,128)(2,1)S(1)}, bf16[96,1024]{1,0:T(8,128)(2,1)S(1)}, u32[]{:S(2)}, u32[]{:S(2)}) collective-permute-start(bf16[96,1024]{1,0:T(8,128)(2,1)S(1)} %get-tuple-element.33), channel_id=1, source_target_pairs={{0,384},{128,0},{256,128},{384,256},{1,385},{129,1},{257,129},{385... | collective-permute-start | bytes 589832 | tf_op jit(solution)/shard_map/ppermute | solution.py:191
  93.8 8.6 %collective-permute-start.4 = (bf16[96,1024]{1,0:T(8,128)(2,1)S(1)}, bf16[96,1024]{1,0:T(8,128)(2,1)S(1)}, u32[]{:S(2)}, u32[]{:S(2)}) collective-permute-start(bf16[96,1024]{1,0:T(8,128)(2,1)S(1)} %get-tuple-element.32), channel_id=1, source_target_pairs={{0,256},{128,384},{256,0},{384,128},{1,257},{129,385},{257,1},{385... | collective-permute-start | bytes 589832 | tf_op jit(solution)/shard_map/ppermute | solution.py:191
  96.2 11.3 %collective-permute-start.3 = (bf16[96,1024]{1,0:T(8,128)(2,1)S(1)}, bf16[96,1024]{1,0:T(8,128)(2,1)S(1)}, u32[]{:S(2)}, u32[]{:S(2)}) collective-permute-start(bf16[96,1024]{1,0:T(8,128)(2,1)S(1)} %get-tuple-element.31), channel_id=1, source_target_pairs={{0,128},{128,256},{256,384},{384,0},{1,129},{129,257},{257,385},{3... | collective-permute-start | bytes 589832 | tf_op jit(solution)/shard_map/ppermute | solution.py:191
  98.7 1.1 copy-start.5
  107.6 15.4 %collective-permute-start.6 = (bf16[96,1024]{1,0:T(8,128)(2,1)S(1)}, bf16[96,1024]{1,0:T(8,128)(2,1)S(1)}, u32[]{:S(2)}, u32[]{:S(2)}) collective-permute-start(bf16[96,1024]{1,0:T(8,128)(2,1)S(1)} %add_convert_fusion.1.refs_0_), channel_id=1, source_target_pairs={{0,128},{128,256},{256,384},{384,0},{1,129},{129,257},{257,385},{3... | collective-permute-start | bytes 589832 | tf_op jit(solution)/shard_map/ppermute | solution.py:191
  109.5 30.1 %collective-permute-start.2 = (bf16[256,768]{1,0:T(8,128)(2,1)S(1)}, bf16[256,768]{1,0:T(8,128)(2,1)S(1)}, u32[]{:S(2)}, u32[]{:S(2)}) collective-permute-start(bf16[256,768]{1,0:T(8,128)(2,1)S(1)} %get-tuple-element.27), channel_id=1, source_target_pairs={{0,384},{128,0},{256,128},{384,256},{1,385},{129,1},{257,129},{385... | collective-permute-start | bytes 1179656 | tf_op jit(solution)/shard_map/ppermute | solution.py:191
  114.1 25.6 %collective-permute-start.1 = (bf16[256,768]{1,0:T(8,128)(2,1)S(1)}, bf16[256,768]{1,0:T(8,128)(2,1)S(1)}, u32[]{:S(2)}, u32[]{:S(2)}) collective-permute-start(bf16[256,768]{1,0:T(8,128)(2,1)S(1)} %get-tuple-element.26), channel_id=1, source_target_pairs={{0,256},{128,384},{256,0},{384,128},{1,257},{129,385},{257,1},{385... | collective-permute-start | bytes 1179656 | tf_op jit(solution)/shard_map/ppermute | solution.py:191
  116.0 24.6 %copy-start = (bf16[64,1024]{1,0:T(8,128)(2,1)S(1)}, bf16[64,1024]{1,0:T(8,128)(2,1)}, u32[]{:S(2)}) copy-start(bf16[64,1024]{1,0:T(8,128)(2,1)} %get-tuple-element.19.pick_t) | copy-start | bytes 393220
  116.0 23.6 %collective-permute-start = (bf16[256,768]{1,0:T(8,128)(2,1)S(1)}, bf16[256,768]{1,0:T(8,128)(2,1)S(1)}, u32[]{:S(2)}, u32[]{:S(2)}) collective-permute-start(bf16[256,768]{1,0:T(8,128)(2,1)S(1)} %get-tuple-element.25), channel_id=1, source_target_pairs={{0,128},{128,256},{256,384},{384,0},{1,129},{129,257},{257,385},{3... | collective-permute-start | bytes 1179656 | tf_op jit(solution)/shard_map/ppermute | solution.py:191
  118.6 20.0 %collective-permute-start.7 = (bf16[96,1024]{1,0:T(8,128)(2,1)S(1)}, bf16[96,1024]{1,0:T(8,128)(2,1)S(1)}, u32[]{:S(2)}, u32[]{:S(2)}) collective-permute-start(bf16[96,1024]{1,0:T(8,128)(2,1)S(1)} %add_convert_fusion.1.refs_0_), channel_id=1, source_target_pairs={{0,256},{128,384},{256,0},{384,128},{1,257},{129,385},{257,1},{385... | collective-permute-start | bytes 589832 | tf_op jit(solution)/shard_map/ppermute | solution.py:191
  123.0 15.7 %collective-permute-start.8 = (bf16[96,1024]{1,0:T(8,128)(2,1)S(1)}, bf16[96,1024]{1,0:T(8,128)(2,1)S(1)}, u32[]{:S(2)}, u32[]{:S(2)}) collective-permute-start(bf16[96,1024]{1,0:T(8,128)(2,1)S(1)} %add_convert_fusion.1.refs_0_), channel_id=1, source_target_pairs={{0,384},{128,0},{256,128},{384,256},{1,385},{129,1},{257,129},{385... | collective-permute-start | bytes 589832 | tf_op jit(solution)/shard_map/ppermute | solution.py:191

commit v3 on v2

--- a/solution.py
+++ b/solution.py
@@ -11,9 +11,11 @@
 SLOTS = 4
 MSG = 2 * SLOTS
 LANES = 128
+CHUNKS = 4
 F32 = jnp.float32
 BF16 = jnp.bfloat16
 VMEM = pl.BlockSpec(memory_space=pltpu.VMEM)
+ANY = pl.BlockSpec(memory_space=pl.ANY)
 SMEM = pl.BlockSpec(memory_space=pltpu.SMEM)
 MIB = 1024 * 1024
 
@@ -28,14 +30,14 @@
 
 
 def call(
-    body, name, out_shape, in_specs, scratch=(), flops=0, bytes_accessed=0, vmem=16 * MIB
+    body, name, out_shape, in_specs, scratch=(), flops=0, bytes_accessed=0, vmem=16 * MIB, out=VMEM
 ):
     return pl.pallas_call(
         body,
         name=name,
         out_shape=out_shape,
         in_specs=in_specs,
-        out_specs=jax.tree.map(lambda _: VMEM, out_shape),
+        out_specs=jax.tree.map(lambda _: out, out_shape),
         scratch_shapes=list(scratch),
         compiler_params=pltpu.CompilerParams(vmem_limit_bytes=vmem),
         cost_estimate=pl.CostEstimate(
@@ -114,21 +116,41 @@
     out[:, half:] = both[count:].astype(BF16)
 
 
-def place_body(ranks, me, *refs):
-    pieces, out = refs[:-1], refs[-1]
-    piece = pieces[0].shape[0]
-    for i in range(ranks):
-        at = lax.rem(me[0] + ranks - i, ranks) * piece
-        out[pl.ds(pl.multiple_of(at, 16), piece), :] = pieces[i][...]
-
-
-def rows_body(recv, w_gate, w_up, w_down, back, tok, og, gu, hid, wide, narrow):
-    total, features = recv.shape
-    peers = total // MSG
-    hidden = w_gate.shape[1]
+def expert_body(
+    ranks, me, recv_hbm, w_gate_hbm, w_up_hbm, w_down_hbm,
+    back_hbm, down_a_hbm, down_b_hbm, gate_send_hbm, up_send_hbm, gate_keep_hbm, up_keep_hbm,
+    recv, w_gate, w_up, w_down,
+    back, down_a, down_b, gate_send, up_send, gate_keep, up_keep,
+    wide, narrow, tok, og, gate_rows, up_rows, hid, total, in_sems, out_sems,
+):
+    rows_in, features = recv.shape
+    peers = rows_in // MSG
     half = features // 2
-    for c in range(features // LANES):
-        wide[c] = recv[:, c * LANES : (c + 1) * LANES].astype(F32)
+    step = rows_in // CHUNKS
+    arrivals = []
+    for n in range(CHUNKS):
+        at = pl.ds(n * step, step)
+        arrivals.append(pltpu.make_async_copy(recv_hbm.at[at], recv.at[at], in_sems.at[n]))
+    for n, (source, target) in enumerate(
+        [(w_gate_hbm, w_gate), (w_up_hbm, w_up), (w_down_hbm, w_down)]
+    ):
+        arrivals.append(pltpu.make_async_copy(source, target, in_sems.at[CHUNKS + n]))
+    for copy in arrivals:
+        copy.start()
+    departures = []
+
+    def send_out(source, target):
+        copy = pltpu.make_async_copy(source, target, out_sems.at[len(departures)])
+        copy.start()
+        departures.append(copy)
+
+    for n in range(CHUNKS):
+        arrivals[n].wait()
+        at = pl.ds(n * step, step)
+        for c in range(features // LANES):
+            wide[c, at, :] = recv[at, c * LANES : (c + 1) * LANES].astype(F32)
+    for copy in arrivals[CHUNKS:]:
+        copy.wait()
     for part in range(2):
         first = part * (SLOTS // 2)
         rows = pl.ds(first * peers, 2 * peers)
@@ -147,8 +169,8 @@
         hid[rows, :] = (act * up_proj).astype(BF16)
         gate_grad = (hidden_grad * up_proj * s * (1.0 + gate_pre * (1.0 - s))).astype(BF16)
         up_grad = (hidden_grad * act).astype(BF16)
-        gu[rows, :hidden] = gate_grad
-        gu[rows, hidden:] = up_grad
+        gate_rows[rows, :] = gate_grad
+        up_rows[rows, :] = up_grad
         grads = dot(gate_grad, w_gate[...], NT) + dot(up_grad, w_up[...], NT)
         for s in range(2):
             piece = grads[s * peers : (s + 1) * peers, :]
@@ -159,43 +181,38 @@
                 narrow[c, pl.ds(first + s + SLOTS, peers, MSG), :] = high
     for c in range(half // LANES):
         back[:, c * LANES : (c + 1) * LANES] = narrow[c].astype(BF16)
-
-
-def weights_body(ranks, me, left, right, own, *rest):
-    sends, total = rest[:-1], rest[-1]
-    total[...] = dot(left[...], right[...], TN)
-    piece = own.shape[0]
-    own[...] = total[pl.ds(pl.multiple_of(me[0] * piece, 8), piece), :]
-    for i in range(1, ranks):
-        at = lax.rem(me[0] + i, ranks) * piece
-        sends[i - 1][...] = total[pl.ds(pl.multiple_of(at, 8), piece), :].astype(BF16)
-
-
-def weight_pieces(name, ranks, me, left, right):
-    rows, depth, width = left.shape[0], left.shape[1], right.shape[1]
-    piece = depth // ranks
-    out = [jax.ShapeDtypeStruct((piece, width), F32)]
-    out += [jax.ShapeDtypeStruct((piece, width), BF16)] * (ranks - 1)
-    return call(
-        functools.partial(weights_body, ranks),
-        name,
-        out,
-        [SMEM, VMEM, VMEM],
-        [pltpu.VMEM((depth, width), F32)],
-        2 * rows * depth * width,
-        2 * (rows * (depth + width) + 2 * depth * width),
-    )(me, left, right)
-
-
-def shift(value, ranks, by):
-    return lax.ppermute(value, "dp", [(s, (s + by) % ranks) for s in range(ranks)])
-
-
-def sum_over(ranks, pieces):
-    total = pieces[0]
-    for i in range(1, ranks):
-        total = total + shift(pieces[i], ranks, i).astype(F32)
-    return total.astype(BF16)
+    send_out(back, back_hbm)
+    piece = gate_keep.shape[0] // 2
+    even = me[0] + 1 - 2 * lax.rem(me[0], 2)
+    mirror = ranks - 1 - me[0]
+    opposite = ranks - 1 - even
+
+    def part_of(index):
+        return total[pl.ds(pl.multiple_of(index * piece, 16), piece), :]
+
+    for grads, keep, send, keep_hbm, send_hbm, near, far in (
+        (gate_rows, gate_keep, gate_send, gate_keep_hbm, gate_send_hbm, even, mirror),
+        (up_rows, up_keep, up_send, up_keep_hbm, up_send_hbm, mirror, even),
+    ):
+        total[...] = dot(tok[...], grads[...], TN)
+        keep[:piece, :] = part_of(me[0])
+        keep[piece:, :] = part_of(near)
+        send_out(keep, keep_hbm)
+        send[:piece, :] = part_of(far).astype(BF16)
+        send[piece:, :] = part_of(opposite).astype(BF16)
+        send_out(send, send_hbm)
+    down = dot(hid[...], og[...], TN)
+    cut = down_a.shape[0]
+    down_a[...] = down[:cut].astype(BF16)
+    send_out(down_a, down_a_hbm)
+    down_b[...] = down[cut:].astype(BF16)
+    send_out(down_b, down_b_hbm)
+    for copy in departures:
+        copy.wait()
+
+
+def add(kept, received):
+    return kept.astype(F32) + received.astype(F32)
 
 
 def shards(tokens, cotangent, routes, combine, hot_experts, extra_slots, w_gate, w_up, w_down):
@@ -212,7 +229,7 @@
             jax.ShapeDtypeStruct((total, features), BF16),
             jax.ShapeDtypeStruct((2 * count, total), BF16),
         ],
-        [pl.BlockSpec(memory_space=pltpu.HBM)] * 6,
+        [ANY] * 6,
         [
             pltpu.VMEM((2 * count, features), BF16),
             pltpu.VMEM(routes.shape[::-1], jnp.int32),
@@ -226,38 +243,59 @@
         64 * MIB - 65536,
     )(tokens, cotangent, routes.T, combine.T, hot_experts, extra_slots)
     recv = lax.all_to_all(send, "expert", split_axis=0, concat_axis=0, tiled=True)
-    back, tok, og, gu, hid = call(
-        rows_body,
-        "rows",
-        [
-            jax.ShapeDtypeStruct((total, features // 2), BF16),
-            jax.ShapeDtypeStruct((rows, features), BF16),
-            jax.ShapeDtypeStruct((rows, features), BF16),
-            jax.ShapeDtypeStruct((rows, 2 * hidden), BF16),
-            jax.ShapeDtypeStruct((rows, hidden), BF16),
-        ],
-        [VMEM] * 4,
-        [
+    me = lax.axis_index("dp").astype(jnp.int32).reshape(1)
+    piece = features // ranks
+    cut = hidden // 2
+    pieces = [
+        jax.ShapeDtypeStruct((total, features // 2), BF16),
+        jax.ShapeDtypeStruct((cut, features), BF16),
+        jax.ShapeDtypeStruct((cut, features), BF16),
+        jax.ShapeDtypeStruct((2 * piece, hidden), BF16),
+        jax.ShapeDtypeStruct((2 * piece, hidden), BF16),
+        jax.ShapeDtypeStruct((2 * piece, hidden), F32),
+        jax.ShapeDtypeStruct((2 * piece, hidden), F32),
+    ]
+    operands = (recv, w_gate[0], w_up[0], w_down[0])
+    back, down_a, down_b, gate_send, up_send, gate_keep, up_keep = call(
+        functools.partial(expert_body, ranks),
+        "expert",
+        pieces,
+        [SMEM] + [ANY] * 4,
+        [pltpu.VMEM(a.shape, a.dtype) for a in operands]
+        + [pltpu.VMEM(a.shape, a.dtype) for a in pieces]
+        + [
             pltpu.VMEM((features // LANES, total, LANES), F32),
             pltpu.VMEM((features // 2 // LANES, total, LANES), F32),
+            pltpu.VMEM((rows, features), BF16),
+            pltpu.VMEM((rows, features), BF16),
+            pltpu.VMEM((rows, hidden), BF16),
+            pltpu.VMEM((rows, hidden), BF16),
+            pltpu.VMEM((rows, hidden), BF16),
+            pltpu.VMEM((features, hidden), F32),
+            pltpu.SemaphoreType.DMA((CHUNKS + 3,)),
+            pltpu.SemaphoreType.DMA((len(pieces),)),
         ],
-        10 * rows * features * hidden,
-        2 * (total * features * 2 + 3 * features * hidden),
-        32 * MIB,
-    )(recv, w_gate[0], w_up[0], w_down[0])
+        16 * rows * features * hidden,
+        2 * (total * features * 2 + 6 * features * hidden),
+        64 * MIB - 65536,
+        ANY,
+    )(me, *operands)
     returned = lax.all_to_all(back, "expert", split_axis=0, concat_axis=0, tiled=True)
-    me = lax.axis_index("dp").astype(jnp.int32).reshape(1)
-    down = sum_over(ranks, weight_pieces("down_grad", ranks, me, hid, og))
-    grad_down = call(
-        functools.partial(place_body, ranks),
-        "place",
-        jax.ShapeDtypeStruct((hidden, features), BF16),
-        [SMEM] + [VMEM] * ranks,
-        (),
-        0,
-        4 * hidden * features,
-    )(me, down, *(shift(down, ranks, i) for i in range(1, ranks)))
-    gate_up = sum_over(ranks, weight_pieces("gate_up_grad", ranks, me, tok, gu))
+
+    def even(value):
+        return lax.ppermute(value, "dp", [(i, i ^ 1) for i in range(ranks)])
+
+    def mirror(value):
+        return lax.ppermute(value, "dp", [(i, ranks - 1 - i) for i in range(ranks)])
+
+    sum_a = add(down_a, even(down_a)).astype(BF16)
+    sum_b = add(down_b, mirror(down_b)).astype(BF16)
+    gate_in, up_in = mirror(gate_send), even(up_send)
+    down = jnp.concatenate([add(sum_a, mirror(sum_a)), add(sum_b, even(sum_b))], axis=0)
+    gate_next = even(add(gate_keep[piece:], gate_in[piece:]).astype(BF16))
+    up_next = mirror(add(up_keep[piece:], up_in[piece:]).astype(BF16))
+    grad_gate = add(add(gate_keep[:piece], gate_in[:piece]), gate_next)
+    grad_up = add(add(up_keep[:piece], up_in[:piece]), up_next)
     token_grads = call(
         token_body,
         "token_grad",
@@ -269,9 +307,9 @@
     )(pick_t, returned)
     return (
         token_grads,
-        gate_up[None, :, :hidden],
-        gate_up[None, :, hidden:],
-        grad_down[None],
+        grad_gate[None].astype(BF16),
+        grad_up[None].astype(BF16),
+        down[None].astype(BF16),
     )
 
 

time: 144 us -> 132 us (0.917)
  blocking collectives: 70.7 us -> 0 us
  waiting for transfers between devices: 18 us -> 58.7 us
  starting transfers between devices: 36.4 us -> 50.3 us
  other arithmetic: 0.28 us -> 6.76 us
  local copies, waits for them, and re-layouts: 2.81 us -> 0.02 us
  Pallas kernels: 12.5 us -> 14 us
    all_to_all x1 -> x0, blocking collectives: 70.7 us -> none  [shards(): lax.all_to_all(send, 'expert', split_axis=0, concat_axis=0, tiled=True)]
    all_to_all x0 -> x1, waiting for transfers between devices: none -> 51.8 us  [shards(): lax.all_to_all(send, 'expert', split_axis=0, concat_axis=0, tiled=True)]
    all_to_all x0 -> x1, starting transfers between devices: none -> 18.9 us  [shards(): lax.all_to_all(send, 'expert', split_axis=0, concat_axis=0, tiled=True)]
    ppermute x9 -> x8, waiting for transfers between devices: 18 us -> 6.39 us  [the longest x4 6.38 us: mirror(): return lax.ppermute(value, 'dp', [(i, ranks - 1 - i) for i in range(ranks)])]
    ppermute x9 -> x8, starting transfers between devices: 28.6 us -> 23 us  [the longest x4 13.1 us: mirror(): return lax.ppermute(value, 'dp', [(i, ranks - 1 - i) for i in range(ranks)])]
    convert_element_type x2 -> x6, other arithmetic: 0.28 us -> 5.57 us  [the longest x1 1.68 us: shards(): grad_gate[None].astype(BF16)]
    unnamed x12 -> x10, local copies, waits for them, and re-layouts: 2.03 us -> 0.02 us
    pallas_call x4 -> x1, Pallas kernels: 8.26 us -> 9.74 us  [shards(): call(functools.partial(expert_body, ranks), 'expert', pieces, [SMEM] + [A...]
  transfers between devices with their start and end apart: 10 -> 10, of which waited for: 3 -> 3; matrix products, arithmetic and copies ran while one was open for 1% -> 5% of each run, Pallas kernels for 2% -> 0%
where the time goes in v3:
time: 132 us; the launch traced here: 131 us
  waiting for transfers between devices  58.7 us (44%)
  starting transfers between devices  50.3 us (38%)
  Pallas kernels  14 us (11%)
  other arithmetic  6.76 us (5%)
    all_to_all x1, waiting for transfers between devices, shards(): lax.all_to_all(send, 'expert', split_axis=0, concat_axis=0, tiled=True)  51.8 us
    all_to_all x1, starting transfers between devices, shards(): lax.all_to_all(send, 'expert', split_axis=0, concat_axis=0, tiled=True)  18.9 us
    ppermute x4, starting transfers between devices, mirror(): return lax.ppermute(value, 'dp', [(i, ranks - 1 - i) for i in range(ranks)])  13.1 us
    ppermute x4, starting transfers between devices, even(): return lax.ppermute(value, 'dp', [(i, i ^ 1) for i in range(ranks)])  9.86 us
    pallas_call x1, Pallas kernels, shards(): call(functools.partial(expert_body, ranks), 'expert', pieces, [SMEM] + [A...  9.74 us
    all_to_all x1, starting transfers between devices, shards(): lax.all_to_all(back, 'expert', split_axis=0, concat_axis=0, tiled=True)  8.41 us
    ppermute x4, waiting for transfers between devices, mirror(): return lax.ppermute(value, 'dp', [(i, ranks - 1 - i) for i in range(ranks)])  6.38 us
    pallas_call x1, Pallas kernels, shards(): call(functools.partial(dispatch_body, experts), 'dispatch', [jax.ShapeDty...  3.32 us
  transfers between devices with their start and end apart: 10, of which 3 were waited for; matrix products, arithmetic and copies ran while one was open for 5% of the time, Pallas kernels for 0%

profile of v3, /device:TPU:1, one launch (start us, length us, event | category | flops | bytes accessed | tf_op | source)
XLA Modules:
  0.0 130.7 jit_solution(18148346929676570646)
XLA Ops:
  0.6 3.3 %dispatch.1 = (bf16[1024,1024]{1,0:T(8,128)(2,1)}, bf16[64,1024]{1,0:T(8,128)(2,1)}) custom-call(bf16[32,1024]{1,0:T(8,128)(2,1)} %tok_hbm.1, bf16[32,1024]{1,0:T(8,128)(2,1)} %cot_hbm.1, s32[8,32]{1,0:T(8,128)} %bitcast.24, bf16[8,32]{1,0:T(8,128)(2,1)} %bitcast.25, s32[4]{0:T(128)} %hot_hbm.1, s32[4]{0:T(128)} %extra_hbm.1), custom_call_target="tpu_custom_call" | custom-call | flops 134217728 | bytes 2097152 | tf_op jit(solution)/shard_map/dispatch/pallas_call | solution.py:225
  4.0 18.9 %all-to-all-start = ((bf16[128,8,1024]{2,1,0:T(8,128)(2,1)}), bf16[128,8,1024]{2,1,0:T(8,128)(2,1)}, u32[]{:S(2)}, u32[]{:S(2)}) async-start(bf16[128,8,1024]{2,1,0:T(8,128)(2,1)} %bitcast.19), calls=%async_computation | async-start | bytes 4194304 | tf_op jit(solution)/shard_map/all_to_all | solution.py:245
  22.9 51.8 %all-to-all-done = bf16[128,8,1024]{2,1,0:T(8,128)(2,1)} async-done(((bf16[128,8,1024]{2,1,0:T(8,128)(2,1)}), bf16[128,8,1024]{2,1,0:T(8,128)(2,1)}, u32[]{:S(2)}, u32[]{:S(2)}) %all-to-all-start) | async-done | bytes 2097184 | tf_op jit(solution)/shard_map/all_to_all | solution.py:245
  74.6 9.7 %expert.1 = (bf16[1024,512]{1,0:T(8,128)(2,1)}, bf16[192,1024]{1,0:T(8,128)(2,1)}, bf16[192,1024]{1,0:T(8,128)(2,1)}, bf16[512,384]{1,0:T(8,128)(2,1)}, bf16[512...) custom-call(s32[1]{0:T(128)} %bitcast.2.me, bf16[1024,1024]{1,0:T(8,128)(2,1)} %bitcast.4.recv_hbm, ...), custom_call_target="tpu_custom_call" | custom-call | flops 3221225472 | bytes 8912896 | tf_op jit(solution)/shard_map/expert/pallas_call | solution.py:259
  84.4 4.5 %collective-permute-start = (bf16[512,384]{1,0:T(8,128)(2,1)}, bf16[512,384]{1,0:T(8,128)(2,1)}, u32[]{:S(2)}, u32[]{:S(2)}) collective-permute-start(bf16[512,384]{1,0:T(8,128)(2,1)} %get-tuple-element.17), channel_id=1, source_target_pairs={{0,384},{128,256},{256,128},{384,0},{1,385},{129,257},{257,129},{3... | collective-permute-start | bytes 1179656 | tf_op jit(solution)/shard_map/ppermute | solution.py:289
  89.0 1.9 %collective-permute-start.2 = (bf16[512,384]{1,0:T(8,128)(2,1)}, bf16[512,384]{1,0:T(8,128)(2,1)}, u32[]{:S(2)}, u32[]{:S(2)}) collective-permute-start(bf16[512,384]{1,0:T(8,128)(2,1)} %get-tuple-element.19), channel_id=1, source_target_pairs={{0,128},{128,0},{256,384},{384,256},{1,129},{129,1},{257,385},{385... | collective-permute-start | bytes 1179656 | tf_op jit(solution)/shard_map/ppermute | solution.py:286
  90.9 8.4 %all-to-all-start.1 = ((bf16[128,8,512]{2,1,0:T(8,128)(2,1)}), bf16[128,8,512]{2,1,0:T(8,128)(2,1)S(1)}, u32[]{:S(2)}, u32[]{:S(2)}) async-start(bf16[128,8,512]{2,1,0:T(8,128)(2,1)} %bitcast.20), calls=%async_computation.1 | async-start | bytes 2097152 | tf_op jit(solution)/shard_map/all_to_all | solution.py:283
  99.3 3.4 %collective-permute-start.4 = (bf16[192,1024]{1,0:T(8,128)(2,1)}, bf16[192,1024]{1,0:T(8,128)(2,1)S(1)}, u32[]{:S(2)}, u32[]{:S(2)}) collective-permute-start(bf16[192,1024]{1,0:T(8,128)(2,1)} %get-tuple-element.20), channel_id=1, source_target_pairs={{0,128},{128,0},{256,384},{384,256},{1,129},{129,1},{257,385},{385... | collective-permute-start | bytes 1179656 | tf_op jit(solution)/shard_map/ppermute | solution.py:286
  102.8 2.1 %collective-permute-start.6 = (bf16[192,1024]{1,0:T(8,128)(2,1)S(1)}, bf16[192,1024]{1,0:T(8,128)(2,1)S(1)}, u32[]{:S(2)}, u32[]{:S(2)}) collective-permute-start(bf16[192,1024]{1,0:T(8,128)(2,1)S(1)} %copy-done.3), channel_id=1, source_target_pairs={{0,384},{128,256},{256,128},{384,0},{1,385},{129,257},{257,129},{3... | collective-permute-start | bytes 1179656 | tf_op jit(solution)/shard_map/ppermute | solution.py:289
  104.9 1.0 add_convert_fusion.7
  105.9 1.9 %collective-permute-start.1 = (bf16[256,384]{1,0:T(8,128)(2,1)S(1)}, bf16[256,384]{1,0:T(8,128)(2,1)S(1)}, u32[]{:S(2)}, u32[]{:S(2)}) collective-permute-start(bf16[256,384]{1,0:T(8,128)(2,1)S(1)} %add_convert_fusion.7), channel_id=1, source_target_pairs={{0,128},{128,0},{256,384},{384,256},{1,129},{129,1},{257,385},{385... | collective-permute-start | bytes 589832 | tf_op jit(solution)/shard_map/ppermute | solution.py:286
  107.8 1.0 add_convert_fusion.5
  108.8 4.4 %collective-permute-start.3 = (bf16[256,384]{1,0:T(8,128)(2,1)S(1)}, bf16[256,384]{1,0:T(8,128)(2,1)S(1)}, u32[]{:S(2)}, u32[]{:S(2)}) collective-permute-start(bf16[256,384]{1,0:T(8,128)(2,1)S(1)} %add_convert_fusion.5), channel_id=1, source_target_pairs={{0,384},{128,256},{256,128},{384,0},{1,385},{129,257},{257,129},{3... | collective-permute-start | bytes 589832 | tf_op jit(solution)/shard_map/ppermute | solution.py:289
  113.2 0.1 add_convert_fusion.3
  113.4 2.1 %collective-permute-start.5 = (bf16[192,1024]{1,0:T(8,128)(2,1)S(1)}, bf16[192,1024]{1,0:T(8,128)(2,1)S(1)}, u32[]{:S(2)}, u32[]{:S(2)}) collective-permute-start(bf16[192,1024]{1,0:T(8,128)(2,1)S(1)} %add_convert_fusion.3), channel_id=1, source_target_pairs={{0,384},{128,256},{256,128},{384,0},{1,385},{129,257},{257,129},{3... | collective-permute-start | bytes 1179656 | tf_op jit(solution)/shard_map/ppermute | solution.py:289
  115.5 0.1 add_convert_fusion.1
  115.6 2.6 %collective-permute-start.7 = (bf16[192,1024]{1,0:T(8,128)(2,1)S(1)}, bf16[192,1024]{1,0:T(8,128)(2,1)S(1)}, u32[]{:S(2)}, u32[]{:S(2)}) collective-permute-start(bf16[192,1024]{1,0:T(8,128)(2,1)S(1)} %add_convert_fusion.1), channel_id=1, source_target_pairs={{0,128},{128,0},{256,384},{384,256},{1,129},{129,1},{257,385},{385... | collective-permute-start | bytes 1179656 | tf_op jit(solution)/shard_map/ppermute | solution.py:286
  118.2 1.7 %fusion.2 = bf16[1,256,384]{2,1,0:T(8,128)(2,1)} fusion(bf16[256,384]{1,0:T(8,128)(2,1)S(1)} %collective-permute-done.1, f32[512,384]{1,0:T(8,128)S(1)} %copy-done.2, bf16[512,384]{1,0:T(8,128)(2,1)} %collective-permute-done), kind=kLoop, calls=%fused_computation.11 | loop fusion | flops 491520 | bytes 983040 | tf_op jit(solution)/shard_map/convert_element_type | solution.py:310
  119.9 1.7 %fusion.3 = bf16[1,256,384]{2,1,0:T(8,128)(2,1)} fusion(bf16[256,384]{1,0:T(8,128)(2,1)S(1)} %collective-permute-done.3, f32[512,384]{1,0:T(8,128)S(1)} %copy-done.1, bf16[512,384]{1,0:T(8,128)(2,1)} %collective-permute-done.2), kind=kLoop, calls=%fused_computation.12 | loop fusion | flops 491520 | bytes 983040 | tf_op jit(solution)/shard_map/convert_element_type | solution.py:311
  121.6 6.4 %collective-permute-done.5 = bf16[192,1024]{1,0:T(8,128)(2,1)S(1)} collective-permute-done((bf16[192,1024]{1,0:T(8,128)(2,1)S(1)}, bf16[192,1024]{1,0:T(8,128)(2,1)S(1)}, u32[]{:S(2)}, u32[]{:S(2)}) %collective-permute-start.5) | collective-permute-done | bytes 393248 | tf_op jit(solution)/shard_map/ppermute | solution.py:289
  128.1 0.1 fusion.1
  128.3 0.9 pad_maximum_fusion
  129.2 0.6 all-to-all-done.1
  129.8 0.9 token_grad.1
  (18 shorter events, 0.2 us)
Async XLA Ops:
  4.0 70.7 %all-to-all-start = ((bf16[128,8,1024]{2,1,0:T(8,128)(2,1)}), bf16[128,8,1024]{2,1,0:T(8,128)(2,1)}, u32[]{:S(2)}, u32[]{:S(2)}) async-start(bf16[128,8,1024]{2,1,0:T(8,128)(2,1)} %bitcast.19), calls=%async_computation | async-start | bytes 4194304 | tf_op jit(solution)/shard_map/all_to_all | solution.py:245
  84.4 18.4 %copy-start.3 = (bf16[192,1024]{1,0:T(8,128)(2,1)S(1)}, bf16[192,1024]{1,0:T(8,128)(2,1)}, u32[]{:S(2)}) copy-start(bf16[192,1024]{1,0:T(8,128)(2,1)} %get-tuple-element.21) | copy-start | bytes 1179652
  84.4 20.5 %copy-start.2 = (f32[512,384]{1,0:T(8,128)S(1)}, f32[512,384]{1,0:T(8,128)}, u32[]{:S(2)}) copy-start(f32[512,384]{1,0:T(8,128)} %get-tuple-element.16) | copy-start | bytes 2359300
  84.4 23.4 %copy-start.1 = (f32[512,384]{1,0:T(8,128)S(1)}, f32[512,384]{1,0:T(8,128)}, u32[]{:S(2)}) copy-start(f32[512,384]{1,0:T(8,128)} %get-tuple-element.18) | copy-start | bytes 2359300
  84.4 20.5 %collective-permute-start = (bf16[512,384]{1,0:T(8,128)(2,1)}, bf16[512,384]{1,0:T(8,128)(2,1)}, u32[]{:S(2)}, u32[]{:S(2)}) collective-permute-start(bf16[512,384]{1,0:T(8,128)(2,1)} %get-tuple-element.17), channel_id=1, source_target_pairs={{0,384},{128,256},{256,128},{384,0},{1,385},{129,257},{257,129},{3... | collective-permute-start | bytes 1179656 | tf_op jit(solution)/shard_map/ppermute | solution.py:289
  89.0 18.9 %collective-permute-start.2 = (bf16[512,384]{1,0:T(8,128)(2,1)}, bf16[512,384]{1,0:T(8,128)(2,1)}, u32[]{:S(2)}, u32[]{:S(2)}) collective-permute-start(bf16[512,384]{1,0:T(8,128)(2,1)} %get-tuple-element.19), channel_id=1, source_target_pairs={{0,128},{128,0},{256,384},{384,256},{1,129},{129,1},{257,385},{385... | collective-permute-start | bytes 1179656 | tf_op jit(solution)/shard_map/ppermute | solution.py:286
  90.9 22.3 %copy-start.4 = (bf16[192,1024]{1,0:T(8,128)(2,1)S(1)}, bf16[192,1024]{1,0:T(8,128)(2,1)}, u32[]{:S(2)}) copy-start(bf16[192,1024]{1,0:T(8,128)(2,1)} %get-tuple-element.20) | copy-start | bytes 1179652
  90.9 38.9 %all-to-all-start.1 = ((bf16[128,8,512]{2,1,0:T(8,128)(2,1)}), bf16[128,8,512]{2,1,0:T(8,128)(2,1)S(1)}, u32[]{:S(2)}, u32[]{:S(2)}) async-start(bf16[128,8,512]{2,1,0:T(8,128)(2,1)} %bitcast.20), calls=%async_computation.1 | async-start | bytes 2097152 | tf_op jit(solution)/shard_map/all_to_all | solution.py:283
  99.3 13.9 %collective-permute-start.4 = (bf16[192,1024]{1,0:T(8,128)(2,1)}, bf16[192,1024]{1,0:T(8,128)(2,1)S(1)}, u32[]{:S(2)}, u32[]{:S(2)}) collective-permute-start(bf16[192,1024]{1,0:T(8,128)(2,1)} %get-tuple-element.20), channel_id=1, source_target_pairs={{0,128},{128,0},{256,384},{384,256},{1,129},{129,1},{257,385},{385... | collective-permute-start | bytes 1179656 | tf_op jit(solution)/shard_map/ppermute | solution.py:286
  102.8 12.7 %collective-permute-start.6 = (bf16[192,1024]{1,0:T(8,128)(2,1)S(1)}, bf16[192,1024]{1,0:T(8,128)(2,1)S(1)}, u32[]{:S(2)}, u32[]{:S(2)}) collective-permute-start(bf16[192,1024]{1,0:T(8,128)(2,1)S(1)} %copy-done.3), channel_id=1, source_target_pairs={{0,384},{128,256},{256,128},{384,0},{1,385},{129,257},{257,129},{3... | collective-permute-start | bytes 1179656 | tf_op jit(solution)/shard_map/ppermute | solution.py:289
  105.9 12.3 %collective-permute-start.1 = (bf16[256,384]{1,0:T(8,128)(2,1)S(1)}, bf16[256,384]{1,0:T(8,128)(2,1)S(1)}, u32[]{:S(2)}, u32[]{:S(2)}) collective-permute-start(bf16[256,384]{1,0:T(8,128)(2,1)S(1)} %add_convert_fusion.7), channel_id=1, source_target_pairs={{0,128},{128,0},{256,384},{384,256},{1,129},{129,1},{257,385},{385... | collective-permute-start | bytes 589832 | tf_op jit(solution)/shard_map/ppermute | solution.py:286
  108.8 11.1 %collective-permute-start.3 = (bf16[256,384]{1,0:T(8,128)(2,1)S(1)}, bf16[256,384]{1,0:T(8,128)(2,1)S(1)}, u32[]{:S(2)}, u32[]{:S(2)}) collective-permute-start(bf16[256,384]{1,0:T(8,128)(2,1)S(1)} %add_convert_fusion.5), channel_id=1, source_target_pairs={{0,384},{128,256},{256,128},{384,0},{1,385},{129,257},{257,129},{3... | collective-permute-start | bytes 589832 | tf_op jit(solution)/shard_map/ppermute | solution.py:289
  113.4 14.6 %collective-permute-start.5 = (bf16[192,1024]{1,0:T(8,128)(2,1)S(1)}, bf16[192,1024]{1,0:T(8,128)(2,1)S(1)}, u32[]{:S(2)}, u32[]{:S(2)}) collective-permute-start(bf16[192,1024]{1,0:T(8,128)(2,1)S(1)} %add_convert_fusion.3), channel_id=1, source_target_pairs={{0,384},{128,256},{256,128},{384,0},{1,385},{129,257},{257,129},{3... | collective-permute-start | bytes 1179656 | tf_op jit(solution)/shard_map/ppermute | solution.py:289
  115.6 12.5 %collective-permute-start.7 = (bf16[192,1024]{1,0:T(8,128)(2,1)S(1)}, bf16[192,1024]{1,0:T(8,128)(2,1)S(1)}, u32[]{:S(2)}, u32[]{:S(2)}) collective-permute-start(bf16[192,1024]{1,0:T(8,128)(2,1)S(1)} %add_convert_fusion.1), channel_id=1, source_target_pairs={{0,128},{128,0},{256,384},{384,256},{1,129},{129,1},{257,385},{385... | collective-permute-start | bytes 1179656 | tf_op jit(solution)/shard_map/ppermute | solution.py:286
  128.1 1.7 %copy-start = (bf16[64,1024]{1,0:T(8,128)(2,1)S(1)}, bf16[64,1024]{1,0:T(8,128)(2,1)}, u32[]{:S(2)}) copy-start(bf16[64,1024]{1,0:T(8,128)(2,1)} %get-tuple-element.13.pick_t) | copy-start | bytes 393220

commit v4 on v3

--- a/solution.py
+++ b/solution.py
@@ -116,14 +116,56 @@
     out[:, half:] = both[count:].astype(BF16)
 
 
+def pack(half_down, buffer):
+    rows, width = half_down.shape
+    wide = 3 * width // 4
+    extra = rows // 3
+    buffer[:rows, :wide] = half_down[:, :wide]
+    for k in range(3):
+        cols = slice(k * (width - wide), (k + 1) * (width - wide))
+        buffer[rows:, cols] = half_down[k * extra : (k + 1) * extra, wide:]
+
+
+def add(kept, received):
+    return kept.astype(F32) + received.astype(F32)
+
+
+def middle_body(send, keep, received, out):
+    wide = keep.shape[1]
+    narrow = wide // 2
+    out[:, :wide] = add(send[:, :wide], received[:, :wide]).astype(BF16)
+    out[:, wide:] = add(keep[:, :narrow], received[:, wide : wide + narrow]).astype(BF16)
+
+
+def final_body(
+    even_keep, even_first, even_sum, even_second, mirror_keep, mirror_first, mirror_sum, mirror_second,
+    grad_gate, grad_up, grad_down,
+):
+    hidden, width = grad_down.shape
+    cut, wide = hidden // 2, 3 * width // 4
+    extra = cut // 3
+    for top, keep, first, middle, second, out in (
+        (0, even_keep, even_first, even_sum, even_second, grad_up),
+        (cut, mirror_keep, mirror_first, mirror_sum, mirror_second, grad_gate),
+    ):
+        down = add(middle[:, :wide], second[:, :wide]).astype(BF16)
+        grad_down[top : top + cut, :wide] = down[:cut]
+        for k in range(3):
+            cols = slice(k * (width - wide), (k + 1) * (width - wide))
+            grad_down[top + k * extra : top + (k + 1) * extra, wide:] = down[cut:, cols]
+        own = add(keep[:, hidden:], first[:, wide + hidden :])
+        out[...] = add(own, second[:, wide:]).astype(BF16)
+
+
 def expert_body(
     ranks, me, recv_hbm, w_gate_hbm, w_up_hbm, w_down_hbm,
-    back_hbm, down_a_hbm, down_b_hbm, gate_send_hbm, up_send_hbm, gate_keep_hbm, up_keep_hbm,
-    recv, w_gate, w_up, w_down,
-    back, down_a, down_b, gate_send, up_send, gate_keep, up_keep,
-    wide, narrow, tok, og, gate_rows, up_rows, hid, total, in_sems, out_sems,
+    back_hbm, even_send_hbm, mirror_send_hbm, even_keep_hbm, mirror_keep_hbm,
+    recv, w_in, w_down,
+    back, even_send, mirror_send, even_keep, mirror_keep,
+    wide, narrow, tok, og, pre, grad, in_rows, hid, total, in_sems, out_sems,
 ):
     rows_in, features = recv.shape
+    hidden = w_down.shape[0]
     peers = rows_in // MSG
     half = features // 2
     step = rows_in // CHUNKS
@@ -132,7 +174,11 @@
         at = pl.ds(n * step, step)
         arrivals.append(pltpu.make_async_copy(recv_hbm.at[at], recv.at[at], in_sems.at[n]))
     for n, (source, target) in enumerate(
-        [(w_gate_hbm, w_gate), (w_up_hbm, w_up), (w_down_hbm, w_down)]
+        [
+            (w_gate_hbm, w_in.at[:, pl.ds(0, hidden)]),
+            (w_up_hbm, w_in.at[:, pl.ds(hidden, hidden)]),
+            (w_down_hbm, w_down),
+        ]
     ):
         arrivals.append(pltpu.make_async_copy(source, target, in_sems.at[CHUNKS + n]))
     for copy in arrivals:
@@ -149,70 +195,63 @@
         at = pl.ds(n * step, step)
         for c in range(features // LANES):
             wide[c, at, :] = recv[at, c * LANES : (c + 1) * LANES].astype(F32)
+    for s in range(SLOTS):
+        at = pl.ds(s * peers, peers)
+        for c in range(features // LANES):
+            cols = slice(c * LANES, (c + 1) * LANES)
+            tok[at, cols] = wide[c, pl.ds(s, peers, MSG), :].astype(BF16)
+            og[at, cols] = wide[c, pl.ds(s + SLOTS, peers, MSG), :].astype(BF16)
     for copy in arrivals[CHUNKS:]:
         copy.wait()
-    for part in range(2):
-        first = part * (SLOTS // 2)
-        rows = pl.ds(first * peers, 2 * peers)
-        for s in range(2):
-            at = pl.ds((first + s) * peers, peers)
-            for c in range(features // LANES):
-                cols = slice(c * LANES, (c + 1) * LANES)
-                tok[at, cols] = wide[c, pl.ds(first + s, peers, MSG), :].astype(BF16)
-                og[at, cols] = wide[c, pl.ds(first + s + SLOTS, peers, MSG), :].astype(BF16)
-        x, g = tok[rows, :], og[rows, :]
-        gate_pre = dot(x, w_gate[...], NN)
-        up_proj = dot(x, w_up[...], NN)
-        hidden_grad = dot(g, w_down[...], NT)
-        s = jax.nn.sigmoid(gate_pre)
-        act = gate_pre * s
-        hid[rows, :] = (act * up_proj).astype(BF16)
-        gate_grad = (hidden_grad * up_proj * s * (1.0 + gate_pre * (1.0 - s))).astype(BF16)
-        up_grad = (hidden_grad * act).astype(BF16)
-        gate_rows[rows, :] = gate_grad
-        up_rows[rows, :] = up_grad
-        grads = dot(gate_grad, w_gate[...], NT) + dot(up_grad, w_up[...], NT)
-        for s in range(2):
-            piece = grads[s * peers : (s + 1) * peers, :]
+    for first in range(0, SLOTS * peers, 512):
+        span = slice(first, first + 512)
+        pre[span, :] = dot(tok[span, :], w_in[...], NN)
+        grad[span, :] = dot(og[span, :], w_down[...], NT)
+        for at in range(first, first + 512, 128):
+            rows = slice(at, at + 128)
+            gate_pre, up_proj, hidden_grad = pre[rows, :hidden], pre[rows, hidden:], grad[rows, :]
+            s = jax.nn.sigmoid(gate_pre)
+            act = gate_pre * s
+            hid[rows, :] = (act * up_proj).astype(BF16)
+            gate_grad = hidden_grad * up_proj * s * (1.0 + gate_pre * (1.0 - s))
+            in_rows[rows, :hidden] = gate_grad.astype(BF16)
+            in_rows[rows, hidden:] = (hidden_grad * act).astype(BF16)
+        grads = dot(in_rows[span, :], w_in[...], NT)
+        for s in range(first // peers, (first + 512) // peers):
+            piece = grads[s * peers - first : (s + 1) * peers - first, :]
             for c in range(half // LANES):
                 low = piece[:, c * LANES : (c + 1) * LANES]
                 high = piece[:, half + c * LANES : half + (c + 1) * LANES]
-                narrow[c, pl.ds(first + s, peers, MSG), :] = low
-                narrow[c, pl.ds(first + s + SLOTS, peers, MSG), :] = high
+                narrow[c, pl.ds(s, peers, MSG), :] = low
+                narrow[c, pl.ds(s + SLOTS, peers, MSG), :] = high
     for c in range(half // LANES):
         back[:, c * LANES : (c + 1) * LANES] = narrow[c].astype(BF16)
     send_out(back, back_hbm)
-    piece = gate_keep.shape[0] // 2
+    down = dot(hid[...], og[...], TN).astype(BF16)
+    cut = hidden // 2
+    pack(down[:cut], even_send)
+    pack(down[cut:], mirror_send)
+    total[...] = dot(tok[...], in_rows[...], TN)
+    piece = features // ranks
     even = me[0] + 1 - 2 * lax.rem(me[0], 2)
     mirror = ranks - 1 - me[0]
     opposite = ranks - 1 - even
-
-    def part_of(index):
-        return total[pl.ds(pl.multiple_of(index * piece, 16), piece), :]
-
-    for grads, keep, send, keep_hbm, send_hbm, near, far in (
-        (gate_rows, gate_keep, gate_send, gate_keep_hbm, gate_send_hbm, even, mirror),
-        (up_rows, up_keep, up_send, up_keep_hbm, up_send_hbm, mirror, even),
+    for cols, keep, send, keep_hbm, send_hbm, here, other in (
+        (slice(hidden, 2 * hidden), even_keep, even_send, even_keep_hbm, even_send_hbm, even, mirror),
+        (slice(0, hidden), mirror_keep, mirror_send, mirror_keep_hbm, mirror_send_hbm, mirror, even),
     ):
-        total[...] = dot(tok[...], grads[...], TN)
-        keep[:piece, :] = part_of(me[0])
-        keep[piece:, :] = part_of(near)
+
+        def part_of(index):
+            return total[pl.ds(pl.multiple_of(index * piece, 16), piece), cols].astype(BF16)
+
+        send[:, 2 * hidden : 3 * hidden] = part_of(opposite)
+        send[:, 3 * hidden :] = part_of(here)
+        send_out(send, send_hbm)
+        keep[:, :hidden] = part_of(other)
+        keep[:, hidden:] = part_of(me[0])
         send_out(keep, keep_hbm)
-        send[:piece, :] = part_of(far).astype(BF16)
-        send[piece:, :] = part_of(opposite).astype(BF16)
-        send_out(send, send_hbm)
-    down = dot(hid[...], og[...], TN)
-    cut = down_a.shape[0]
-    down_a[...] = down[:cut].astype(BF16)
-    send_out(down_a, down_a_hbm)
-    down_b[...] = down[cut:].astype(BF16)
-    send_out(down_b, down_b_hbm)
     for copy in departures:
         copy.wait()
-
-
-def add(kept, received):
-    return kept.astype(F32) + received.astype(F32)
 
 
 def shards(tokens, cotangent, routes, combine, hot_experts, extra_slots, w_gate, w_up, w_down):
@@ -245,33 +284,30 @@
     recv = lax.all_to_all(send, "expert", split_axis=0, concat_axis=0, tiled=True)
     me = lax.axis_index("dp").astype(jnp.int32).reshape(1)
     piece = features // ranks
-    cut = hidden // 2
-    pieces = [
-        jax.ShapeDtypeStruct((total, features // 2), BF16),
-        jax.ShapeDtypeStruct((cut, features), BF16),
-        jax.ShapeDtypeStruct((cut, features), BF16),
-        jax.ShapeDtypeStruct((2 * piece, hidden), BF16),
-        jax.ShapeDtypeStruct((2 * piece, hidden), BF16),
-        jax.ShapeDtypeStruct((2 * piece, hidden), F32),
-        jax.ShapeDtypeStruct((2 * piece, hidden), F32),
-    ]
-    operands = (recv, w_gate[0], w_up[0], w_down[0])
-    back, down_a, down_b, gate_send, up_send, gate_keep, up_keep = call(
+    packed = jax.ShapeDtypeStruct((piece, 4 * hidden), BF16)
+    kept = jax.ShapeDtypeStruct((piece, 2 * hidden), BF16)
+    pieces = [jax.ShapeDtypeStruct((total, features // 2), BF16), packed, packed, kept, kept]
+    back, even_send, mirror_send, even_keep, mirror_keep = call(
         functools.partial(expert_body, ranks),
         "expert",
         pieces,
         [SMEM] + [ANY] * 4,
-        [pltpu.VMEM(a.shape, a.dtype) for a in operands]
+        [
+            pltpu.VMEM((total, features), BF16),
+            pltpu.VMEM((features, 2 * hidden), BF16),
+            pltpu.VMEM((hidden, features), BF16),
+        ]
         + [pltpu.VMEM(a.shape, a.dtype) for a in pieces]
         + [
             pltpu.VMEM((features // LANES, total, LANES), F32),
             pltpu.VMEM((features // 2 // LANES, total, LANES), F32),
             pltpu.VMEM((rows, features), BF16),
             pltpu.VMEM((rows, features), BF16),
+            pltpu.VMEM((rows, 2 * hidden), F32),
+            pltpu.VMEM((rows, hidden), F32),
+            pltpu.VMEM((rows, 2 * hidden), BF16),
             pltpu.VMEM((rows, hidden), BF16),
-            pltpu.VMEM((rows, hidden), BF16),
-            pltpu.VMEM((rows, hidden), BF16),
-            pltpu.VMEM((features, hidden), F32),
+            pltpu.VMEM((features, 2 * hidden), F32),
             pltpu.SemaphoreType.DMA((CHUNKS + 3,)),
             pltpu.SemaphoreType.DMA((len(pieces),)),
         ],
@@ -279,7 +315,7 @@
         2 * (total * features * 2 + 6 * features * hidden),
         64 * MIB - 65536,
         ANY,
-    )(me, *operands)
+    )(me, recv, w_gate[0], w_up[0], w_down[0])
     returned = lax.all_to_all(back, "expert", split_axis=0, concat_axis=0, tiled=True)
 
     def even(value):
@@ -288,14 +324,38 @@
     def mirror(value):
         return lax.ppermute(value, "dp", [(i, ranks - 1 - i) for i in range(ranks)])
 
-    sum_a = add(down_a, even(down_a)).astype(BF16)
-    sum_b = add(down_b, mirror(down_b)).astype(BF16)
-    gate_in, up_in = mirror(gate_send), even(up_send)
-    down = jnp.concatenate([add(sum_a, mirror(sum_a)), add(sum_b, even(sum_b))], axis=0)
-    gate_next = even(add(gate_keep[piece:], gate_in[piece:]).astype(BF16))
-    up_next = mirror(add(up_keep[piece:], up_in[piece:]).astype(BF16))
-    grad_gate = add(add(gate_keep[:piece], gate_in[:piece]), gate_next)
-    grad_up = add(add(up_keep[:piece], up_in[:piece]), up_next)
+    def middle(send, keep, received):
+        return call(
+            middle_body,
+            "middle",
+            jax.ShapeDtypeStruct((piece, 3 * hidden), BF16),
+            [VMEM] * 3,
+            (),
+            2 * piece * 3 * hidden,
+            6 * piece * 4 * hidden,
+        )(send, keep, received)
+
+    even_first, mirror_first = even(even_send), mirror(mirror_send)
+    even_sum = middle(even_send, even_keep, even_first)
+    even_second = mirror(even_sum)
+    mirror_sum = middle(mirror_send, mirror_keep, mirror_first)
+    mirror_second = even(mirror_sum)
+    grad_gate, grad_up, grad_down = call(
+        final_body,
+        "final",
+        [
+            jax.ShapeDtypeStruct((piece, hidden), BF16),
+            jax.ShapeDtypeStruct((piece, hidden), BF16),
+            jax.ShapeDtypeStruct((hidden, features), BF16),
+        ],
+        [VMEM] * 8,
+        (),
+        4 * piece * 4 * hidden,
+        12 * piece * 4 * hidden,
+    )(
+        even_keep, even_first, even_sum, even_second,
+        mirror_keep, mirror_first, mirror_sum, mirror_second,
+    )
     token_grads = call(
         token_body,
         "token_grad",
@@ -305,12 +365,7 @@
         2 * total * count * features,
         2 * total * features,
     )(pick_t, returned)
-    return (
-        token_grads,
-        grad_gate[None].astype(BF16),
-        grad_up[None].astype(BF16),
-        down[None].astype(BF16),
-    )
+    return token_grads, grad_gate[None], grad_up[None], grad_down[None]
 
 
 def solution(mesh):

time: 132 us -> 135 us (1.023)
  waiting for transfers between devices: 58.7 us -> 77.7 us
  starting transfers between devices: 50.3 us -> 40.1 us
  other arithmetic: 6.76 us -> 0 us
    ppermute x4 -> x2, waiting for transfers between devices: 0.01 us -> 16.4 us  [even(): return lax.ppermute(value, 'dp', [(i, i ^ 1) for i in range(ranks)])]
    convert_element_type x6 -> x0, other arithmetic: 5.57 us -> none  [the longest x1 1.68 us: shards(): grad_gate[None].astype(BF16)]
    ppermute x4 -> x2, starting transfers between devices: 13.1 us -> 8.12 us  [mirror(): return lax.ppermute(value, 'dp', [(i, ranks - 1 - i) for i in range(ranks)])]
    ppermute x4 -> x2, starting transfers between devices: 9.86 us -> 5.16 us  [even(): return lax.ppermute(value, 'dp', [(i, i ^ 1) for i in range(ranks)])]
    ppermute x4 -> x2, waiting for transfers between devices: 6.38 us -> 9.49 us  [mirror(): return lax.ppermute(value, 'dp', [(i, ranks - 1 - i) for i in range(ranks)])]
    pallas_call x1, Pallas kernels: 9.74 us -> 8.19 us  [shards(): call(functools.partial(expert_body, ranks), 'expert', pieces, [SMEM] + [A...]
    pallas_call x0 -> x3, Pallas kernels: none -> 1.53 us  [the longest x1 1.25 us: shards(): call(final_body, 'final', [jax.ShapeDtypeStruct((piece, hidden), BF16), j...]
  transfers between devices with their start and end apart: 10 -> 6, of which waited for: 3 -> 4; matrix products, arithmetic and copies ran while one was open for 5% -> 0% of each run, Pallas kernels for 0% -> 1%
where the time goes in v4:
time: 135 us; the launch traced here: 133 us
  waiting for transfers between devices  77.7 us (58%)
  starting transfers between devices  40.1 us (30%)
  Pallas kernels  14 us (10%)
    all_to_all x1, waiting for transfers between devices, shards(): lax.all_to_all(send, 'expert', split_axis=0, concat_axis=0, tiled=True)  51.8 us
    all_to_all x1, starting transfers between devices, shards(): lax.all_to_all(send, 'expert', split_axis=0, concat_axis=0, tiled=True)  18.9 us
    ppermute x2, waiting for transfers between devices, even(): return lax.ppermute(value, 'dp', [(i, i ^ 1) for i in range(ranks)])  16.4 us
    ppermute x2, waiting for transfers between devices, mirror(): return lax.ppermute(value, 'dp', [(i, ranks - 1 - i) for i in range(ranks)])  9.49 us
    pallas_call x1, Pallas kernels, shards(): call(functools.partial(expert_body, ranks), 'expert', pieces, [SMEM] + [A...  8.19 us
    ppermute x2, starting transfers between devices, mirror(): return lax.ppermute(value, 'dp', [(i, ranks - 1 - i) for i in range(ranks)])  8.12 us
    all_to_all x1, starting transfers between devices, shards(): lax.all_to_all(back, 'expert', split_axis=0, concat_axis=0, tiled=True)  7.93 us
    ppermute x2, starting transfers between devices, even(): return lax.ppermute(value, 'dp', [(i, i ^ 1) for i in range(ranks)])  5.16 us
  transfers between devices with their start and end apart: 6, of which 4 were waited for; matrix products, arithmetic and copies ran while one was open for 0% of the time, Pallas kernels for 1%

profile of v4, /device:TPU:1, one launch (start us, length us, event | category | flops | bytes accessed | tf_op | source)
XLA Modules:
  0.0 132.6 jit_solution(901554580011066705)
XLA Ops:
  0.6 3.3 %dispatch.1 = (bf16[1024,1024]{1,0:T(8,128)(2,1)}, bf16[64,1024]{1,0:T(8,128)(2,1)}) custom-call(bf16[32,1024]{1,0:T(8,128)(2,1)} %tok_hbm.1, bf16[32,1024]{1,0:T(8,128)(2,1)} %cot_hbm.1, s32[8,32]{1,0:T(8,128)} %bitcast.22, bf16[8,32]{1,0:T(8,128)(2,1)} %bitcast.23, s32[4]{0:T(128)} %hot_hbm.1, s32[4]{0:T(128)} %extra_hbm.1), custom_call_target="tpu_custom_call" | custom-call | flops 134217728 | bytes 2097152 | tf_op jit(solution)/shard_map/dispatch/pallas_call | solution.py:264
  4.0 18.9 %all-to-all-start = ((bf16[128,8,1024]{2,1,0:T(8,128)(2,1)}), bf16[128,8,1024]{2,1,0:T(8,128)(2,1)}, u32[]{:S(2)}, u32[]{:S(2)}) async-start(bf16[128,8,1024]{2,1,0:T(8,128)(2,1)} %bitcast.14), calls=%async_computation | async-start | bytes 4194304 | tf_op jit(solution)/shard_map/all_to_all | solution.py:284
  22.9 51.8 %all-to-all-done = bf16[128,8,1024]{2,1,0:T(8,128)(2,1)} async-done(((bf16[128,8,1024]{2,1,0:T(8,128)(2,1)}), bf16[128,8,1024]{2,1,0:T(8,128)(2,1)}, u32[]{:S(2)}, u32[]{:S(2)}) %all-to-all-start) | async-done | bytes 2097184 | tf_op jit(solution)/shard_map/all_to_all | solution.py:284
  74.7 8.2 %expert.1 = (bf16[1024,512]{1,0:T(8,128)(2,1)}, bf16[256,1536]{1,0:T(8,128)(2,1)}, bf16[256,1536]{1,0:T(8,128)(2,1)}, bf16[256,768]{1,0:T(8,128)(2,1)}, bf16[256,768]{1,0:T(8,128)(2,1)}) custom-call(s32[1]{0:T(128)} %bitcast.2.me, bf16[1024,1024]{1,0:T(8,128)(2,1)} %bitcast.4.recv_hbm, bf16[1024,384]{1,0:T(8,128)(2,1)} %bitcast.16, ...), custom_call_target="tpu_custom_call" | custom-call | flops 3221225472 | bytes 8912896 | tf_op jit(solution)/shard_map/expert/pallas_call | solution.py:290
  82.9 0.0 copy-start.3
  82.9 0.0 copy-start.2
  82.9 0.0 copy-start
  82.9 7.9 %all-to-all-start.1 = ((bf16[128,8,512]{2,1,0:T(8,128)(2,1)}), bf16[128,8,512]{2,1,0:T(8,128)(2,1)S(1)}, u32[]{:S(2)}, u32[]{:S(2)}) async-start(bf16[128,8,512]{2,1,0:T(8,128)(2,1)} %bitcast.15), calls=%async_computation.1 | async-start | bytes 2097152 | tf_op jit(solution)/shard_map/all_to_all | solution.py:319
  90.9 0.0 copy-done.3
  90.9 3.1 %collective-permute-start = (bf16[256,1536]{1,0:T(8,128)(2,1)S(1)}, bf16[256,1536]{1,0:T(8,128)(2,1)S(1)}, u32[]{:S(2)}, u32[]{:S(2)}) collective-permute-start(bf16[256,1536]{1,0:T(8,128)(2,1)S(1)} %copy-done.3), channel_id=1, source_target_pairs={{0,128},{128,0},{256,384},{384,256},{1,129},{129,1},{257,385},{385... | collective-permute-start | bytes 2359304 | tf_op jit(solution)/shard_map/ppermute | solution.py:322
  94.0 3.7 %collective-permute-start.2 = (bf16[256,1536]{1,0:T(8,128)(2,1)S(1)}, bf16[256,1536]{1,0:T(8,128)(2,1)S(1)}, u32[]{:S(2)}, u32[]{:S(2)}) collective-permute-start(bf16[256,1536]{1,0:T(8,128)(2,1)S(1)} %copy-done.2), channel_id=1, source_target_pairs={{0,384},{128,256},{256,128},{384,0},{1,385},{129,257},{257,129},{3... | collective-permute-start | bytes 2359304 | tf_op jit(solution)/shard_map/ppermute | solution.py:325
  97.7 13.2 %collective-permute-done.received.even_first = bf16[256,1536]{1,0:T(8,128)(2,1)S(1)} collective-permute-done((bf16[256,1536]{1,0:T(8,128)(2,1)S(1)}, bf16[256,1536]{1,0:T(8,128)(2,1)S(1)}, u32[]{:S(2)}, u32[]{:S(2)}) %collective-permute-start) | collective-permute-done | bytes 786464 | tf_op jit(solution)/shard_map/ppermute | solution.py:322
  110.9 0.0 copy-done
  110.9 0.1 middle.2.even_sum
  111.1 4.4 %collective-permute-start.1 = (bf16[256,1152]{1,0:T(8,128)(2,1)S(1)}, bf16[256,1152]{1,0:T(8,128)(2,1)S(1)}, u32[]{:S(2)}, u32[]{:S(2)}) collective-permute-start(bf16[256,1152]{1,0:T(8,128)(2,1)S(1)} %middle.2.even_sum), channel_id=1, source_target_pairs={{0,384},{128,256},{256,128},{384,0},{1,385},{129,257},{257,129},{3... | collective-permute-start | bytes 1769480 | tf_op jit(solution)/shard_map/ppermute | solution.py:325
  115.5 0.0 collective-permute-done.2.received.mirror_first
  115.5 0.1 middle.3.mirror_sum
  115.6 0.0 copy-start.4
  115.6 2.1 %collective-permute-start.3 = (bf16[256,1152]{1,0:T(8,128)(2,1)S(1)}, bf16[256,1152]{1,0:T(8,128)(2,1)S(1)}, u32[]{:S(2)}, u32[]{:S(2)}) collective-permute-start(bf16[256,1152]{1,0:T(8,128)(2,1)S(1)} %middle.3.mirror_sum), channel_id=1, source_target_pairs={{0,128},{128,0},{256,384},{384,256},{1,129},{129,1},{257,385},{385... | collective-permute-start | bytes 1769480 | tf_op jit(solution)/shard_map/ppermute | solution.py:322
  117.7 9.5 %collective-permute-done.1.even_second = bf16[256,1152]{1,0:T(8,128)(2,1)S(1)} collective-permute-done((bf16[256,1152]{1,0:T(8,128)(2,1)S(1)}, bf16[256,1152]{1,0:T(8,128)(2,1)S(1)}, u32[]{:S(2)}, u32[]{:S(2)}) %collective-permute-start.1) | collective-permute-done | bytes 589856 | tf_op jit(solution)/shard_map/ppermute | solution.py:325
  127.2 3.2 %collective-permute-done.3.mirror_second = bf16[256,1152]{1,0:T(8,128)(2,1)S(1)} collective-permute-done((bf16[256,1152]{1,0:T(8,128)(2,1)S(1)}, bf16[256,1152]{1,0:T(8,128)(2,1)S(1)}, u32[]{:S(2)}, u32[]{:S(2)}) %collective-permute-start.3) | collective-permute-done | bytes 589856 | tf_op jit(solution)/shard_map/ppermute | solution.py:322
  130.4 1.2 final.1
  131.7 0.0 all-to-all-done.1
  131.7 0.9 token_grad.1
  (4 shorter events, 0.0 us)
Async XLA Ops:
  4.0 70.7 %all-to-all-start = ((bf16[128,8,1024]{2,1,0:T(8,128)(2,1)}), bf16[128,8,1024]{2,1,0:T(8,128)(2,1)}, u32[]{:S(2)}, u32[]{:S(2)}) async-start(bf16[128,8,1024]{2,1,0:T(8,128)(2,1)} %bitcast.14), calls=%async_computation | async-start | bytes 4194304 | tf_op jit(solution)/shard_map/all_to_all | solution.py:284
  82.9 8.0 %copy-start.3 = (bf16[256,1536]{1,0:T(8,128)(2,1)S(1)}, bf16[256,1536]{1,0:T(8,128)(2,1)}, u32[]{:S(2)}) copy-start(bf16[256,1536]{1,0:T(8,128)(2,1)} %get-tuple-element.18.send) | copy-start | bytes 2359300
  82.9 11.1 %copy-start.2 = (bf16[256,1536]{1,0:T(8,128)(2,1)S(1)}, bf16[256,1536]{1,0:T(8,128)(2,1)}, u32[]{:S(2)}) copy-start(bf16[256,1536]{1,0:T(8,128)(2,1)} %get-tuple-element.20.send) | copy-start | bytes 2359300
  82.9 28.0 %copy-start = (bf16[256,768]{1,0:T(8,128)(2,1)S(1)}, bf16[256,768]{1,0:T(8,128)(2,1)}, u32[]{:S(2)}) copy-start(bf16[256,768]{1,0:T(8,128)(2,1)} %get-tuple-element.17.keep.even_keep) | copy-start | bytes 1179652
  82.9 32.6 %copy-start.1 = (bf16[256,768]{1,0:T(8,128)(2,1)S(1)}, bf16[256,768]{1,0:T(8,128)(2,1)}, u32[]{:S(2)}) copy-start(bf16[256,768]{1,0:T(8,128)(2,1)} %get-tuple-element.19.keep.mirror_keep) | copy-start | bytes 1179652
  82.9 48.7 %all-to-all-start.1 = ((bf16[128,8,512]{2,1,0:T(8,128)(2,1)}), bf16[128,8,512]{2,1,0:T(8,128)(2,1)S(1)}, u32[]{:S(2)}, u32[]{:S(2)}) async-start(bf16[128,8,512]{2,1,0:T(8,128)(2,1)} %bitcast.15), calls=%async_computation.1 | async-start | bytes 2097152 | tf_op jit(solution)/shard_map/all_to_all | solution.py:319
  90.9 20.1 %collective-permute-start = (bf16[256,1536]{1,0:T(8,128)(2,1)S(1)}, bf16[256,1536]{1,0:T(8,128)(2,1)S(1)}, u32[]{:S(2)}, u32[]{:S(2)}) collective-permute-start(bf16[256,1536]{1,0:T(8,128)(2,1)S(1)} %copy-done.3), channel_id=1, source_target_pairs={{0,128},{128,0},{256,384},{384,256},{1,129},{129,1},{257,385},{385... | collective-permute-start | bytes 2359304 | tf_op jit(solution)/shard_map/ppermute | solution.py:322
  94.0 21.5 %collective-permute-start.2 = (bf16[256,1536]{1,0:T(8,128)(2,1)S(1)}, bf16[256,1536]{1,0:T(8,128)(2,1)S(1)}, u32[]{:S(2)}, u32[]{:S(2)}) collective-permute-start(bf16[256,1536]{1,0:T(8,128)(2,1)S(1)} %copy-done.2), channel_id=1, source_target_pairs={{0,384},{128,256},{256,128},{384,0},{1,385},{129,257},{257,129},{3... | collective-permute-start | bytes 2359304 | tf_op jit(solution)/shard_map/ppermute | solution.py:325
  111.1 16.1 %collective-permute-start.1 = (bf16[256,1152]{1,0:T(8,128)(2,1)S(1)}, bf16[256,1152]{1,0:T(8,128)(2,1)S(1)}, u32[]{:S(2)}, u32[]{:S(2)}) collective-permute-start(bf16[256,1152]{1,0:T(8,128)(2,1)S(1)} %middle.2.even_sum), channel_id=1, source_target_pairs={{0,384},{128,256},{256,128},{384,0},{1,385},{129,257},{257,129},{3... | collective-permute-start | bytes 1769480 | tf_op jit(solution)/shard_map/ppermute | solution.py:325
  115.6 16.0 %copy-start.4 = (bf16[64,1024]{1,0:T(8,128)(2,1)S(1)}, bf16[64,1024]{1,0:T(8,128)(2,1)}, u32[]{:S(2)}) copy-start(bf16[64,1024]{1,0:T(8,128)(2,1)} %get-tuple-element.14.pick_t) | copy-start | bytes 393220
  115.6 14.8 %collective-permute-start.3 = (bf16[256,1152]{1,0:T(8,128)(2,1)S(1)}, bf16[256,1152]{1,0:T(8,128)(2,1)S(1)}, u32[]{:S(2)}, u32[]{:S(2)}) collective-permute-start(bf16[256,1152]{1,0:T(8,128)(2,1)S(1)} %middle.3.mirror_sum), channel_id=1, source_target_pairs={{0,128},{128,0},{256,384},{384,256},{1,129},{129,1},{257,385},{385... | collective-permute-start | bytes 1769480 | tf_op jit(solution)/shard_map/ppermute | solution.py:322

commit v5 on v4

v5 whole, which is shorter than its diff:
```python
import functools

import jax
import jax.numpy as jnp
from jax import lax
from jax.experimental import pallas as pl
from jax.experimental.pallas import tpu as pltpu
from jax.sharding import PartitionSpec as P

BASE = 2
SLOTS = 4
MSG = 2 * SLOTS
LANES = 128
CHUNKS = 4
F32 = jnp.float32
BF16 = jnp.bfloat16
VMEM = pl.BlockSpec(memory_space=pltpu.VMEM)
ANY = pl.BlockSpec(memory_space=pl.ANY)
SMEM = pl.BlockSpec(memory_space=pltpu.SMEM)
MIB = 1024 * 1024


NN = (((1,), (0,)), ((), ()))
NT = (((1,), (1,)), ((), ()))
TN = (((0,), (0,)), ((), ()))


def dot(a, b, dims):
    return lax.dot_general(a, b, dims, preferred_element_type=F32)


def call(
    body, name, out_shape, in_specs, scratch=(), flops=0, bytes_accessed=0, vmem=16 * MIB, out=VMEM
):
    return pl.pallas_call(
        body,
        name=name,
        out_shape=out_shape,
        in_specs=in_specs,
        out_specs=jax.tree.map(lambda _: out, out_shape),
        scratch_shapes=list(scratch),
        compiler_params=pltpu.CompilerParams(vmem_limit_bytes=vmem),
        cost_estimate=pl.CostEstimate(
            flops=flops, bytes_accessed=bytes_accessed, transcendentals=0
        ),
    )


def identity(n):
    rows = lax.broadcasted_iota(jnp.int32, (n, n), 0)
    return jnp.where(rows == lax.broadcasted_iota(jnp.int32, (n, n), 1), 1.0, 0.0).astype(BF16)


def dispatch_body(
    experts, tok_hbm, cot_hbm, routes_hbm, combine_hbm, hot_hbm, extra_hbm,
    send, pick_t, both, routes_in, combine_in, hot, extra, sems,
):
    count = tok_hbm.shape[0]
    copies = [
        pltpu.make_async_copy(source, target, sems.at[i])
        for i, (source, target) in enumerate(
            [
                (routes_hbm, routes_in),
                (combine_hbm, combine_in),
                (hot_hbm, hot),
                (extra_hbm, extra),
                (tok_hbm, both.at[pl.ds(0, count)]),
                (cot_hbm, both.at[pl.ds(count, count)]),
            ]
        )
    ]
    for copy in copies:
        copy.start()
    for copy in copies[:4]:
        copy.wait()
    lanes = 2 * count
    src = lax.broadcasted_iota(jnp.int32, (count, lanes), 0)
    dst = lax.broadcasted_iota(jnp.int32, (count, lanes), 1)
    dst = jnp.where(dst >= count, dst - count, dst)
    twice = jnp.where(src == dst, 1.0, 0.0).astype(BF16)
    routes = dot(routes_in[...].astype(F32).astype(BF16), twice, NN)
    combine = dot(combine_in[...], twice, NN)
    expert_id = lax.broadcasted_iota(jnp.int32, (experts, lanes), 0)
    lane = lax.broadcasted_iota(jnp.int32, (experts, lanes), 1)
    named = jnp.zeros((experts, lanes), F32)
    weight = jnp.zeros((experts, lanes), F32)
    expert_number = expert_id.astype(F32)
    for k in range(routes.shape[0]):
        match = expert_number == routes[k : k + 1, :]
        named = named + jnp.where(match, 1.0, 0.0)
        weight = weight + jnp.where(match, combine[k : k + 1, :], 0.0)
    before = jnp.where(src < dst, 1.0, 0.0).astype(BF16)
    rank = dot(named[:, :count].astype(BF16), before, NN)
    limit = jnp.full((experts, lanes), float(BASE), F32)
    for j in range(hot.shape[0]):
        limit = limit + jnp.where(expert_id == hot[j], extra[j].astype(F32), 0.0)
    place = jnp.where(lane >= count, rank + float(SLOTS), rank)
    place = jnp.where(named > 0.5, place, -1.0)
    place = jnp.where(rank < limit, place, -1.0)
    weight = jnp.where(lane >= count, weight, 1.0)
    slot = lax.broadcasted_iota(jnp.int32, (experts, MSG, lanes), 1).astype(F32)
    hit = jnp.broadcast_to(place[:, None, :], (experts, MSG, lanes)) == slot
    scaled = jnp.where(hit, jnp.broadcast_to(weight[:, None, :], hit.shape), 0.0)
    scaled = scaled.reshape(experts * MSG, lanes).astype(BF16)
    for copy in copies[4:]:
        copy.wait()
    send[...] = jnp.dot(scaled, both[...], preferred_element_type=F32).astype(BF16)
    pick = jnp.where(hit, 1.0, 0.0).reshape(experts * MSG, lanes).astype(BF16)
    pick_t[...] = dot(identity(lanes), pick, NT).astype(BF16)


def token_body(pick_t, returned, out):
    count, half = out.shape[0], returned.shape[1]
    both = dot(pick_t[...], returned[...], NN)
    out[:, :half] = both[:count].astype(BF16)
    out[:, half:] = both[count:].astype(BF16)


def start_all(copies):
    for copy in copies:
        copy.start()
    return copies


def wait_all(copies):
    for copy in copies:
        copy.wait()


def rows_body(
    recv_hbm, w_gate_hbm, w_up_hbm, w_down_hbm, back_hbm, tok_hbm, og_hbm, in_rows_hbm, hid_hbm,
    recv, w_in, w_down, back, tok, og, in_rows, hid, wide, narrow, pre, grad, in_sems, out_sems,
):
    rows_in, features = recv.shape
    hidden = w_down.shape[0]
    peers = rows_in // MSG
    half = features // 2
    step = rows_in // CHUNKS
    chunks = [pl.ds(n * step, step) for n in range(CHUNKS)]
    arrivals = start_all(
        [
            pltpu.make_async_copy(recv_hbm.at[at], recv.at[at], in_sems.at[n])
            for n, at in enumerate(chunks)
        ]
    )
    weights = start_all(
        [
            pltpu.make_async_copy(source, target, in_sems.at[CHUNKS + n])
            for n, (source, target) in enumerate(
                [
                    (w_gate_hbm, w_in.at[:, pl.ds(0, hidden)]),
                    (w_up_hbm, w_in.at[:, pl.ds(hidden, hidden)]),
                    (w_down_hbm, w_down),
                ]
            )
        ]
    )
    departures = []

    def send_out(source, target):
        copy = pltpu.make_async_copy(source, target, out_sems.at[len(departures)])
        departures.extend(start_all([copy]))

    for copy, at in zip(arrivals, chunks):
        copy.wait()
        for c in range(features // LANES):
            wide[c, at, :] = recv[at, c * LANES : (c + 1) * LANES].astype(F32)
    for s in range(SLOTS):
        at = pl.ds(s * peers, peers)
        for c in range(features // LANES):
            cols = slice(c * LANES, (c + 1) * LANES)
            tok[at, cols] = wide[c, pl.ds(s, peers, MSG), :].astype(BF16)
            og[at, cols] = wide[c, pl.ds(s + SLOTS, peers, MSG), :].astype(BF16)
    wait_all(weights)
    send_out(tok, tok_hbm)
    send_out(og, og_hbm)
    pre[...] = dot(tok[...], w_in[...], NN)
    grad[...] = dot(og[...], w_down[...], NT)
    for at in range(0, SLOTS * peers, peers):
        rows = slice(at, at + peers)
        gate_pre, up_proj, hidden_grad = pre[rows, :hidden], pre[rows, hidden:], grad[rows, :]
        s = jax.nn.sigmoid(gate_pre)
        act = gate_pre * s
        hid[rows, :] = (act * up_proj).astype(BF16)
        gate_grad = hidden_grad * up_proj * s * (1.0 + gate_pre * (1.0 - s))
        in_rows[rows, :hidden] = gate_grad.astype(BF16)
        in_rows[rows, hidden:] = (hidden_grad * act).astype(BF16)
    send_out(hid, hid_hbm)
    send_out(in_rows, in_rows_hbm)
    grads = dot(in_rows[...], w_in[...], NT)
    for s in range(SLOTS):
        piece = grads[s * peers : (s + 1) * peers, :]
        for c in range(half // LANES):
            low = piece[:, c * LANES : (c + 1) * LANES]
            high = piece[:, half + c * LANES : half + (c + 1) * LANES]
            narrow[c, pl.ds(s, peers, MSG), :] = low
            narrow[c, pl.ds(s + SLOTS, peers, MSG), :] = high
    for c in range(half // LANES):
        back[:, c * LANES : (c + 1) * LANES] = narrow[c].astype(BF16)
    send_out(back, back_hbm)
    wait_all(departures)


def weights_body(
    ranks, me, tok_hbm, og_hbm, in_rows_hbm, hid_hbm,
    down_a_hbm, down_b_hbm, even_send_hbm, mirror_send_hbm, even_keep_hbm, mirror_keep_hbm,
    tok, og, in_rows, hid,
    down_a, down_b, even_send, mirror_send, even_keep, mirror_keep,
    total, in_sems, out_sems,
):
    features, hidden = tok.shape[1], hid.shape[1]
    arrivals = start_all(
        [
            pltpu.make_async_copy(source, target, in_sems.at[n])
            for n, (source, target) in enumerate(
                [(hid_hbm, hid), (og_hbm, og), (tok_hbm, tok), (in_rows_hbm, in_rows)]
            )
        ]
    )
    departures = []

    def send_out(source, target):
        copy = pltpu.make_async_copy(source, target, out_sems.at[len(departures)])
        departures.extend(start_all([copy]))

    wait_all(arrivals[:2])
    down = dot(hid[...], og[...], TN).astype(BF16)
    cut = hidden // 2
    down_a[...] = down[:cut]
    send_out(down_a, down_a_hbm)
    down_b[...] = down[cut:]
    send_out(down_b, down_b_hbm)
    wait_all(arrivals[2:])
    total[...] = dot(tok[...], in_rows[...], TN)
    piece = features // ranks
    even = me[0] + 1 - 2 * lax.rem(me[0], 2)
    mirror = ranks - 1 - me[0]
    opposite = ranks - 1 - even
    for cols, keep, send, keep_hbm, send_hbm, here, other in (
        (slice(hidden, 2 * hidden), even_keep, even_send, even_keep_hbm, even_send_hbm, even, mirror),
        (slice(0, hidden), mirror_keep, mirror_send, mirror_keep_hbm, mirror_send_hbm, mirror, even),
    ):

        def part_of(index):
            return total[pl.ds(pl.multiple_of(index * piece, 16), piece), cols].astype(BF16)

        send[:, :hidden] = part_of(opposite)
        send[:, hidden:] = part_of(here)
        send_out(send, send_hbm)
        keep[:, :hidden] = part_of(other)
        keep[:, hidden:] = part_of(me[0])
        send_out(keep, keep_hbm)
    wait_all(departures)


def add(kept, received):
    return kept.astype(F32) + received.astype(F32)


def sum_body(kept, received, out):
    width = out.shape[1]
    out[...] = add(kept[:, :width], received[:, :width]).astype(BF16)


def down_body(sum_a, next_a, sum_b, next_b, out):
    cut = sum_a.shape[0]
    out[:cut, :] = add(sum_a[...], next_a[...]).astype(BF16)
    out[cut:, :] = add(sum_b[...], next_b[...]).astype(BF16)


def pair_body(gate_keep, gate_first, gate_next, up_keep, up_first, up_next, grad_gate, grad_up):
    hidden = grad_gate.shape[1]
    gate = add(gate_keep[:, hidden:], gate_first[:, hidden:]) + gate_next[...].astype(F32)
    up = add(up_keep[:, hidden:], up_first[:, hidden:]) + up_next[...].astype(F32)
    grad_gate[...] = gate.astype(BF16)
    grad_up[...] = up.astype(BF16)


def shards(tokens, cotangent, routes, combine, hot_experts, extra_slots, w_gate, w_up, w_down):
    experts = lax.axis_size("expert")
    ranks = lax.axis_size("dp")
    count, features = tokens.shape
    hidden = w_gate.shape[2]
    total = experts * MSG
    rows = experts * SLOTS
    send, pick_t = call(
        functools.partial(dispatch_body, experts),
        "dispatch",
        [
            jax.ShapeDtypeStruct((total, features), BF16),
            jax.ShapeDtypeStruct((2 * count, total), BF16),
        ],
        [ANY] * 6,
        [
            pltpu.VMEM((2 * count, features), BF16),
            pltpu.VMEM(routes.shape[::-1], jnp.int32),
            pltpu.VMEM(combine.shape[::-1], BF16),
            pltpu.SMEM(hot_experts.shape, jnp.int32),
            pltpu.SMEM(extra_slots.shape, jnp.int32),
            pltpu.SemaphoreType.DMA((6,)),
        ],
        2 * total * 2 * count * features,
        2 * total * features,
        64 * MIB - 65536,
    )(tokens, cotangent, routes.T, combine.T, hot_experts, extra_slots)
    recv = lax.all_to_all(send, "expert", split_axis=0, concat_axis=0, tiled=True)
    me = lax.axis_index("dp").astype(jnp.int32).reshape(1)
    piece = features // ranks
    cut = hidden // 2
    shape = jax.ShapeDtypeStruct
    saved = [
        shape((rows, features), BF16),
        shape((rows, features), BF16),
        shape((rows, 2 * hidden), BF16),
        shape((rows, hidden), BF16),
    ]
    out = [shape((total, features // 2), BF16)] + saved
    back, *kept_rows = call(
        rows_body,
        "rows",
        out,
        [ANY] * 4,
        [
            pltpu.VMEM((total, features), BF16),
            pltpu.VMEM((features, 2 * hidden), BF16),
            pltpu.VMEM((hidden, features), BF16),
        ]
        + [pltpu.VMEM(a.shape, a.dtype) for a in out]
        + [
            pltpu.VMEM((features // LANES, total, LANES), F32),
            pltpu.VMEM((features // 2 // LANES, total, LANES), F32),
            pltpu.VMEM((rows, 2 * hidden), F32),
            pltpu.VMEM((rows, hidden), F32),
            pltpu.SemaphoreType.DMA((CHUNKS + 3,)),
            pltpu.SemaphoreType.DMA((len(out),)),
        ],
        10 * rows * features * hidden,
        2 * (total * features * 2 + 3 * features * hidden),
        64 * MIB - 65536,
        ANY,
    )(recv, w_gate[0], w_up[0], w_down[0])
    returned = lax.all_to_all(back, "expert", split_axis=0, concat_axis=0, tiled=True)
    out = [shape((cut, features), BF16)] * 2 + [shape((piece, 2 * hidden), BF16)] * 4
    down_a, down_b, even_send, mirror_send, even_keep, mirror_keep = call(
        functools.partial(weights_body, ranks),
        "weight_grads",
        out,
        [SMEM] + [ANY] * 4,
        [pltpu.VMEM(a.shape, a.dtype) for a in saved]
        + [pltpu.VMEM(a.shape, a.dtype) for a in out]
        + [
            pltpu.VMEM((features, 2 * hidden), F32),
            pltpu.SemaphoreType.DMA((len(saved),)),
            pltpu.SemaphoreType.DMA((len(out),)),
        ],
        6 * rows * features * hidden,
        2 * (rows * (2 * features + 3 * hidden) + 3 * features * hidden),
        64 * MIB - 65536,
        ANY,
    )(me, *kept_rows)

    def even(value):
        return lax.ppermute(value, "dp", [(i, i ^ 1) for i in range(ranks)])

    def mirror(value):
        return lax.ppermute(value, "dp", [(i, ranks - 1 - i) for i in range(ranks)])

    def small(body, name, out, *operands):
        return call(body, name, out, [VMEM] * len(operands))(*operands)

    first_a, first_b = even(down_a), mirror(down_b)
    up_first, gate_first = even(even_send), mirror(mirror_send)
    half_down = shape((cut, features), BF16)
    one_piece = shape((piece, hidden), BF16)
    sum_a = small(sum_body, "down_a", half_down, down_a, first_a)
    next_a = mirror(sum_a)
    sum_b = small(sum_body, "down_b", half_down, down_b, first_b)
    next_b = even(sum_b)
    up_next = mirror(small(sum_body, "up", one_piece, even_keep, up_first))
    gate_next = even(small(sum_body, "gate", one_piece, mirror_keep, gate_first))
    grad_down = small(
        down_body, "down", shape((hidden, features), BF16), sum_a, next_a, sum_b, next_b
    )
    grad_gate, grad_up = small(
        pair_body,
        "pair",
        [one_piece, one_piece],
        mirror_keep, gate_first, gate_next, even_keep, up_first, up_next,
    )
    token_grads = call(
        token_body,
        "token_grad",
        jax.ShapeDtypeStruct((count, features), BF16),
        [VMEM, VMEM],
        (),
        2 * total * count * features,
        2 * total * features,
    )(pick_t, returned)
    return token_grads, grad_gate[None], grad_up[None], grad_down[None]


def solution(mesh):
    in_specs = (
        P(("dp", "expert"), None),
        P(("dp", "expert"), None),
        P(("dp", "expert"), None),
        P(("dp", "expert"), None),
        P(),
        P(),
        P("expert", None, None),
        P("expert", None, None),
        P("expert", None, None),
    )
    out_specs = (
        P(("dp", "expert"), None),
        P("expert", "dp", None),
        P("expert", "dp", None),
        P("expert", None, None),
    )
    return jax.shard_map(shards, mesh=mesh, in_specs=in_specs, out_specs=out_specs, check_vma=False)
```

time: 135 us -> 136 us (level)
  blocking collectives: 0 us -> 70.7 us
  waiting for transfers between devices: 77.7 us -> 10.2 us
  starting transfers between devices: 40.1 us -> 32 us
  Pallas kernels: 14 us -> 18.6 us
  local copies, waits for them, and re-layouts: 0.02 us -> 2 us
    all_to_all x0 -> x1, blocking collectives: none -> 70.7 us  [shards(): lax.all_to_all(send, 'expert', split_axis=0, concat_axis=0, tiled=True)]
    all_to_all x1 -> x0, waiting for transfers between devices: 51.8 us -> none  [shards(): lax.all_to_all(send, 'expert', split_axis=0, concat_axis=0, tiled=True)]
    all_to_all x1 -> x0, starting transfers between devices: 18.9 us -> none  [shards(): lax.all_to_all(send, 'expert', split_axis=0, concat_axis=0, tiled=True)]
    ppermute x2 -> x4, waiting for transfers between devices: 16.4 us -> 3.29 us  [even(): return lax.ppermute(value, 'dp', [(i, i ^ 1) for i in range(ranks)])]
    ppermute x2 -> x4, starting transfers between devices: 8.12 us -> 14.8 us  [mirror(): return lax.ppermute(value, 'dp', [(i, ranks - 1 - i) for i in range(ranks)])]
    ppermute x2 -> x4, starting transfers between devices: 5.16 us -> 9 us  [even(): return lax.ppermute(value, 'dp', [(i, i ^ 1) for i in range(ranks)])]
    pallas_call x4 -> x8, Pallas kernels: 9.72 us -> 13.2 us  [the longest x1 6.67 us: shards(): call(rows_body, 'rows', out, [ANY] * 4, [pltpu.VMEM((total, features), BF...]
    ppermute x2 -> x4, waiting for transfers between devices: 9.49 us -> 6.9 us  [mirror(): return lax.ppermute(value, 'dp', [(i, ranks - 1 - i) for i in range(ranks)])]
  transfers between devices with their start and end apart: 6 -> 9, of which waited for: 4 -> 4; matrix products, arithmetic and copies ran while one was open for 0% -> 0% of each run, Pallas kernels for 1% -> 5%
where the time goes in v5:
time: 136 us; the launch traced here: 134 us
  blocking collectives  70.7 us (52%)
  starting transfers between devices  32 us (24%)
  Pallas kernels  18.6 us (14%)
  waiting for transfers between devices  10.2 us (7%)
  local copies, waits for them, and re-layouts  2 us (1%)
    all_to_all x1, blocking collectives, shards(): lax.all_to_all(send, 'expert', split_axis=0, concat_axis=0, tiled=True)  70.7 us
    ppermute x4, starting transfers between devices, mirror(): return lax.ppermute(value, 'dp', [(i, ranks - 1 - i) for i in range(ranks)])  14.8 us
    ppermute x4, starting transfers between devices, even(): return lax.ppermute(value, 'dp', [(i, i ^ 1) for i in range(ranks)])  9 us
    all_to_all x1, starting transfers between devices, shards(): lax.all_to_all(back, 'expert', split_axis=0, concat_axis=0, tiled=True)  8.26 us
    ppermute x4, waiting for transfers between devices, mirror(): return lax.ppermute(value, 'dp', [(i, ranks - 1 - i) for i in range(ranks)])  6.9 us
    pallas_call x1, Pallas kernels, shards(): call(rows_body, 'rows', out, [ANY] * 4, [pltpu.VMEM((total, features), BF...  6.67 us
    pallas_call x1, Pallas kernels, shards(): call(functools.partial(weights_body, ranks), 'weight_grads', out, [SMEM]...  4.33 us
    pallas_call x1, Pallas kernels, shards(): call(functools.partial(dispatch_body, experts), 'dispatch', [jax.ShapeDty...  3.31 us
  transfers between devices with their start and end apart: 9, of which 4 were waited for; matrix products, arithmetic and copies ran while one was open for 0% of the time, Pallas kernels for 5%

profile of v5, /device:TPU:1, one launch (start us, length us, event | category | flops | bytes accessed | tf_op | source)
XLA Modules:
  0.0 134.4 jit_solution(11533905983230719785)
XLA Ops:
  0.6 3.3 %dispatch.1 = (bf16[1024,1024]{1,0:T(8,128)(2,1)}, bf16[64,1024]{1,0:T(8,128)(2,1)}) custom-call(bf16[32,1024]{1,0:T(8,128)(2,1)} %tok_hbm.1, bf16[32,1024]{1,0:T(8,128)(2,1)} %cot_hbm.1, s32[8,32]{1,0:T(8,128)} %bitcast.22, bf16[8,32]{1,0:T(8,128)(2,1)} %bitcast.23, s32[4]{0:T(128)} %hot_hbm.1, s32[4]{0:T(128)} %extra_hbm.1), custom_call_target="tpu_custom_call" | custom-call | flops 134217728 | bytes 2097152 | tf_op jit(solution)/shard_map/dispatch/pallas_call | solution.py:286
  4.0 70.7 %all_to_all.22 = bf16[128,8,1024]{2,1,0:T(8,128)(2,1)} all-to-all(bf16[128,8,1024]{2,1,0:T(8,128)(2,1)} %bitcast.14), channel_id=1, replica_groups=mesh['dp'=4,'expert'=128] {'expert'}, dimensions={0} | all-to-all | bytes 4194304 | tf_op jit(solution)/shard_map/all_to_all | solution.py:306
  74.6 6.7 %rows.1 = (bf16[1024,512]{1,0:T(8,128)(2,1)}, bf16[512,1024]{1,0:T(8,128)(2,1)}, bf16[512,1024]{1,0:T(8,128)(2,1)}, bf16[512,768]{1,0:T(8,128)(2,1)}, bf16[512,384]{1,0:T(8,128)(2,1)}) custom-call(bf16[1024,1024]{1,0:T(8,128)(2,1)} %bitcast.13, bf16[1024,384]{1,0:T(8,128)(2,1)} %bitcast.17, bf16[1024,384]{1,0:T(8,128)(2,1)} %bitcast.18, ...), custom_call_target="tpu_custom_call" | custom-call | flops 2013265920 | bytes 6553600 | tf_op jit(solution)/shard_map/rows/pallas_call | solution.py:318
  81.3 8.3 %all-to-all-start.1 = ((bf16[128,8,512]{2,1,0:T(8,128)(2,1)}), bf16[128,8,512]{2,1,0:T(8,128)(2,1)}, u32[]{:S(2)}, u32[]{:S(2)}) async-start(bf16[128,8,512]{2,1,0:T(8,128)(2,1)} %bitcast.15), calls=%async_computation.1 | async-start | bytes 2097152 | tf_op jit(solution)/shard_map/all_to_all | solution.py:342
  89.6 4.3 %weight_grads.1 = (bf16[192,1024]{1,0:T(8,128)(2,1)}, bf16[192,1024]{1,0:T(8,128)(2,1)}, bf16[256,768]{1,0:T(8,128)(2,1)}, bf16[256,768]{1,0:T(8,128)(2,1)}, bf1...) custom-call(s32[1]{0:T(128)} %bitcast.9.me, bf16[512,1024]{1,0:T(8,128)(2,1)} %get-tuple-element.22.tok_hbm, ...), custom_call_target="tpu_custom_call" | custom-call | flops 1207959552 | bytes 5636096 | tf_op jit(solution)/shard_map/weight_grads/pallas_call | solution.py:344
  93.9 3.2 %collective-permute-start.4 = (bf16[192,1024]{1,0:T(8,128)(2,1)}, bf16[192,1024]{1,0:T(8,128)(2,1)S(1)}, u32[]{:S(2)}, u32[]{:S(2)}) collective-permute-start(bf16[192,1024]{1,0:T(8,128)(2,1)} %get-tuple-element.32.kept), channel_id=1, source_target_pairs={{0,128},{128,0},{256,384},{384,256},{1,129},{129,1},{257,385},{385... | collective-permute-start | bytes 1179656 | tf_op jit(solution)/shard_map/ppermute | solution.py:363
  97.2 3.7 %collective-permute-start.6 = (bf16[192,1024]{1,0:T(8,128)(2,1)}, bf16[192,1024]{1,0:T(8,128)(2,1)S(1)}, u32[]{:S(2)}, u32[]{:S(2)}) collective-permute-start(bf16[192,1024]{1,0:T(8,128)(2,1)} %get-tuple-element.33.kept), channel_id=1, source_target_pairs={{0,384},{128,256},{256,128},{384,0},{1,385},{129,257},{257,129},{3... | collective-permute-start | bytes 1179656 | tf_op jit(solution)/shard_map/ppermute | solution.py:366
  100.9 2.8 %collective-permute-start = (bf16[256,768]{1,0:T(8,128)(2,1)}, bf16[256,768]{1,0:T(8,128)(2,1)S(1)}, u32[]{:S(2)}, u32[]{:S(2)}) collective-permute-start(bf16[256,768]{1,0:T(8,128)(2,1)} %get-tuple-element.27), channel_id=1, source_target_pairs={{0,384},{128,256},{256,128},{384,0},{1,385},{129,257},{257,129},{3... | collective-permute-start | bytes 1179656 | tf_op jit(solution)/shard_map/ppermute | solution.py:366
  103.7 1.9 %collective-permute-start.2 = (bf16[256,768]{1,0:T(8,128)(2,1)}, bf16[256,768]{1,0:T(8,128)(2,1)S(1)}, u32[]{:S(2)}, u32[]{:S(2)}) collective-permute-start(bf16[256,768]{1,0:T(8,128)(2,1)} %get-tuple-element.29), channel_id=1, source_target_pairs={{0,128},{128,0},{256,384},{384,256},{1,129},{129,1},{257,385},{385... | collective-permute-start | bytes 1179656 | tf_op jit(solution)/shard_map/ppermute | solution.py:363
  105.6 0.3 collective-permute-done.4.received
  105.9 1.0 copy-done.3
  106.9 0.1 down_a.1.sum_a
  107.0 4.4 %collective-permute-start.5 = (bf16[192,1024]{1,0:T(8,128)(2,1)S(1)}, bf16[192,1024]{1,0:T(8,128)(2,1)S(1)}, u32[]{:S(2)}, u32[]{:S(2)}) collective-permute-start(bf16[192,1024]{1,0:T(8,128)(2,1)S(1)} %down_a.1.sum_a), channel_id=1, source_target_pairs={{0,384},{128,256},{256,128},{384,0},{1,385},{129,257},{257,129},{3... | collective-permute-start | bytes 1179656 | tf_op jit(solution)/shard_map/ppermute | solution.py:366
  111.5 1.0 copy-done.2
  112.4 0.1 down_b.1.sum_b
  112.5 1.9 %collective-permute-start.7 = (bf16[192,1024]{1,0:T(8,128)(2,1)S(1)}, bf16[192,1024]{1,0:T(8,128)(2,1)S(1)}, u32[]{:S(2)}, u32[]{:S(2)}) collective-permute-start(bf16[192,1024]{1,0:T(8,128)(2,1)S(1)} %down_b.1.sum_b), channel_id=1, source_target_pairs={{0,128},{128,0},{256,384},{384,256},{1,129},{129,1},{257,385},{385... | collective-permute-start | bytes 1179656 | tf_op jit(solution)/shard_map/ppermute | solution.py:363
  114.5 3.9 %collective-permute-done.received.gate_first = bf16[256,768]{1,0:T(8,128)(2,1)S(1)} collective-permute-done((bf16[256,768]{1,0:T(8,128)(2,1)}, bf16[256,768]{1,0:T(8,128)(2,1)S(1)}, u32[]{:S(2)}, u32[]{:S(2)}) %collective-permute-start) | collective-permute-done | bytes 393248 | tf_op jit(solution)/shard_map/ppermute | solution.py:366
  118.4 1.9 %collective-permute-start.1 = (bf16[256,384]{1,0:T(8,128)(2,1)S(1)}, bf16[256,384]{1,0:T(8,128)(2,1)S(1)}, u32[]{:S(2)}, u32[]{:S(2)}) collective-permute-start(bf16[256,384]{1,0:T(8,128)(2,1)S(1)} %gate.1), channel_id=1, source_target_pairs={{0,128},{128,0},{256,384},{384,256},{1,129},{129,1},{257,385},{385... | collective-permute-start | bytes 589832 | tf_op jit(solution)/shard_map/ppermute | solution.py:363
  120.5 3.9 %collective-permute-start.3 = (bf16[256,384]{1,0:T(8,128)(2,1)S(1)}, bf16[256,384]{1,0:T(8,128)(2,1)S(1)}, u32[]{:S(2)}, u32[]{:S(2)}) collective-permute-start(bf16[256,384]{1,0:T(8,128)(2,1)S(1)} %up.1), channel_id=1, source_target_pairs={{0,384},{128,256},{256,128},{384,0},{1,385},{129,257},{257,129},{3... | collective-permute-start | bytes 589832 | tf_op jit(solution)/shard_map/ppermute | solution.py:366
  124.3 3.0 %collective-permute-done.1.gate_next = bf16[256,384]{1,0:T(8,128)(2,1)S(1)} collective-permute-done((bf16[256,384]{1,0:T(8,128)(2,1)S(1)}, bf16[256,384]{1,0:T(8,128)(2,1)S(1)}, u32[]{:S(2)}, u32[]{:S(2)}) %collective-permute-start.1) | collective-permute-done | bytes 196640 | tf_op jit(solution)/shard_map/ppermute | solution.py:363
  127.3 3.0 %collective-permute-done.3.up_next = bf16[256,384]{1,0:T(8,128)(2,1)S(1)} collective-permute-done((bf16[256,384]{1,0:T(8,128)(2,1)S(1)}, bf16[256,384]{1,0:T(8,128)(2,1)S(1)}, u32[]{:S(2)}, u32[]{:S(2)}) %collective-permute-start.3) | collective-permute-done | bytes 196640 | tf_op jit(solution)/shard_map/ppermute | solution.py:366
  130.3 0.8 pair.1
  131.1 1.1 down.1
  132.2 2.2 %token_grad.1 = bf16[32,1024]{1,0:T(8,128)(2,1)} custom-call(bf16[64,1024]{1,0:T(8,128)(2,1)S(1)} %copy-done.4, bf16[1024,512]{1,0:T(8,128)(2,1)} %bitcast.8.returned), custom_call_target="tpu_custom_call" | custom-call | flops 67108864 | bytes 2097152 | tf_op jit(solution)/shard_map/token_grad/pallas_call | solution.py:390
  (15 shorter events, 0.1 us)
Async XLA Ops:
  81.3 50.9 %all-to-all-start.1 = ((bf16[128,8,512]{2,1,0:T(8,128)(2,1)}), bf16[128,8,512]{2,1,0:T(8,128)(2,1)}, u32[]{:S(2)}, u32[]{:S(2)}) async-start(bf16[128,8,512]{2,1,0:T(8,128)(2,1)} %bitcast.15), calls=%async_computation.1 | async-start | bytes 2097152 | tf_op jit(solution)/shard_map/all_to_all | solution.py:342
  93.9 24.5 %copy-start.1 = (bf16[256,768]{1,0:T(8,128)(2,1)S(1)}, bf16[256,768]{1,0:T(8,128)(2,1)}, u32[]{:S(2)}) copy-start(bf16[256,768]{1,0:T(8,128)(2,1)} %get-tuple-element.26.kept.gate_keep) | copy-start | bytes 1179652
  93.9 26.5 %copy-start = (bf16[256,768]{1,0:T(8,128)(2,1)S(1)}, bf16[256,768]{1,0:T(8,128)(2,1)}, u32[]{:S(2)}) copy-start(bf16[256,768]{1,0:T(8,128)(2,1)} %get-tuple-element.28.kept.up_keep) | copy-start | bytes 1179652
  93.9 12.0 %collective-permute-start.4 = (bf16[192,1024]{1,0:T(8,128)(2,1)}, bf16[192,1024]{1,0:T(8,128)(2,1)S(1)}, u32[]{:S(2)}, u32[]{:S(2)}) collective-permute-start(bf16[192,1024]{1,0:T(8,128)(2,1)} %get-tuple-element.32.kept), channel_id=1, source_target_pairs={{0,128},{128,0},{256,384},{384,256},{1,129},{129,1},{257,385},{385... | collective-permute-start | bytes 1179656 | tf_op jit(solution)/shard_map/ppermute | solution.py:363
  97.2 14.3 %collective-permute-start.6 = (bf16[192,1024]{1,0:T(8,128)(2,1)}, bf16[192,1024]{1,0:T(8,128)(2,1)S(1)}, u32[]{:S(2)}, u32[]{:S(2)}) collective-permute-start(bf16[192,1024]{1,0:T(8,128)(2,1)} %get-tuple-element.33.kept), channel_id=1, source_target_pairs={{0,384},{128,256},{256,128},{384,0},{1,385},{129,257},{257,129},{3... | collective-permute-start | bytes 1179656 | tf_op jit(solution)/shard_map/ppermute | solution.py:366
  100.9 17.5 %collective-permute-start = (bf16[256,768]{1,0:T(8,128)(2,1)}, bf16[256,768]{1,0:T(8,128)(2,1)S(1)}, u32[]{:S(2)}, u32[]{:S(2)}) collective-permute-start(bf16[256,768]{1,0:T(8,128)(2,1)} %get-tuple-element.27), channel_id=1, source_target_pairs={{0,384},{128,256},{256,128},{384,0},{1,385},{129,257},{257,129},{3... | collective-permute-start | bytes 1179656 | tf_op jit(solution)/shard_map/ppermute | solution.py:366
  103.7 16.7 %collective-permute-start.2 = (bf16[256,768]{1,0:T(8,128)(2,1)}, bf16[256,768]{1,0:T(8,128)(2,1)S(1)}, u32[]{:S(2)}, u32[]{:S(2)}) collective-permute-start(bf16[256,768]{1,0:T(8,128)(2,1)} %get-tuple-element.29), channel_id=1, source_target_pairs={{0,128},{128,0},{256,384},{384,256},{1,129},{129,1},{257,385},{385... | collective-permute-start | bytes 1179656 | tf_op jit(solution)/shard_map/ppermute | solution.py:363
  105.9 1.0 copy-start.3
  107.0 24.1 %collective-permute-start.5 = (bf16[192,1024]{1,0:T(8,128)(2,1)S(1)}, bf16[192,1024]{1,0:T(8,128)(2,1)S(1)}, u32[]{:S(2)}, u32[]{:S(2)}) collective-permute-start(bf16[192,1024]{1,0:T(8,128)(2,1)S(1)} %down_a.1.sum_a), channel_id=1, source_target_pairs={{0,384},{128,256},{256,128},{384,0},{1,385},{129,257},{257,129},{3... | collective-permute-start | bytes 1179656 | tf_op jit(solution)/shard_map/ppermute | solution.py:366
  111.4 1.0 copy-start.2
  112.5 18.6 %collective-permute-start.7 = (bf16[192,1024]{1,0:T(8,128)(2,1)S(1)}, bf16[192,1024]{1,0:T(8,128)(2,1)S(1)}, u32[]{:S(2)}, u32[]{:S(2)}) collective-permute-start(bf16[192,1024]{1,0:T(8,128)(2,1)S(1)} %down_b.1.sum_b), channel_id=1, source_target_pairs={{0,128},{128,0},{256,384},{384,256},{1,129},{129,1},{257,385},{385... | collective-permute-start | bytes 1179656 | tf_op jit(solution)/shard_map/ppermute | solution.py:363
  118.4 8.9 %collective-permute-start.1 = (bf16[256,384]{1,0:T(8,128)(2,1)S(1)}, bf16[256,384]{1,0:T(8,128)(2,1)S(1)}, u32[]{:S(2)}, u32[]{:S(2)}) collective-permute-start(bf16[256,384]{1,0:T(8,128)(2,1)S(1)} %gate.1), channel_id=1, source_target_pairs={{0,128},{128,0},{256,384},{384,256},{1,129},{129,1},{257,385},{385... | collective-permute-start | bytes 589832 | tf_op jit(solution)/shard_map/ppermute | solution.py:363
  120.5 11.7 %copy-start.4 = (bf16[64,1024]{1,0:T(8,128)(2,1)S(1)}, bf16[64,1024]{1,0:T(8,128)(2,1)}, u32[]{:S(2)}) copy-start(bf16[64,1024]{1,0:T(8,128)(2,1)} %get-tuple-element.19.pick_t) | copy-start | bytes 393220
  120.5 9.8 %collective-permute-start.3 = (bf16[256,384]{1,0:T(8,128)(2,1)S(1)}, bf16[256,384]{1,0:T(8,128)(2,1)S(1)}, u32[]{:S(2)}, u32[]{:S(2)}) collective-permute-start(bf16[256,384]{1,0:T(8,128)(2,1)S(1)} %up.1), channel_id=1, source_target_pairs={{0,384},{128,256},{256,128},{384,0},{1,385},{129,257},{257,129},{3... | collective-permute-start | bytes 589832 | tf_op jit(solution)/shard_map/ppermute | solution.py:366

commit v6 on v5

--- a/solution.py
+++ b/solution.py
@@ -53,7 +53,7 @@
 
 def dispatch_body(
     experts, tok_hbm, cot_hbm, routes_hbm, combine_hbm, hot_hbm, extra_hbm,
-    send, pick_t, both, routes_in, combine_in, hot, extra, sems,
+    send_hbm, pick_hbm, send, pick_t, both, routes_in, combine_in, hot, extra, sems, out_sems,
 ):
     count = tok_hbm.shape[0]
     copies = [
@@ -104,9 +104,17 @@
     scaled = scaled.reshape(experts * MSG, lanes).astype(BF16)
     for copy in copies[4:]:
         copy.wait()
-    send[...] = jnp.dot(scaled, both[...], preferred_element_type=F32).astype(BF16)
+    part = send.shape[0] // CHUNKS
+    departures = []
+    for n in range(CHUNKS):
+        at = pl.ds(n * part, part)
+        block = dot(scaled[n * part : (n + 1) * part, :], both[...], NN)
+        send[at, :] = block.astype(BF16)
+        departures += start_all([pltpu.make_async_copy(send.at[at], send_hbm.at[at], out_sems.at[n])])
     pick = jnp.where(hit, 1.0, 0.0).reshape(experts * MSG, lanes).astype(BF16)
     pick_t[...] = dot(identity(lanes), pick, NT).astype(BF16)
+    departures += start_all([pltpu.make_async_copy(pick_t, pick_hbm, out_sems.at[CHUNKS])])
+    wait_all(departures)
 
 
 def token_body(pick_t, returned, out):
@@ -127,9 +135,11 @@
         copy.wait()
 
 
-def rows_body(
-    recv_hbm, w_gate_hbm, w_up_hbm, w_down_hbm, back_hbm, tok_hbm, og_hbm, in_rows_hbm, hid_hbm,
-    recv, w_in, w_down, back, tok, og, in_rows, hid, wide, narrow, pre, grad, in_sems, out_sems,
+def expert_body(
+    ranks, me, recv_hbm, w_gate_hbm, w_up_hbm, w_down_hbm,
+    back_hbm, down_a_hbm, down_b_hbm, even_send_hbm, mirror_send_hbm, even_keep_hbm, mirror_keep_hbm,
+    back, down_a, down_b, even_send, mirror_send, even_keep, mirror_keep,
+    recv, w_in, w_down, wide, narrow, tok, og, pre, grad, in_rows, hid, total, in_sems, out_sems,
 ):
     rows_in, features = recv.shape
     hidden = w_down.shape[0]
@@ -172,8 +182,6 @@
             tok[at, cols] = wide[c, pl.ds(s, peers, MSG), :].astype(BF16)
             og[at, cols] = wide[c, pl.ds(s + SLOTS, peers, MSG), :].astype(BF16)
     wait_all(weights)
-    send_out(tok, tok_hbm)
-    send_out(og, og_hbm)
     pre[...] = dot(tok[...], w_in[...], NN)
     grad[...] = dot(og[...], w_down[...], NT)
     for at in range(0, SLOTS * peers, peers):
@@ -185,8 +193,6 @@
         gate_grad = hidden_grad * up_proj * s * (1.0 + gate_pre * (1.0 - s))
         in_rows[rows, :hidden] = gate_grad.astype(BF16)
         in_rows[rows, hidden:] = (hidden_grad * act).astype(BF16)
-    send_out(hid, hid_hbm)
-    send_out(in_rows, in_rows_hbm)
     grads = dot(in_rows[...], w_in[...], NT)
     for s in range(SLOTS):
         piece = grads[s * peers : (s + 1) * peers, :]
@@ -198,39 +204,6 @@
     for c in range(half // LANES):
         back[:, c * LANES : (c + 1) * LANES] = narrow[c].astype(BF16)
     send_out(back, back_hbm)
-    wait_all(departures)
-
-
-def weights_body(
-    ranks, me, tok_hbm, og_hbm, in_rows_hbm, hid_hbm,
-    down_a_hbm, down_b_hbm, even_send_hbm, mirror_send_hbm, even_keep_hbm, mirror_keep_hbm,
-    tok, og, in_rows, hid,
-    down_a, down_b, even_send, mirror_send, even_keep, mirror_keep,
-    total, in_sems, out_sems,
-):
-    features, hidden = tok.shape[1], hid.shape[1]
-    arrivals = start_all(
-        [
-            pltpu.make_async_copy(source, target, in_sems.at[n])
-            for n, (source, target) in enumerate(
-                [(hid_hbm, hid), (og_hbm, og), (tok_hbm, tok), (in_rows_hbm, in_rows)]
-            )
-        ]
-    )
-    departures = []
-
-    def send_out(source, target):
-        copy = pltpu.make_async_copy(source, target, out_sems.at[len(departures)])
-        departures.extend(start_all([copy]))
-
-    wait_all(arrivals[:2])
-    down = dot(hid[...], og[...], TN).astype(BF16)
-    cut = hidden // 2
-    down_a[...] = down[:cut]
-    send_out(down_a, down_a_hbm)
-    down_b[...] = down[cut:]
-    send_out(down_b, down_b_hbm)
-    wait_all(arrivals[2:])
     total[...] = dot(tok[...], in_rows[...], TN)
     piece = features // ranks
     even = me[0] + 1 - 2 * lax.rem(me[0], 2)
@@ -250,6 +223,12 @@
         keep[:, :hidden] = part_of(other)
         keep[:, hidden:] = part_of(me[0])
         send_out(keep, keep_hbm)
+    down = dot(hid[...], og[...], TN).astype(BF16)
+    cut = hidden // 2
+    down_a[...] = down[:cut]
+    send_out(down_a, down_a_hbm)
+    down_b[...] = down[cut:]
+    send_out(down_b, down_b_hbm)
     wait_all(departures)
 
 
@@ -283,6 +262,8 @@
     hidden = w_gate.shape[2]
     total = experts * MSG
     rows = experts * SLOTS
+    me = lax.axis_index("dp").astype(jnp.int32).reshape(1)
+    me, hot_experts = lax.optimization_barrier((me, hot_experts))
     send, pick_t = call(
         functools.partial(dispatch_body, experts),
         "dispatch",
@@ -292,72 +273,55 @@
         ],
         [ANY] * 6,
         [
+            pltpu.VMEM((total, features), BF16),
+            pltpu.VMEM((2 * count, total), BF16),
             pltpu.VMEM((2 * count, features), BF16),
             pltpu.VMEM(routes.shape[::-1], jnp.int32),
             pltpu.VMEM(combine.shape[::-1], BF16),
             pltpu.SMEM(hot_experts.shape, jnp.int32),
             pltpu.SMEM(extra_slots.shape, jnp.int32),
             pltpu.SemaphoreType.DMA((6,)),
+            pltpu.SemaphoreType.DMA((CHUNKS + 1,)),
         ],
         2 * total * 2 * count * features,
         2 * total * features,
         64 * MIB - 65536,
+        ANY,
     )(tokens, cotangent, routes.T, combine.T, hot_experts, extra_slots)
     recv = lax.all_to_all(send, "expert", split_axis=0, concat_axis=0, tiled=True)
-    me = lax.axis_index("dp").astype(jnp.int32).reshape(1)
     piece = features // ranks
     cut = hidden // 2
     shape = jax.ShapeDtypeStruct
-    saved = [
-        shape((rows, features), BF16),
-        shape((rows, features), BF16),
-        shape((rows, 2 * hidden), BF16),
-        shape((rows, hidden), BF16),
-    ]
-    out = [shape((total, features // 2), BF16)] + saved
-    back, *kept_rows = call(
-        rows_body,
-        "rows",
+    out = [shape((total, features // 2), BF16)]
+    out += [shape((cut, features), BF16)] * 2 + [shape((piece, 2 * hidden), BF16)] * 4
+    back, down_a, down_b, even_send, mirror_send, even_keep, mirror_keep = call(
+        functools.partial(expert_body, ranks),
+        "expert",
         out,
-        [ANY] * 4,
-        [
+        [SMEM] + [ANY] * 4,
+        [pltpu.VMEM(a.shape, a.dtype) for a in out]
+        + [
             pltpu.VMEM((total, features), BF16),
             pltpu.VMEM((features, 2 * hidden), BF16),
             pltpu.VMEM((hidden, features), BF16),
-        ]
-        + [pltpu.VMEM(a.shape, a.dtype) for a in out]
-        + [
             pltpu.VMEM((features // LANES, total, LANES), F32),
             pltpu.VMEM((features // 2 // LANES, total, LANES), F32),
+            pltpu.VMEM((rows, features), BF16),
+            pltpu.VMEM((rows, features), BF16),
             pltpu.VMEM((rows, 2 * hidden), F32),
             pltpu.VMEM((rows, hidden), F32),
+            pltpu.VMEM((rows, 2 * hidden), BF16),
+            pltpu.VMEM((rows, hidden), BF16),
+            pltpu.VMEM((features, 2 * hidden), F32),
             pltpu.SemaphoreType.DMA((CHUNKS + 3,)),
             pltpu.SemaphoreType.DMA((len(out),)),
         ],
-        10 * rows * features * hidden,
-        2 * (total * features * 2 + 3 * features * hidden),
-        64 * MIB - 65536,
+        16 * rows * features * hidden,
+        2 * (total * features * 2 + 6 * features * hidden),
+        48 * MIB,
         ANY,
-    )(recv, w_gate[0], w_up[0], w_down[0])
+    )(me, recv, w_gate[0], w_up[0], w_down[0])
     returned = lax.all_to_all(back, "expert", split_axis=0, concat_axis=0, tiled=True)
-    out = [shape((cut, features), BF16)] * 2 + [shape((piece, 2 * hidden), BF16)] * 4
-    down_a, down_b, even_send, mirror_send, even_keep, mirror_keep = call(
-        functools.partial(weights_body, ranks),
-        "weight_grads",
-        out,
-        [SMEM] + [ANY] * 4,
-        [pltpu.VMEM(a.shape, a.dtype) for a in saved]
-        + [pltpu.VMEM(a.shape, a.dtype) for a in out]
-        + [
-            pltpu.VMEM((features, 2 * hidden), F32),
-            pltpu.SemaphoreType.DMA((len(saved),)),
-            pltpu.SemaphoreType.DMA((len(out),)),
-        ],
-        6 * rows * features * hidden,
-        2 * (rows * (2 * features + 3 * hidden) + 3 * features * hidden),
-        64 * MIB - 65536,
-        ANY,
-    )(me, *kept_rows)
 
     def even(value):
         return lax.ppermute(value, "dp", [(i, i ^ 1) for i in range(ranks)])
@@ -366,7 +330,10 @@
         return lax.ppermute(value, "dp", [(i, ranks - 1 - i) for i in range(ranks)])
 
     def small(body, name, out, *operands):
-        return call(body, name, out, [VMEM] * len(operands))(*operands)
+        moved = sum(2 * a.size for a in operands) + sum(2 * a.size for a in jax.tree.leaves(out))
+        return call(
+            body, name, out, [VMEM] * len(operands), bytes_accessed=moved
+        )(*operands)
 
     first_a, first_b = even(down_a), mirror(down_b)
     up_first, gate_first = even(even_send), mirror(mirror_send)

time: 136 us -> 132 us (0.971)
  Pallas kernels: 18.6 us -> 14.5 us
  local copies, waits for them, and re-layouts: 2 us -> 0.02 us
  waiting for transfers between devices: 10.2 us -> 11.9 us
    pallas_call x8 -> x7, Pallas kernels: 13.2 us -> 10.6 us  [the longest x1 8.43 us: shards(): call(functools.partial(expert_body, ranks), 'expert', out, [SMEM] + [ANY]...]
    unnamed x10 -> x8, local copies, waits for them, and re-layouts: 2 us -> 0.02 us
    ppermute x4, waiting for transfers between devices: 6.9 us -> 8.56 us  [mirror(): return lax.ppermute(value, 'dp', [(i, ranks - 1 - i) for i in range(ranks)])]
  transfers between devices with their start and end apart: 9 -> 9, of which waited for: 4 -> 4; matrix products, arithmetic and copies ran while one was open for 0% -> 0% of each run, Pallas kernels for 5% -> 2%
where the time goes in v6:
time: 132 us; the launch traced here: 130 us
  blocking collectives  70.8 us (54%)
  starting transfers between devices  31.6 us (24%)
  Pallas kernels  14.5 us (11%)
  waiting for transfers between devices  11.9 us (9%)
    all_to_all x1, blocking collectives, shards(): lax.all_to_all(send, 'expert', split_axis=0, concat_axis=0, tiled=True)  70.8 us
    ppermute x4, starting transfers between devices, mirror(): return lax.ppermute(value, 'dp', [(i, ranks - 1 - i) for i in range(ranks)])  14.7 us
    ppermute x4, starting transfers between devices, even(): return lax.ppermute(value, 'dp', [(i, i ^ 1) for i in range(ranks)])  9.03 us
    ppermute x4, waiting for transfers between devices, mirror(): return lax.ppermute(value, 'dp', [(i, ranks - 1 - i) for i in range(ranks)])  8.56 us
    pallas_call x1, Pallas kernels, shards(): call(functools.partial(expert_body, ranks), 'expert', out, [SMEM] + [ANY]...  8.43 us
    all_to_all x1, starting transfers between devices, shards(): lax.all_to_all(back, 'expert', split_axis=0, concat_axis=0, tiled=True)  7.8 us
    ppermute x4, waiting for transfers between devices, even(): return lax.ppermute(value, 'dp', [(i, i ^ 1) for i in range(ranks)])  3.33 us
    pallas_call x1, Pallas kernels, shards(): call(functools.partial(dispatch_body, experts), 'dispatch', [jax.ShapeDty...  2.96 us
  transfers between devices with their start and end apart: 9, of which 4 were waited for; matrix products, arithmetic and copies ran while one was open for 0% of the time, Pallas kernels for 2%

profile of v6, /device:TPU:1, one launch (start us, length us, event | category | flops | bytes accessed | tf_op | source)
XLA Modules:
  0.0 129.6 jit_solution(1975416460153712981)
XLA Ops:
  0.6 3.0 %dispatch.1 = (bf16[1024,1024]{1,0:T(8,128)(2,1)}, bf16[64,1024]{1,0:T(8,128)(2,1)}) custom-call(bf16[32,1024]{1,0:T(8,128)(2,1)} %tok_hbm.1, bf16[32,1024]{1,0:T(8,128)(2,1)} %cot_hbm.1, s32[8,32]{1,0:T(8,128)} %bitcast.22, bf16[8,32]{1,0:T(8,128)(2,1)} %bitcast.23, s32[4]{0:T(128)} %hot_hbm, s32[4]{0:T(128)} %extra_hbm.1), custom_call_target="tpu_custom_call" | custom-call | flops 134217728 | bytes 2097152 | tf_op jit(solution)/shard_map/dispatch/pallas_call | solution.py:267
  3.6 0.0 copy-start.3
  3.6 70.8 %all_to_all.22 = bf16[128,8,1024]{2,1,0:T(8,128)(2,1)} all-to-all(bf16[128,8,1024]{2,1,0:T(8,128)(2,1)} %bitcast.18), channel_id=1, replica_groups=mesh['dp'=4,'expert'=128] {'expert'}, dimensions={0} | all-to-all | bytes 4194304 | tf_op jit(solution)/shard_map/all_to_all | solution.py:291
  74.5 8.4 %expert.1 = (bf16[1024,512]{1,0:T(8,128)(2,1)}, bf16[192,1024]{1,0:T(8,128)(2,1)S(1)}, bf16[192,1024]{1,0:T(8,128)(2,1)S(1)}, bf16[256,768]{1,0:T(8,128)(2,1)S(1...) custom-call(s32[1]{0:T(128)} %bitcast.2.me, ...), custom_call_target="tpu_custom_call" | custom-call | flops 3221225472 | bytes 8912896 | tf_op jit(solution)/shard_map/expert/pallas_call | solution.py:297
  82.9 7.8 %all-to-all-start.1 = ((bf16[128,8,512]{2,1,0:T(8,128)(2,1)}), bf16[128,8,512]{2,1,0:T(8,128)(2,1)S(1)}, u32[]{:S(2)}, u32[]{:S(2)}) async-start(bf16[128,8,512]{2,1,0:T(8,128)(2,1)} %bitcast.8), calls=%async_computation.1 | async-start | bytes 2097152 | tf_op jit(solution)/shard_map/all_to_all | solution.py:324
  90.7 3.1 %collective-permute-start.4 = (bf16[192,1024]{1,0:T(8,128)(2,1)S(1)}, bf16[192,1024]{1,0:T(8,128)(2,1)S(1)}, u32[]{:S(2)}, u32[]{:S(2)}) collective-permute-start(bf16[192,1024]{1,0:T(8,128)(2,1)S(1)} %get-tuple-element.28.kept), channel_id=1, source_target_pairs={{0,128},{128,0},{256,384},{384,256},{1,129},{129,1},{257,385},{385... | collective-permute-start | bytes 1179656 | tf_op jit(solution)/shard_map/ppermute | solution.py:327
  93.9 3.7 %collective-permute-start.6 = (bf16[192,1024]{1,0:T(8,128)(2,1)S(1)}, bf16[192,1024]{1,0:T(8,128)(2,1)S(1)}, u32[]{:S(2)}, u32[]{:S(2)}) collective-permute-start(bf16[192,1024]{1,0:T(8,128)(2,1)S(1)} %get-tuple-element.29.kept), channel_id=1, source_target_pairs={{0,384},{128,256},{256,128},{384,0},{1,385},{129,257},{257,129},{3... | collective-permute-start | bytes 1179656 | tf_op jit(solution)/shard_map/ppermute | solution.py:330
  97.6 2.8 %collective-permute-start = (bf16[256,768]{1,0:T(8,128)(2,1)S(1)}, bf16[256,768]{1,0:T(8,128)(2,1)S(1)}, u32[]{:S(2)}, u32[]{:S(2)}) collective-permute-start(bf16[256,768]{1,0:T(8,128)(2,1)S(1)} %get-tuple-element.23), channel_id=1, source_target_pairs={{0,384},{128,256},{256,128},{384,0},{1,385},{129,257},{257,129},{3... | collective-permute-start | bytes 1179656 | tf_op jit(solution)/shard_map/ppermute | solution.py:330
  100.4 1.9 %collective-permute-start.2 = (bf16[256,768]{1,0:T(8,128)(2,1)S(1)}, bf16[256,768]{1,0:T(8,128)(2,1)S(1)}, u32[]{:S(2)}, u32[]{:S(2)}) collective-permute-start(bf16[256,768]{1,0:T(8,128)(2,1)S(1)} %get-tuple-element.25), channel_id=1, source_target_pairs={{0,128},{128,0},{256,384},{384,256},{1,129},{129,1},{257,385},{385... | collective-permute-start | bytes 1179656 | tf_op jit(solution)/shard_map/ppermute | solution.py:327
  102.3 0.1 collective-permute-done.4.received
  102.3 0.1 down_a.1.sum_a
  102.4 4.4 %collective-permute-start.5 = (bf16[192,1024]{1,0:T(8,128)(2,1)S(1)}, bf16[192,1024]{1,0:T(8,128)(2,1)S(1)}, u32[]{:S(2)}, u32[]{:S(2)}) collective-permute-start(bf16[192,1024]{1,0:T(8,128)(2,1)S(1)} %down_a.1.sum_a), channel_id=1, source_target_pairs={{0,384},{128,256},{256,128},{384,0},{1,385},{129,257},{257,129},{3... | collective-permute-start | bytes 1179656 | tf_op jit(solution)/shard_map/ppermute | solution.py:330
  106.8 0.1 down_b.1.sum_b
  106.9 2.1 %collective-permute-start.7 = (bf16[192,1024]{1,0:T(8,128)(2,1)S(1)}, bf16[192,1024]{1,0:T(8,128)(2,1)S(1)}, u32[]{:S(2)}, u32[]{:S(2)}) collective-permute-start(bf16[192,1024]{1,0:T(8,128)(2,1)S(1)} %down_b.1.sum_b), channel_id=1, source_target_pairs={{0,128},{128,0},{256,384},{384,256},{1,129},{129,1},{257,385},{385... | collective-permute-start | bytes 1179656 | tf_op jit(solution)/shard_map/ppermute | solution.py:327
  109.0 5.8 %collective-permute-done.received.gate_first = bf16[256,768]{1,0:T(8,128)(2,1)S(1)} collective-permute-done((bf16[256,768]{1,0:T(8,128)(2,1)S(1)}, bf16[256,768]{1,0:T(8,128)(2,1)S(1)}, u32[]{:S(2)}, u32[]{:S(2)}) %collective-permute-start) | collective-permute-done | bytes 393248 | tf_op jit(solution)/shard_map/ppermute | solution.py:330
  114.8 0.1 gate.1
  114.9 1.9 %collective-permute-start.1 = (bf16[256,384]{1,0:T(8,128)(2,1)S(1)}, bf16[256,384]{1,0:T(8,128)(2,1)S(1)}, u32[]{:S(2)}, u32[]{:S(2)}) collective-permute-start(bf16[256,384]{1,0:T(8,128)(2,1)S(1)} %gate.1), channel_id=1, source_target_pairs={{0,128},{128,0},{256,384},{384,256},{1,129},{129,1},{257,385},{385... | collective-permute-start | bytes 589832 | tf_op jit(solution)/shard_map/ppermute | solution.py:327
  116.8 0.1 up.1
  116.9 3.9 %collective-permute-start.3 = (bf16[256,384]{1,0:T(8,128)(2,1)S(1)}, bf16[256,384]{1,0:T(8,128)(2,1)S(1)}, u32[]{:S(2)}, u32[]{:S(2)}) collective-permute-start(bf16[256,384]{1,0:T(8,128)(2,1)S(1)} %up.1), channel_id=1, source_target_pairs={{0,384},{128,256},{256,128},{384,0},{1,385},{129,257},{257,129},{3... | collective-permute-start | bytes 589832 | tf_op jit(solution)/shard_map/ppermute | solution.py:330
  120.7 3.3 %collective-permute-done.1.gate_next = bf16[256,384]{1,0:T(8,128)(2,1)S(1)} collective-permute-done((bf16[256,384]{1,0:T(8,128)(2,1)S(1)}, bf16[256,384]{1,0:T(8,128)(2,1)S(1)}, u32[]{:S(2)}, u32[]{:S(2)}) %collective-permute-start.1) | collective-permute-done | bytes 196640 | tf_op jit(solution)/shard_map/ppermute | solution.py:327
  124.0 2.7 %collective-permute-done.3.up_next = bf16[256,384]{1,0:T(8,128)(2,1)S(1)} collective-permute-done((bf16[256,384]{1,0:T(8,128)(2,1)S(1)}, bf16[256,384]{1,0:T(8,128)(2,1)S(1)}, u32[]{:S(2)}, u32[]{:S(2)}) %collective-permute-start.3) | collective-permute-done | bytes 196640 | tf_op jit(solution)/shard_map/ppermute | solution.py:330
  126.8 0.8 pair.1
  127.6 1.1 down.1
  128.7 0.9 token_grad.1
  (12 shorter events, 0.0 us)
Async XLA Ops:
  3.6 70.9 %copy-start.1 = (bf16[1,1024,384]{2,1,0:T(8,128)(2,1)S(1)}, bf16[1,1024,384]{2,1,0:T(8,128)(2,1)}, u32[]{:S(2)}) copy-start(bf16[1,1024,384]{2,1,0:T(8,128)(2,1)} %param.15) | copy-start | bytes 2359300
  3.6 70.8 %copy-start.2 = (bf16[1,1024,384]{2,1,0:T(8,128)(2,1)S(1)}, bf16[1,1024,384]{2,1,0:T(8,128)(2,1)}, u32[]{:S(2)}) copy-start(bf16[1,1024,384]{2,1,0:T(8,128)(2,1)} %param.16) | copy-start | bytes 2359300
  3.6 70.8 %copy-start.3 = (bf16[1,384,1024]{2,1,0:T(8,128)(2,1)S(1)}, bf16[1,384,1024]{2,1,0:T(8,128)(2,1)}, u32[]{:S(2)}) copy-start(bf16[1,384,1024]{2,1,0:T(8,128)(2,1)} %param.17) | copy-start | bytes 2359300
  82.9 45.7 %all-to-all-start.1 = ((bf16[128,8,512]{2,1,0:T(8,128)(2,1)}), bf16[128,8,512]{2,1,0:T(8,128)(2,1)S(1)}, u32[]{:S(2)}, u32[]{:S(2)}) async-start(bf16[128,8,512]{2,1,0:T(8,128)(2,1)} %bitcast.8), calls=%async_computation.1 | async-start | bytes 2097152 | tf_op jit(solution)/shard_map/all_to_all | solution.py:324
  90.7 11.6 %collective-permute-start.4 = (bf16[192,1024]{1,0:T(8,128)(2,1)S(1)}, bf16[192,1024]{1,0:T(8,128)(2,1)S(1)}, u32[]{:S(2)}, u32[]{:S(2)}) collective-permute-start(bf16[192,1024]{1,0:T(8,128)(2,1)S(1)} %get-tuple-element.28.kept), channel_id=1, source_target_pairs={{0,128},{128,0},{256,384},{384,256},{1,129},{129,1},{257,385},{385... | collective-permute-start | bytes 1179656 | tf_op jit(solution)/shard_map/ppermute | solution.py:327
  93.9 13.0 %collective-permute-start.6 = (bf16[192,1024]{1,0:T(8,128)(2,1)S(1)}, bf16[192,1024]{1,0:T(8,128)(2,1)S(1)}, u32[]{:S(2)}, u32[]{:S(2)}) collective-permute-start(bf16[192,1024]{1,0:T(8,128)(2,1)S(1)} %get-tuple-element.29.kept), channel_id=1, source_target_pairs={{0,384},{128,256},{256,128},{384,0},{1,385},{129,257},{257,129},{3... | collective-permute-start | bytes 1179656 | tf_op jit(solution)/shard_map/ppermute | solution.py:330
  97.6 17.2 %collective-permute-start = (bf16[256,768]{1,0:T(8,128)(2,1)S(1)}, bf16[256,768]{1,0:T(8,128)(2,1)S(1)}, u32[]{:S(2)}, u32[]{:S(2)}) collective-permute-start(bf16[256,768]{1,0:T(8,128)(2,1)S(1)} %get-tuple-element.23), channel_id=1, source_target_pairs={{0,384},{128,256},{256,128},{384,0},{1,385},{129,257},{257,129},{3... | collective-permute-start | bytes 1179656 | tf_op jit(solution)/shard_map/ppermute | solution.py:330
  100.4 16.4 %collective-permute-start.2 = (bf16[256,768]{1,0:T(8,128)(2,1)S(1)}, bf16[256,768]{1,0:T(8,128)(2,1)S(1)}, u32[]{:S(2)}, u32[]{:S(2)}) collective-permute-start(bf16[256,768]{1,0:T(8,128)(2,1)S(1)} %get-tuple-element.25), channel_id=1, source_target_pairs={{0,128},{128,0},{256,384},{384,256},{1,129},{129,1},{257,385},{385... | collective-permute-start | bytes 1179656 | tf_op jit(solution)/shard_map/ppermute | solution.py:327
  102.4 25.1 %collective-permute-start.5 = (bf16[192,1024]{1,0:T(8,128)(2,1)S(1)}, bf16[192,1024]{1,0:T(8,128)(2,1)S(1)}, u32[]{:S(2)}, u32[]{:S(2)}) collective-permute-start(bf16[192,1024]{1,0:T(8,128)(2,1)S(1)} %down_a.1.sum_a), channel_id=1, source_target_pairs={{0,384},{128,256},{256,128},{384,0},{1,385},{129,257},{257,129},{3... | collective-permute-start | bytes 1179656 | tf_op jit(solution)/shard_map/ppermute | solution.py:330
  106.9 20.6 %collective-permute-start.7 = (bf16[192,1024]{1,0:T(8,128)(2,1)S(1)}, bf16[192,1024]{1,0:T(8,128)(2,1)S(1)}, u32[]{:S(2)}, u32[]{:S(2)}) collective-permute-start(bf16[192,1024]{1,0:T(8,128)(2,1)S(1)} %down_b.1.sum_b), channel_id=1, source_target_pairs={{0,128},{128,0},{256,384},{384,256},{1,129},{129,1},{257,385},{385... | collective-permute-start | bytes 1179656 | tf_op jit(solution)/shard_map/ppermute | solution.py:327
  114.9 9.1 %collective-permute-start.1 = (bf16[256,384]{1,0:T(8,128)(2,1)S(1)}, bf16[256,384]{1,0:T(8,128)(2,1)S(1)}, u32[]{:S(2)}, u32[]{:S(2)}) collective-permute-start(bf16[256,384]{1,0:T(8,128)(2,1)S(1)} %gate.1), channel_id=1, source_target_pairs={{0,128},{128,0},{256,384},{384,256},{1,129},{129,1},{257,385},{385... | collective-permute-start | bytes 589832 | tf_op jit(solution)/shard_map/ppermute | solution.py:327
  116.9 11.8 %copy-start = (bf16[64,1024]{1,0:T(8,128)(2,1)S(1)}, bf16[64,1024]{1,0:T(8,128)(2,1)}, u32[]{:S(2)}) copy-start(bf16[64,1024]{1,0:T(8,128)(2,1)} %get-tuple-element.18.pick_t) | copy-start | bytes 393220
  116.9 9.9 %collective-permute-start.3 = (bf16[256,384]{1,0:T(8,128)(2,1)S(1)}, bf16[256,384]{1,0:T(8,128)(2,1)S(1)}, u32[]{:S(2)}, u32[]{:S(2)}) collective-permute-start(bf16[256,384]{1,0:T(8,128)(2,1)S(1)} %up.1), channel_id=1, source_target_pairs={{0,384},{128,256},{256,128},{384,0},{1,385},{129,257},{257,129},{3... | collective-permute-start | bytes 589832 | tf_op jit(solution)/shard_map/ppermute | solution.py:330

commit v7 on v6

--- a/solution.py
+++ b/solution.py
@@ -12,6 +12,7 @@
 MSG = 2 * SLOTS
 LANES = 128
 CHUNKS = 4
+EARLY = 10**10
 F32 = jnp.float32
 BF16 = jnp.bfloat16
 VMEM = pl.BlockSpec(memory_space=pltpu.VMEM)
@@ -137,8 +138,7 @@
 
 def expert_body(
     ranks, me, recv_hbm, w_gate_hbm, w_up_hbm, w_down_hbm,
-    back_hbm, down_a_hbm, down_b_hbm, even_send_hbm, mirror_send_hbm, even_keep_hbm, mirror_keep_hbm,
-    back, down_a, down_b, even_send, mirror_send, even_keep, mirror_keep,
+    back_hbm, down_a_hbm, down_b_hbm, send_hbm, keep_hbm, back, down_a, down_b, send, keep,
     recv, w_in, w_down, wide, narrow, tok, og, pre, grad, in_rows, hid, total, in_sems, out_sems,
 ):
     rows_in, features = recv.shape
@@ -207,22 +207,16 @@
     total[...] = dot(tok[...], in_rows[...], TN)
     piece = features // ranks
     even = me[0] + 1 - 2 * lax.rem(me[0], 2)
-    mirror = ranks - 1 - me[0]
-    opposite = ranks - 1 - even
-    for cols, keep, send, keep_hbm, send_hbm, here, other in (
-        (slice(hidden, 2 * hidden), even_keep, even_send, even_keep_hbm, even_send_hbm, even, mirror),
-        (slice(0, hidden), mirror_keep, mirror_send, mirror_keep_hbm, mirror_send_hbm, mirror, even),
-    ):
-
-        def part_of(index):
-            return total[pl.ds(pl.multiple_of(index * piece, 16), piece), cols].astype(BF16)
-
-        send[:, :hidden] = part_of(opposite)
-        send[:, hidden:] = part_of(here)
-        send_out(send, send_hbm)
-        keep[:, :hidden] = part_of(other)
-        keep[:, hidden:] = part_of(me[0])
-        send_out(keep, keep_hbm)
+
+    def part_of(index):
+        return total[pl.ds(pl.multiple_of(index * piece, 16), piece), :].astype(BF16)
+
+    send[:, : 2 * hidden] = part_of(ranks - 1 - even)
+    send[:, 2 * hidden :] = part_of(even)
+    send_out(send, send_hbm)
+    keep[:, : 2 * hidden] = part_of(ranks - 1 - me[0])
+    keep[:, 2 * hidden :] = part_of(me[0])
+    send_out(keep, keep_hbm)
     down = dot(hid[...], og[...], TN).astype(BF16)
     cut = hidden // 2
     down_a[...] = down[:cut]
@@ -247,12 +241,11 @@
     out[cut:, :] = add(sum_b[...], next_b[...]).astype(BF16)
 
 
-def pair_body(gate_keep, gate_first, gate_next, up_keep, up_first, up_next, grad_gate, grad_up):
+def pair_body(keep, first, second, grad_gate, grad_up):
     hidden = grad_gate.shape[1]
-    gate = add(gate_keep[:, hidden:], gate_first[:, hidden:]) + gate_next[...].astype(F32)
-    up = add(up_keep[:, hidden:], up_first[:, hidden:]) + up_next[...].astype(F32)
-    grad_gate[...] = gate.astype(BF16)
-    grad_up[...] = up.astype(BF16)
+    own = add(keep[:, 2 * hidden :], first[:, 2 * hidden :]) + second[...].astype(F32)
+    grad_gate[...] = own[:, :hidden].astype(BF16)
+    grad_up[...] = own[:, hidden:].astype(BF16)
 
 
 def shards(tokens, cotangent, routes, combine, hot_experts, extra_slots, w_gate, w_up, w_down):
@@ -293,8 +286,8 @@
     cut = hidden // 2
     shape = jax.ShapeDtypeStruct
     out = [shape((total, features // 2), BF16)]
-    out += [shape((cut, features), BF16)] * 2 + [shape((piece, 2 * hidden), BF16)] * 4
-    back, down_a, down_b, even_send, mirror_send, even_keep, mirror_keep = call(
+    out += [shape((cut, features), BF16)] * 2 + [shape((piece, 4 * hidden), BF16)] * 2
+    back, down_a, down_b, send, keep = call(
         functools.partial(expert_body, ranks),
         "expert",
         out,
@@ -318,7 +311,7 @@
         ],
         16 * rows * features * hidden,
         2 * (total * features * 2 + 6 * features * hidden),
-        48 * MIB,
+        44 * MIB,
         ANY,
     )(me, recv, w_gate[0], w_up[0], w_down[0])
     returned = lax.all_to_all(back, "expert", split_axis=0, concat_axis=0, tiled=True)
@@ -329,31 +322,29 @@
     def mirror(value):
         return lax.ppermute(value, "dp", [(i, ranks - 1 - i) for i in range(ranks)])
 
-    def small(body, name, out, *operands):
+    def small(body, name, out, *operands, work=0):
         moved = sum(2 * a.size for a in operands) + sum(2 * a.size for a in jax.tree.leaves(out))
         return call(
-            body, name, out, [VMEM] * len(operands), bytes_accessed=moved
+            body, name, out, [VMEM] * len(operands), flops=work, bytes_accessed=moved
         )(*operands)
 
-    first_a, first_b = even(down_a), mirror(down_b)
-    up_first, gate_first = even(even_send), mirror(mirror_send)
     half_down = shape((cut, features), BF16)
     one_piece = shape((piece, hidden), BF16)
-    sum_a = small(sum_body, "down_a", half_down, down_a, first_a)
-    next_a = mirror(sum_a)
+    first = even(send)
+    first_b = mirror(down_b)
+    first_a = even(down_a)
+    both_pieces = shape((piece, 2 * hidden), BF16)
     sum_b = small(sum_body, "down_b", half_down, down_b, first_b)
     next_b = even(sum_b)
-    up_next = mirror(small(sum_body, "up", one_piece, even_keep, up_first))
-    gate_next = even(small(sum_body, "gate", one_piece, mirror_keep, gate_first))
+    pair_sum = small(sum_body, "pair_sum", both_pieces, keep, first, work=EARLY)
+    second = mirror(pair_sum)
+    kept_a, _, _ = lax.optimization_barrier((down_a, sum_b, pair_sum))
+    sum_a = small(sum_body, "down_a", half_down, kept_a, first_a)
+    next_a = mirror(sum_a)
     grad_down = small(
         down_body, "down", shape((hidden, features), BF16), sum_a, next_a, sum_b, next_b
     )
-    grad_gate, grad_up = small(
-        pair_body,
-        "pair",
-        [one_piece, one_piece],
-        mirror_keep, gate_first, gate_next, even_keep, up_first, up_next,
-    )
+    grad_gate, grad_up = small(pair_body, "pair", [one_piece, one_piece], keep, first, second)
     token_grads = call(
         token_body,
         "token_grad",

time: 132 us -> 132 us (level)
  waiting for transfers between devices: 11.9 us -> 19 us
  starting transfers between devices: 31.6 us -> 26.3 us
  Pallas kernels: 14.5 us -> 12.8 us
    ppermute x4 -> x3, waiting for transfers between devices: 8.56 us -> 19 us  [mirror(): return lax.ppermute(value, 'dp', [(i, ranks - 1 - i) for i in range(ranks)])]
    ppermute x4 -> x3, starting transfers between devices: 14.7 us -> 11 us  [mirror(): return lax.ppermute(value, 'dp', [(i, ranks - 1 - i) for i in range(ranks)])]
    ppermute x4 -> x3, waiting for transfers between devices: 3.33 us -> 0.01 us  [even(): return lax.ppermute(value, 'dp', [(i, i ^ 1) for i in range(ranks)])]
    ppermute x4 -> x3, starting transfers between devices: 9.03 us -> 7.26 us  [even(): return lax.ppermute(value, 'dp', [(i, i ^ 1) for i in range(ranks)])]
    pallas_call x1, Pallas kernels: 8.43 us -> 6.75 us  [shards(): call(functools.partial(expert_body, ranks), 'expert', out, [SMEM] + [ANY]...]
  transfers between devices with their start and end apart: 9 -> 7, of which waited for: 4 -> 3; matrix products, arithmetic and copies ran while one was open for 0% -> 0% of each run, Pallas kernels for 2% -> 2%
where the time goes in v7:
time: 132 us; the launch traced here: 130 us
  blocking collectives  70.7 us (54%)
  starting transfers between devices  26.3 us (20%)
  waiting for transfers between devices  19 us (14%)
  Pallas kernels  12.8 us (10%)
    all_to_all x1, blocking collectives, shards(): lax.all_to_all(send, 'expert', split_axis=0, concat_axis=0, tiled=True)  70.7 us
    ppermute x3, waiting for transfers between devices, mirror(): return lax.ppermute(value, 'dp', [(i, ranks - 1 - i) for i in range(ranks)])  19 us
    ppermute x3, starting transfers between devices, mirror(): return lax.ppermute(value, 'dp', [(i, ranks - 1 - i) for i in range(ranks)])  11 us
    all_to_all x1, starting transfers between devices, shards(): lax.all_to_all(back, 'expert', split_axis=0, concat_axis=0, tiled=True)  8.08 us
    ppermute x3, starting transfers between devices, even(): return lax.ppermute(value, 'dp', [(i, i ^ 1) for i in range(ranks)])  7.26 us
    pallas_call x1, Pallas kernels, shards(): call(functools.partial(expert_body, ranks), 'expert', out, [SMEM] + [ANY]...  6.75 us
    pallas_call x1, Pallas kernels, shards(): call(functools.partial(dispatch_body, experts), 'dispatch', [jax.ShapeDty...  2.95 us
  transfers between devices with their start and end apart: 7, of which 3 were waited for; matrix products, arithmetic and copies ran while one was open for 0% of the time, Pallas kernels for 2%

profile of v7, /device:TPU:1, one launch (start us, length us, event | category | flops | bytes accessed | tf_op | source)
XLA Modules:
  0.0 129.6 jit_solution(5266628130667787974)
XLA Ops:
  0.6 2.9 %dispatch.1 = (bf16[1024,1024]{1,0:T(8,128)(2,1)}, bf16[64,1024]{1,0:T(8,128)(2,1)}) custom-call(bf16[32,1024]{1,0:T(8,128)(2,1)} %tok_hbm.1, bf16[32,1024]{1,0:T(8,128)(2,1)} %cot_hbm.1, s32[8,32]{1,0:T(8,128)} %bitcast.22, bf16[8,32]{1,0:T(8,128)(2,1)} %bitcast.23, s32[4]{0:T(128)} %hot_hbm, s32[4]{0:T(128)} %extra_hbm.1), custom_call_target="tpu_custom_call" | custom-call | flops 134217728 | bytes 2097152 | tf_op jit(solution)/shard_map/dispatch/pallas_call | solution.py:260
  3.6 0.0 copy-start.1
  3.6 0.0 copy-start.2
  3.6 0.0 copy-start.3
  3.6 70.7 %all_to_all.22 = bf16[128,8,1024]{2,1,0:T(8,128)(2,1)S(1)} all-to-all(bf16[128,8,1024]{2,1,0:T(8,128)(2,1)} %bitcast.18), channel_id=1, replica_groups=mesh['dp'=4,'expert'=128] {'expert'}, dimensions={0} | all-to-all | bytes 4194304 | tf_op jit(solution)/shard_map/all_to_all | solution.py:284
  74.3 6.7 %expert.1 = (bf16[1024,512]{1,0:T(8,128)(2,1)}, bf16[192,1024]{1,0:T(8,128)(2,1)S(1)}, bf16[192,1024]{1,0:T(8,128)(2,1)S(1)}, bf16[256,1536]{1,0:T(8,128)(2,1)}, bf16[256,1536]{1,0:T(8,128)(2,1)S(1)}) custom-call(s32[1]{0:T(128)} %bitcast.2.me, bf16[1024,1024]{1,0:T(8,128)(2,1)S(1)} %bitcast.14, bf16[1024,384]{1,0:T(8,128)(2,1)S(1)} %bitcast.15, ...), custom_call_target="tpu_custom_call" | custom-call | flops 3221225472 | bytes 8912896 | tf_op jit(solution)/shard_map/expert/pallas_call | solution.py:290
  81.1 3.1 %collective-permute-start = (bf16[256,1536]{1,0:T(8,128)(2,1)}, bf16[256,1536]{1,0:T(8,128)(2,1)S(1)}, u32[]{:S(2)}, u32[]{:S(2)}) collective-permute-start(bf16[256,1536]{1,0:T(8,128)(2,1)} %get-tuple-element.22), channel_id=1, source_target_pairs={{0,128},{128,0},{256,384},{384,256},{1,129},{129,1},{257,385},{385... | collective-permute-start | bytes 2359304 | tf_op jit(solution)/shard_map/ppermute | solution.py:320
  84.2 8.1 %all-to-all-start.1 = ((bf16[128,8,512]{2,1,0:T(8,128)(2,1)}), bf16[128,8,512]{2,1,0:T(8,128)(2,1)S(1)}, u32[]{:S(2)}, u32[]{:S(2)}) async-start(bf16[128,8,512]{2,1,0:T(8,128)(2,1)} %bitcast.8), calls=%async_computation.1 | async-start | bytes 2097152 | tf_op jit(solution)/shard_map/all_to_all | solution.py:317
  92.3 3.7 %collective-permute-start.2 = (bf16[192,1024]{1,0:T(8,128)(2,1)S(1)}, bf16[192,1024]{1,0:T(8,128)(2,1)S(1)}, u32[]{:S(2)}, u32[]{:S(2)}) collective-permute-start(bf16[192,1024]{1,0:T(8,128)(2,1)S(1)} %get-tuple-element.26.kept), channel_id=1, source_target_pairs={{0,384},{128,256},{256,128},{384,0},{1,385},{129,257},{257,129},{3... | collective-permute-start | bytes 1179656 | tf_op jit(solution)/shard_map/ppermute | solution.py:323
  96.1 2.2 %collective-permute-start.3 = (bf16[192,1024]{1,0:T(8,128)(2,1)S(1)}, bf16[192,1024]{1,0:T(8,128)(2,1)S(1)}, u32[]{:S(2)}, u32[]{:S(2)}) collective-permute-start(bf16[192,1024]{1,0:T(8,128)(2,1)S(1)} %get-tuple-element.27.kept), channel_id=1, source_target_pairs={{0,128},{128,0},{256,384},{384,256},{1,129},{129,1},{257,385},{385... | collective-permute-start | bytes 1179656 | tf_op jit(solution)/shard_map/ppermute | solution.py:320
  98.3 6.9 %collective-permute-done.2.received = bf16[192,1024]{1,0:T(8,128)(2,1)S(1)} collective-permute-done((bf16[192,1024]{1,0:T(8,128)(2,1)S(1)}, bf16[192,1024]{1,0:T(8,128)(2,1)S(1)}, u32[]{:S(2)}, u32[]{:S(2)}) %collective-permute-start.2) | collective-permute-done | bytes 393248 | tf_op jit(solution)/shard_map/ppermute | solution.py:323
  105.2 0.1 down_b.1.sum_b
  105.3 1.9 %collective-permute-start.5 = (bf16[192,1024]{1,0:T(8,128)(2,1)S(1)}, bf16[192,1024]{1,0:T(8,128)(2,1)S(1)}, u32[]{:S(2)}, u32[]{:S(2)}) collective-permute-start(bf16[192,1024]{1,0:T(8,128)(2,1)S(1)} %down_b.1.sum_b), channel_id=1, source_target_pairs={{0,128},{128,0},{256,384},{384,256},{1,129},{129,1},{257,385},{385... | collective-permute-start | bytes 1179656 | tf_op jit(solution)/shard_map/ppermute | solution.py:320
  107.2 0.0 collective-permute-done.received.first
  107.2 0.1 pair_sum.1
  107.3 3.7 %collective-permute-start.1 = (bf16[256,768]{1,0:T(8,128)(2,1)S(1)}, bf16[256,768]{1,0:T(8,128)(2,1)S(1)}, u32[]{:S(2)}, u32[]{:S(2)}) collective-permute-start(bf16[256,768]{1,0:T(8,128)(2,1)S(1)} %pair_sum.1), channel_id=1, source_target_pairs={{0,384},{128,256},{256,128},{384,0},{1,385},{129,257},{257,129},{3... | collective-permute-start | bytes 1179656 | tf_op jit(solution)/shard_map/ppermute | solution.py:323
  111.0 0.1 down_a.1.sum_a
  111.1 3.5 %collective-permute-start.4 = (bf16[192,1024]{1,0:T(8,128)(2,1)S(1)}, bf16[192,1024]{1,0:T(8,128)(2,1)S(1)}, u32[]{:S(2)}, u32[]{:S(2)}) collective-permute-start(bf16[192,1024]{1,0:T(8,128)(2,1)S(1)} %down_a.1.sum_a), channel_id=1, source_target_pairs={{0,384},{128,256},{256,128},{384,0},{1,385},{129,257},{257,129},{3... | collective-permute-start | bytes 1179656 | tf_op jit(solution)/shard_map/ppermute | solution.py:323
  114.7 4.5 %collective-permute-done.1.second = bf16[256,768]{1,0:T(8,128)(2,1)S(1)} collective-permute-done((bf16[256,768]{1,0:T(8,128)(2,1)S(1)}, bf16[256,768]{1,0:T(8,128)(2,1)S(1)}, u32[]{:S(2)}, u32[]{:S(2)}) %collective-permute-start.1) | collective-permute-done | bytes 393248 | tf_op jit(solution)/shard_map/ppermute | solution.py:323
  119.2 0.8 pair.1
  120.0 0.0 collective-permute-done.5.next_b
  120.0 7.6 %collective-permute-done.4.next_a = bf16[192,1024]{1,0:T(8,128)(2,1)S(1)} collective-permute-done((bf16[192,1024]{1,0:T(8,128)(2,1)S(1)}, bf16[192,1024]{1,0:T(8,128)(2,1)S(1)}, u32[]{:S(2)}, u32[]{:S(2)}) %collective-permute-start.4) | collective-permute-done | bytes 393248 | tf_op jit(solution)/shard_map/ppermute | solution.py:323
  127.6 1.1 down.1
  128.7 0.9 token_grad.1
  (7 shorter events, 0.0 us)
Async XLA Ops:
  3.6 70.7 %copy-start.1 = (bf16[1,1024,384]{2,1,0:T(8,128)(2,1)S(1)}, bf16[1,1024,384]{2,1,0:T(8,128)(2,1)}, u32[]{:S(2)}) copy-start(bf16[1,1024,384]{2,1,0:T(8,128)(2,1)} %param.15) | copy-start | bytes 2359300
  3.6 70.7 %copy-start.2 = (bf16[1,1024,384]{2,1,0:T(8,128)(2,1)S(1)}, bf16[1,1024,384]{2,1,0:T(8,128)(2,1)}, u32[]{:S(2)}) copy-start(bf16[1,1024,384]{2,1,0:T(8,128)(2,1)} %param.16) | copy-start | bytes 2359300
  3.6 70.7 %copy-start.3 = (bf16[1,384,1024]{2,1,0:T(8,128)(2,1)S(1)}, bf16[1,384,1024]{2,1,0:T(8,128)(2,1)}, u32[]{:S(2)}) copy-start(bf16[1,384,1024]{2,1,0:T(8,128)(2,1)} %param.17) | copy-start | bytes 2359300
  81.1 26.1 %collective-permute-start = (bf16[256,1536]{1,0:T(8,128)(2,1)}, bf16[256,1536]{1,0:T(8,128)(2,1)S(1)}, u32[]{:S(2)}, u32[]{:S(2)}) collective-permute-start(bf16[256,1536]{1,0:T(8,128)(2,1)} %get-tuple-element.22), channel_id=1, source_target_pairs={{0,128},{128,0},{256,384},{384,256},{1,129},{129,1},{257,385},{385... | collective-permute-start | bytes 2359304 | tf_op jit(solution)/shard_map/ppermute | solution.py:320
  84.2 44.5 %all-to-all-start.1 = ((bf16[128,8,512]{2,1,0:T(8,128)(2,1)}), bf16[128,8,512]{2,1,0:T(8,128)(2,1)S(1)}, u32[]{:S(2)}, u32[]{:S(2)}) async-start(bf16[128,8,512]{2,1,0:T(8,128)(2,1)} %bitcast.8), calls=%async_computation.1 | async-start | bytes 2097152 | tf_op jit(solution)/shard_map/all_to_all | solution.py:317
  92.3 12.8 %collective-permute-start.2 = (bf16[192,1024]{1,0:T(8,128)(2,1)S(1)}, bf16[192,1024]{1,0:T(8,128)(2,1)S(1)}, u32[]{:S(2)}, u32[]{:S(2)}) collective-permute-start(bf16[192,1024]{1,0:T(8,128)(2,1)S(1)} %get-tuple-element.26.kept), channel_id=1, source_target_pairs={{0,384},{128,256},{256,128},{384,0},{1,385},{129,257},{257,129},{3... | collective-permute-start | bytes 1179656 | tf_op jit(solution)/shard_map/ppermute | solution.py:323
  96.1 15.0 %collective-permute-start.3 = (bf16[192,1024]{1,0:T(8,128)(2,1)S(1)}, bf16[192,1024]{1,0:T(8,128)(2,1)S(1)}, u32[]{:S(2)}, u32[]{:S(2)}) collective-permute-start(bf16[192,1024]{1,0:T(8,128)(2,1)S(1)} %get-tuple-element.27.kept), channel_id=1, source_target_pairs={{0,128},{128,0},{256,384},{384,256},{1,129},{129,1},{257,385},{385... | collective-permute-start | bytes 1179656 | tf_op jit(solution)/shard_map/ppermute | solution.py:320
  105.3 14.8 %collective-permute-start.5 = (bf16[192,1024]{1,0:T(8,128)(2,1)S(1)}, bf16[192,1024]{1,0:T(8,128)(2,1)S(1)}, u32[]{:S(2)}, u32[]{:S(2)}) collective-permute-start(bf16[192,1024]{1,0:T(8,128)(2,1)S(1)} %down_b.1.sum_b), channel_id=1, source_target_pairs={{0,128},{128,0},{256,384},{384,256},{1,129},{129,1},{257,385},{385... | collective-permute-start | bytes 1179656 | tf_op jit(solution)/shard_map/ppermute | solution.py:320
  107.3 11.9 %collective-permute-start.1 = (bf16[256,768]{1,0:T(8,128)(2,1)S(1)}, bf16[256,768]{1,0:T(8,128)(2,1)S(1)}, u32[]{:S(2)}, u32[]{:S(2)}) collective-permute-start(bf16[256,768]{1,0:T(8,128)(2,1)S(1)} %pair_sum.1), channel_id=1, source_target_pairs={{0,384},{128,256},{256,128},{384,0},{1,385},{129,257},{257,129},{3... | collective-permute-start | bytes 1179656 | tf_op jit(solution)/shard_map/ppermute | solution.py:323
  111.1 17.6 %copy-start = (bf16[64,1024]{1,0:T(8,128)(2,1)S(1)}, bf16[64,1024]{1,0:T(8,128)(2,1)}, u32[]{:S(2)}) copy-start(bf16[64,1024]{1,0:T(8,128)(2,1)} %get-tuple-element.17.pick_t) | copy-start | bytes 393220
  111.1 16.5 %collective-permute-start.4 = (bf16[192,1024]{1,0:T(8,128)(2,1)S(1)}, bf16[192,1024]{1,0:T(8,128)(2,1)S(1)}, u32[]{:S(2)}, u32[]{:S(2)}) collective-permute-start(bf16[192,1024]{1,0:T(8,128)(2,1)S(1)} %down_a.1.sum_a), channel_id=1, source_target_pairs={{0,384},{128,256},{256,128},{384,0},{1,385},{129,257},{257,129},{3... | collective-permute-start | bytes 1179656 | tf_op jit(solution)/shard_map/ppermute | solution.py:323

commit v8 on v7

--- a/solution.py
+++ b/solution.py
@@ -12,7 +12,7 @@
 MSG = 2 * SLOTS
 LANES = 128
 CHUNKS = 4
-EARLY = 10**10
+EARLY = 3 * 10**10
 F32 = jnp.float32
 BF16 = jnp.bfloat16
 VMEM = pl.BlockSpec(memory_space=pltpu.VMEM)
@@ -218,7 +218,7 @@
     keep[:, 2 * hidden :] = part_of(me[0])
     send_out(keep, keep_hbm)
     down = dot(hid[...], og[...], TN).astype(BF16)
-    cut = hidden // 2
+    cut = down_a.shape[0]
     down_a[...] = down[:cut]
     send_out(down_a, down_a_hbm)
     down_b[...] = down[cut:]
@@ -283,10 +283,11 @@
     )(tokens, cotangent, routes.T, combine.T, hot_experts, extra_slots)
     recv = lax.all_to_all(send, "expert", split_axis=0, concat_axis=0, tiled=True)
     piece = features // ranks
-    cut = hidden // 2
+    cut = hidden // 3
     shape = jax.ShapeDtypeStruct
     out = [shape((total, features // 2), BF16)]
-    out += [shape((cut, features), BF16)] * 2 + [shape((piece, 4 * hidden), BF16)] * 2
+    parts = [shape((cut, features), BF16), shape((hidden - cut, features), BF16)]
+    out += parts + [shape((piece, 4 * hidden), BF16)] * 2
     back, down_a, down_b, send, keep = call(
         functools.partial(expert_body, ranks),
         "expert",
@@ -328,18 +329,17 @@
             body, name, out, [VMEM] * len(operands), flops=work, bytes_accessed=moved
         )(*operands)
 
-    half_down = shape((cut, features), BF16)
     one_piece = shape((piece, hidden), BF16)
     first = even(send)
     first_b = mirror(down_b)
     first_a = even(down_a)
     both_pieces = shape((piece, 2 * hidden), BF16)
-    sum_b = small(sum_body, "down_b", half_down, down_b, first_b)
+    sum_b = small(sum_body, "down_b", parts[1], down_b, first_b)
     next_b = even(sum_b)
     pair_sum = small(sum_body, "pair_sum", both_pieces, keep, first, work=EARLY)
     second = mirror(pair_sum)
     kept_a, _, _ = lax.optimization_barrier((down_a, sum_b, pair_sum))
-    sum_a = small(sum_body, "down_a", half_down, kept_a, first_a)
+    sum_a = small(sum_body, "down_a", parts[0], kept_a, first_a)
     next_a = mirror(sum_a)
     grad_down = small(
         down_body, "down", shape((hidden, features), BF16), sum_a, next_a, sum_b, next_b

time: 132 us -> 128 us (0.970); the launches traced: 130 us -> 127 us
  waiting for transfers between devices: 19 us -> 14.8 us
    ppermute x3, waiting for transfers between devices: 19 us -> 3.51 us  [mirror(): return lax.ppermute(value, 'dp', [(i, ranks - 1 - i) for i in range(ranks)])]
    ppermute x3, waiting for transfers between devices: 0.01 us -> 7.02 us  [even(): return lax.ppermute(value, 'dp', [(i, i ^ 1) for i in range(ranks)])]
    all_to_all x1, waiting for transfers between devices: 0.01 us -> 4.27 us  [shards(): lax.all_to_all(back, 'expert', split_axis=0, concat_axis=0, tiled=True)]
  transfers between devices with their start and end apart: 7 -> 7, of which waited for: 3 -> 5; matrix products, arithmetic and copies ran while one was open for 0% -> 0% of each run, Pallas kernels for 2% -> 3%
where the time goes in v8:
time: 128 us; the launch traced here: 127 us
  blocking collectives  70.7 us (55%)
  starting transfers between devices  27.6 us (22%)
  waiting for transfers between devices  14.8 us (12%)
  Pallas kernels  13.5 us (11%)
    all_to_all x1, blocking collectives, shards(): lax.all_to_all(send, 'expert', split_axis=0, concat_axis=0, tiled=True)  70.7 us
    ppermute x3, starting transfers between devices, mirror(): return lax.ppermute(value, 'dp', [(i, ranks - 1 - i) for i in range(ranks)])  12 us
    all_to_all x1, starting transfers between devices, shards(): lax.all_to_all(back, 'expert', split_axis=0, concat_axis=0, tiled=True)  8.36 us
    ppermute x3, starting transfers between devices, even(): return lax.ppermute(value, 'dp', [(i, i ^ 1) for i in range(ranks)])  7.26 us
    ppermute x3, waiting for transfers between devices, even(): return lax.ppermute(value, 'dp', [(i, i ^ 1) for i in range(ranks)])  7.02 us
    pallas_call x1, Pallas kernels, shards(): call(functools.partial(expert_body, ranks), 'expert', out, [SMEM] + [ANY]...  6.44 us
    all_to_all x1, waiting for transfers between devices, shards(): lax.all_to_all(back, 'expert', split_axis=0, concat_axis=0, tiled=True)  4.27 us
    ppermute x3, waiting for transfers between devices, mirror(): return lax.ppermute(value, 'dp', [(i, ranks - 1 - i) for i in range(ranks)])  3.51 us
  transfers between devices with their start and end apart: 7, of which 5 were waited for; matrix products, arithmetic and copies ran while one was open for 0% of the time, Pallas kernels for 3%

profile of v8, /device:TPU:1, one launch (start us, length us, event | category | flops | bytes accessed | tf_op | source)
XLA Modules:
  0.0 127.4 jit_solution(6495899202778365345)
XLA Ops:
  0.6 2.9 %dispatch.1 = (bf16[1024,1024]{1,0:T(8,128)(2,1)}, bf16[64,1024]{1,0:T(8,128)(2,1)}) custom-call(bf16[32,1024]{1,0:T(8,128)(2,1)} %tok_hbm.1, bf16[32,1024]{1,0:T(8,128)(2,1)} %cot_hbm.1, s32[8,32]{1,0:T(8,128)} %bitcast.22, bf16[8,32]{1,0:T(8,128)(2,1)} %bitcast.23, s32[4]{0:T(128)} %hot_hbm, s32[4]{0:T(128)} %extra_hbm.1), custom_call_target="tpu_custom_call" | custom-call | flops 134217728 | bytes 2097152 | tf_op jit(solution)/shard_map/dispatch/pallas_call | solution.py:260
  3.6 0.0 copy-start.1
  3.6 0.0 copy-start.2
  3.6 0.0 copy-start.3
  3.6 70.7 %all_to_all.22 = bf16[128,8,1024]{2,1,0:T(8,128)(2,1)S(1)} all-to-all(bf16[128,8,1024]{2,1,0:T(8,128)(2,1)} %bitcast.18), channel_id=1, replica_groups=mesh['dp'=4,'expert'=128] {'expert'}, dimensions={0} | all-to-all | bytes 4194304 | tf_op jit(solution)/shard_map/all_to_all | solution.py:284
  74.3 6.4 %expert.1 = (bf16[1024,512]{1,0:T(8,128)(2,1)}, bf16[128,1024]{1,0:T(8,128)(2,1)S(1)}, bf16[256,1024]{1,0:T(8,128)(2,1)S(1)}, bf16[256,1536]{1,0:T(8,128)(2,1)}, bf16[256,1536]{1,0:T(8,128)(2,1)S(1)}) custom-call(s32[1]{0:T(128)} %bitcast.2.me, bf16[1024,1024]{1,0:T(8,128)(2,1)S(1)} %bitcast.14, bf16[1024,384]{1,0:T(8,128)(2,1)S(1)} %bitcast.15, ...), custom_call_target="tpu_custom_call" | custom-call | flops 3221225472 | bytes 8912896 | tf_op jit(solution)/shard_map/expert/pallas_call | solution.py:291
  80.8 3.1 %collective-permute-start = (bf16[256,1536]{1,0:T(8,128)(2,1)}, bf16[256,1536]{1,0:T(8,128)(2,1)S(1)}, u32[]{:S(2)}, u32[]{:S(2)}) collective-permute-start(bf16[256,1536]{1,0:T(8,128)(2,1)} %get-tuple-element.22), channel_id=1, source_target_pairs={{0,128},{128,0},{256,384},{384,256},{1,129},{129,1},{257,385},{385... | collective-permute-start | bytes 2359304 | tf_op jit(solution)/shard_map/ppermute | solution.py:321
  83.9 3.7 %collective-permute-start.2 = (bf16[256,1024]{1,0:T(8,128)(2,1)S(1)}, bf16[256,1024]{1,0:T(8,128)(2,1)}, u32[]{:S(2)}, u32[]{:S(2)}) collective-permute-start(bf16[256,1024]{1,0:T(8,128)(2,1)S(1)} %get-tuple-element.26.kept), channel_id=1, source_target_pairs={{0,384},{128,256},{256,128},{384,0},{1,385},{129,257},{257,129},{3... | collective-permute-start | bytes 1572872 | tf_op jit(solution)/shard_map/ppermute | solution.py:324
  87.7 8.4 %all-to-all-start.1 = ((bf16[128,8,512]{2,1,0:T(8,128)(2,1)}), bf16[128,8,512]{2,1,0:T(8,128)(2,1)S(1)}, u32[]{:S(2)}, u32[]{:S(2)}) async-start(bf16[128,8,512]{2,1,0:T(8,128)(2,1)} %bitcast.8), calls=%async_computation.1 | async-start | bytes 2097152 | tf_op jit(solution)/shard_map/all_to_all | solution.py:318
  96.0 2.2 %collective-permute-start.3 = (bf16[128,1024]{1,0:T(8,128)(2,1)S(1)}, bf16[128,1024]{1,0:T(8,128)(2,1)S(1)}, u32[]{:S(2)}, u32[]{:S(2)}) collective-permute-start(bf16[128,1024]{1,0:T(8,128)(2,1)S(1)} %get-tuple-element.27.kept), channel_id=1, source_target_pairs={{0,128},{128,0},{256,384},{384,256},{1,129},{129,1},{257,385},{385... | collective-permute-start | bytes 786440 | tf_op jit(solution)/shard_map/ppermute | solution.py:321
  98.3 1.4 %collective-permute-done.2.received = bf16[256,1024]{1,0:T(8,128)(2,1)} collective-permute-done((bf16[256,1024]{1,0:T(8,128)(2,1)S(1)}, bf16[256,1024]{1,0:T(8,128)(2,1)}, u32[]{:S(2)}, u32[]{:S(2)}) %collective-permute-start.2) | collective-permute-done | bytes 524320 | tf_op jit(solution)/shard_map/ppermute | solution.py:324
  99.6 1.2 down_b.1.sum_b
  100.8 1.9 %collective-permute-start.5 = (bf16[256,1024]{1,0:T(8,128)(2,1)S(1)}, bf16[256,1024]{1,0:T(8,128)(2,1)S(1)}, u32[]{:S(2)}, u32[]{:S(2)}) collective-permute-start(bf16[256,1024]{1,0:T(8,128)(2,1)S(1)} %down_b.1.sum_b), channel_id=1, source_target_pairs={{0,128},{128,0},{256,384},{384,256},{1,129},{129,1},{257,385},{385... | collective-permute-start | bytes 1572872 | tf_op jit(solution)/shard_map/ppermute | solution.py:321
  102.7 0.1 pair_sum.1
  102.8 3.7 %collective-permute-start.1 = (bf16[256,768]{1,0:T(8,128)(2,1)S(1)}, bf16[256,768]{1,0:T(8,128)(2,1)S(1)}, u32[]{:S(2)}, u32[]{:S(2)}) collective-permute-start(bf16[256,768]{1,0:T(8,128)(2,1)S(1)} %pair_sum.1), channel_id=1, source_target_pairs={{0,384},{128,256},{256,128},{384,0},{1,385},{129,257},{257,129},{3... | collective-permute-start | bytes 1179656 | tf_op jit(solution)/shard_map/ppermute | solution.py:324
  106.6 0.4 collective-permute-done.3.received
  106.9 0.1 down_a.1.sum_a
  107.0 4.5 %collective-permute-start.4 = (bf16[128,1024]{1,0:T(8,128)(2,1)S(1)}, bf16[128,1024]{1,0:T(8,128)(2,1)S(1)}, u32[]{:S(2)}, u32[]{:S(2)}) collective-permute-start(bf16[128,1024]{1,0:T(8,128)(2,1)S(1)} %down_a.1.sum_a), channel_id=1, source_target_pairs={{0,384},{128,256},{256,128},{384,0},{1,385},{129,257},{257,129},{3... | collective-permute-start | bytes 786440 | tf_op jit(solution)/shard_map/ppermute | solution.py:324
  111.5 6.6 %collective-permute-done.5.next_b = bf16[256,1024]{1,0:T(8,128)(2,1)S(1)} collective-permute-done((bf16[256,1024]{1,0:T(8,128)(2,1)S(1)}, bf16[256,1024]{1,0:T(8,128)(2,1)S(1)}, u32[]{:S(2)}, u32[]{:S(2)}) %collective-permute-start.5) | collective-permute-done | bytes 524320 | tf_op jit(solution)/shard_map/ppermute | solution.py:321
  118.2 2.1 %collective-permute-done.4.next_a = bf16[128,1024]{1,0:T(8,128)(2,1)S(1)} collective-permute-done((bf16[128,1024]{1,0:T(8,128)(2,1)S(1)}, bf16[128,1024]{1,0:T(8,128)(2,1)S(1)}, u32[]{:S(2)}, u32[]{:S(2)}) %collective-permute-start.4) | collective-permute-done | bytes 262176 | tf_op jit(solution)/shard_map/ppermute | solution.py:324
  120.3 1.1 down.1
  121.4 0.8 pair.1
  122.2 4.3 %all-to-all-done.1 = bf16[128,8,512]{2,1,0:T(8,128)(2,1)S(1)} async-done(((bf16[128,8,512]{2,1,0:T(8,128)(2,1)}), bf16[128,8,512]{2,1,0:T(8,128)(2,1)S(1)}, u32[]{:S(2)}, u32[]{:S(2)}) %all-to-all-start.1) | async-done | bytes 1048608 | tf_op jit(solution)/shard_map/all_to_all | solution.py:318
  126.5 0.9 token_grad.1
  (7 shorter events, 0.0 us)
Async XLA Ops:
  3.6 70.7 %copy-start.1 = (bf16[1,1024,384]{2,1,0:T(8,128)(2,1)S(1)}, bf16[1,1024,384]{2,1,0:T(8,128)(2,1)}, u32[]{:S(2)}) copy-start(bf16[1,1024,384]{2,1,0:T(8,128)(2,1)} %param.15) | copy-start | bytes 2359300
  3.6 70.7 %copy-start.2 = (bf16[1,1024,384]{2,1,0:T(8,128)(2,1)S(1)}, bf16[1,1024,384]{2,1,0:T(8,128)(2,1)}, u32[]{:S(2)}) copy-start(bf16[1,1024,384]{2,1,0:T(8,128)(2,1)} %param.16) | copy-start | bytes 2359300
  3.6 70.7 %copy-start.3 = (bf16[1,384,1024]{2,1,0:T(8,128)(2,1)S(1)}, bf16[1,384,1024]{2,1,0:T(8,128)(2,1)}, u32[]{:S(2)}) copy-start(bf16[1,384,1024]{2,1,0:T(8,128)(2,1)} %param.17) | copy-start | bytes 2359300
  80.8 21.9 %collective-permute-start = (bf16[256,1536]{1,0:T(8,128)(2,1)}, bf16[256,1536]{1,0:T(8,128)(2,1)S(1)}, u32[]{:S(2)}, u32[]{:S(2)}) collective-permute-start(bf16[256,1536]{1,0:T(8,128)(2,1)} %get-tuple-element.22), channel_id=1, source_target_pairs={{0,128},{128,0},{256,384},{384,256},{1,129},{129,1},{257,385},{385... | collective-permute-start | bytes 2359304 | tf_op jit(solution)/shard_map/ppermute | solution.py:321
  83.9 15.7 %collective-permute-start.2 = (bf16[256,1024]{1,0:T(8,128)(2,1)S(1)}, bf16[256,1024]{1,0:T(8,128)(2,1)}, u32[]{:S(2)}, u32[]{:S(2)}) collective-permute-start(bf16[256,1024]{1,0:T(8,128)(2,1)S(1)} %get-tuple-element.26.kept), channel_id=1, source_target_pairs={{0,384},{128,256},{256,128},{384,0},{1,385},{129,257},{257,129},{3... | collective-permute-start | bytes 1572872 | tf_op jit(solution)/shard_map/ppermute | solution.py:324
  87.7 38.8 %all-to-all-start.1 = ((bf16[128,8,512]{2,1,0:T(8,128)(2,1)}), bf16[128,8,512]{2,1,0:T(8,128)(2,1)S(1)}, u32[]{:S(2)}, u32[]{:S(2)}) async-start(bf16[128,8,512]{2,1,0:T(8,128)(2,1)} %bitcast.8), calls=%async_computation.1 | async-start | bytes 2097152 | tf_op jit(solution)/shard_map/all_to_all | solution.py:318
  96.0 10.9 %collective-permute-start.3 = (bf16[128,1024]{1,0:T(8,128)(2,1)S(1)}, bf16[128,1024]{1,0:T(8,128)(2,1)S(1)}, u32[]{:S(2)}, u32[]{:S(2)}) collective-permute-start(bf16[128,1024]{1,0:T(8,128)(2,1)S(1)} %get-tuple-element.27.kept), channel_id=1, source_target_pairs={{0,128},{128,0},{256,384},{384,256},{1,129},{129,1},{257,385},{385... | collective-permute-start | bytes 786440 | tf_op jit(solution)/shard_map/ppermute | solution.py:321
  100.8 17.4 %collective-permute-start.5 = (bf16[256,1024]{1,0:T(8,128)(2,1)S(1)}, bf16[256,1024]{1,0:T(8,128)(2,1)S(1)}, u32[]{:S(2)}, u32[]{:S(2)}) collective-permute-start(bf16[256,1024]{1,0:T(8,128)(2,1)S(1)} %down_b.1.sum_b), channel_id=1, source_target_pairs={{0,128},{128,0},{256,384},{384,256},{1,129},{129,1},{257,385},{385... | collective-permute-start | bytes 1572872 | tf_op jit(solution)/shard_map/ppermute | solution.py:321
  102.8 18.5 %collective-permute-start.1 = (bf16[256,768]{1,0:T(8,128)(2,1)S(1)}, bf16[256,768]{1,0:T(8,128)(2,1)S(1)}, u32[]{:S(2)}, u32[]{:S(2)}) collective-permute-start(bf16[256,768]{1,0:T(8,128)(2,1)S(1)} %pair_sum.1), channel_id=1, source_target_pairs={{0,384},{128,256},{256,128},{384,0},{1,385},{129,257},{257,129},{3... | collective-permute-start | bytes 1179656 | tf_op jit(solution)/shard_map/ppermute | solution.py:324
  107.0 19.5 %copy-start = (bf16[64,1024]{1,0:T(8,128)(2,1)S(1)}, bf16[64,1024]{1,0:T(8,128)(2,1)}, u32[]{:S(2)}) copy-start(bf16[64,1024]{1,0:T(8,128)(2,1)} %get-tuple-element.17.pick_t) | copy-start | bytes 393220
  107.0 13.3 %collective-permute-start.4 = (bf16[128,1024]{1,0:T(8,128)(2,1)S(1)}, bf16[128,1024]{1,0:T(8,128)(2,1)S(1)}, u32[]{:S(2)}, u32[]{:S(2)}) collective-permute-start(bf16[128,1024]{1,0:T(8,128)(2,1)S(1)} %down_a.1.sum_a), channel_id=1, source_target_pairs={{0,384},{128,256},{256,128},{384,0},{1,385},{129,257},{257,129},{3... | collective-permute-start | bytes 786440 | tf_op jit(solution)/shard_map/ppermute | solution.py:324

commit v9 on v8

--- a/solution.py
+++ b/solution.py
@@ -12,7 +12,8 @@
 MSG = 2 * SLOTS
 LANES = 128
 CHUNKS = 4
-EARLY = 3 * 10**10
+LATER = 10**10
+SOONER = 5 * 10**9
 F32 = jnp.float32
 BF16 = jnp.bfloat16
 VMEM = pl.BlockSpec(memory_space=pltpu.VMEM)
@@ -137,25 +138,17 @@
 
 
 def expert_body(
-    ranks, me, recv_hbm, w_gate_hbm, w_up_hbm, w_down_hbm,
+    ranks, me, recv, w_gate_hbm, w_up_hbm, w_down_hbm,
     back_hbm, down_a_hbm, down_b_hbm, send_hbm, keep_hbm, back, down_a, down_b, send, keep,
-    recv, w_in, w_down, wide, narrow, tok, og, pre, grad, in_rows, hid, total, in_sems, out_sems,
+    w_in, w_down, wide, narrow, tok, og, pre, grad, in_rows, hid, total, in_sems, out_sems,
 ):
     rows_in, features = recv.shape
     hidden = w_down.shape[0]
     peers = rows_in // MSG
     half = features // 2
-    step = rows_in // CHUNKS
-    chunks = [pl.ds(n * step, step) for n in range(CHUNKS)]
-    arrivals = start_all(
-        [
-            pltpu.make_async_copy(recv_hbm.at[at], recv.at[at], in_sems.at[n])
-            for n, at in enumerate(chunks)
-        ]
-    )
     weights = start_all(
         [
-            pltpu.make_async_copy(source, target, in_sems.at[CHUNKS + n])
+            pltpu.make_async_copy(source, target, in_sems.at[n])
             for n, (source, target) in enumerate(
                 [
                     (w_gate_hbm, w_in.at[:, pl.ds(0, hidden)]),
@@ -171,10 +164,8 @@
         copy = pltpu.make_async_copy(source, target, out_sems.at[len(departures)])
         departures.extend(start_all([copy]))
 
-    for copy, at in zip(arrivals, chunks):
-        copy.wait()
-        for c in range(features // LANES):
-            wide[c, at, :] = recv[at, c * LANES : (c + 1) * LANES].astype(F32)
+    for c in range(features // LANES):
+        wide[c] = recv[:, c * LANES : (c + 1) * LANES].astype(F32)
     for s in range(SLOTS):
         at = pl.ds(s * peers, peers)
         for c in range(features // LANES):
@@ -292,10 +283,9 @@
         functools.partial(expert_body, ranks),
         "expert",
         out,
-        [SMEM] + [ANY] * 4,
+        [SMEM, VMEM] + [ANY] * 3,
         [pltpu.VMEM(a.shape, a.dtype) for a in out]
         + [
-            pltpu.VMEM((total, features), BF16),
             pltpu.VMEM((features, 2 * hidden), BF16),
             pltpu.VMEM((hidden, features), BF16),
             pltpu.VMEM((features // LANES, total, LANES), F32),
@@ -307,7 +297,7 @@
             pltpu.VMEM((rows, 2 * hidden), BF16),
             pltpu.VMEM((rows, hidden), BF16),
             pltpu.VMEM((features, 2 * hidden), F32),
-            pltpu.SemaphoreType.DMA((CHUNKS + 3,)),
+            pltpu.SemaphoreType.DMA((3,)),
             pltpu.SemaphoreType.DMA((len(out),)),
         ],
         16 * rows * features * hidden,
@@ -334,12 +324,12 @@
     first_b = mirror(down_b)
     first_a = even(down_a)
     both_pieces = shape((piece, 2 * hidden), BF16)
-    sum_b = small(sum_body, "down_b", parts[1], down_b, first_b)
+    sum_b = small(sum_body, "down_b", parts[1], down_b, first_b, work=SOONER)
     next_b = even(sum_b)
-    pair_sum = small(sum_body, "pair_sum", both_pieces, keep, first, work=EARLY)
+    pair_sum = small(sum_body, "pair_sum", both_pieces, keep, first, work=LATER)
     second = mirror(pair_sum)
     kept_a, _, _ = lax.optimization_barrier((down_a, sum_b, pair_sum))
-    sum_a = small(sum_body, "down_a", parts[0], kept_a, first_a)
+    sum_a = small(sum_body, "down_a", parts[0], kept_a, first_a, work=LATER)
     next_a = mirror(sum_a)
     grad_down = small(
         down_body, "down", shape((hidden, features), BF16), sum_a, next_a, sum_b, next_b

time: 128 us -> 129 us (level)
  starting transfers between devices: 27.6 us -> 24.3 us
  waiting for transfers between devices: 14.8 us -> 17.3 us
    ppermute x3, waiting for transfers between devices: 7.02 us -> 15.4 us  [even(): return lax.ppermute(value, 'dp', [(i, i ^ 1) for i in range(ranks)])]
    ppermute x3, starting transfers between devices: 12 us -> 8.74 us  [mirror(): return lax.ppermute(value, 'dp', [(i, ranks - 1 - i) for i in range(ranks)])]
    ppermute x3, waiting for transfers between devices: 3.51 us -> 0.47 us  [mirror(): return lax.ppermute(value, 'dp', [(i, ranks - 1 - i) for i in range(ranks)])]
    all_to_all x1, waiting for transfers between devices: 4.27 us -> 1.48 us  [shards(): lax.all_to_all(back, 'expert', split_axis=0, concat_axis=0, tiled=True)]
where the time goes in v9:
time: 129 us; the launch traced here: 128 us
  blocking collectives  70.7 us (55%)
  starting transfers between devices  24.3 us (19%)
  waiting for transfers between devices  17.3 us (13%)
  Pallas kernels  14.5 us (11%)
    all_to_all x1, blocking collectives, shards(): lax.all_to_all(send, 'expert', split_axis=0, concat_axis=0, tiled=True)  70.7 us
    ppermute x3, waiting for transfers between devices, even(): return lax.ppermute(value, 'dp', [(i, i ^ 1) for i in range(ranks)])  15.4 us
    ppermute x3, starting transfers between devices, mirror(): return lax.ppermute(value, 'dp', [(i, ranks - 1 - i) for i in range(ranks)])  8.74 us
    all_to_all x1, starting transfers between devices, shards(): lax.all_to_all(back, 'expert', split_axis=0, concat_axis=0, tiled=True)  8.3 us
    ppermute x3, starting transfers between devices, even(): return lax.ppermute(value, 'dp', [(i, i ^ 1) for i in range(ranks)])  7.26 us
    pallas_call x1, Pallas kernels, shards(): call(functools.partial(expert_body, ranks), 'expert', out, [SMEM, VMEM] +...  7.23 us
    pallas_call x5, Pallas kernels, small(): call(body, name, out, [VMEM] * len(operands), flops=work, bytes_accessed=...  3.36 us
    pallas_call x1, Pallas kernels, shards(): call(functools.partial(dispatch_body, experts), 'dispatch', [jax.ShapeDty...  2.96 us
  transfers between devices with their start and end apart: 7, of which 5 were waited for; matrix products, arithmetic and copies ran while one was open for 0% of the time, Pallas kernels for 3%

profile of v9, /device:TPU:1, one launch (start us, length us, event | category | flops | bytes accessed | tf_op | source)
XLA Modules:
  0.0 127.6 jit_solution(17731371307157687189)
XLA Ops:
  0.6 3.0 %dispatch.1 = (bf16[1024,1024]{1,0:T(8,128)(2,1)}, bf16[64,1024]{1,0:T(8,128)(2,1)}) custom-call(bf16[32,1024]{1,0:T(8,128)(2,1)} %tok_hbm.1, bf16[32,1024]{1,0:T(8,128)(2,1)} %cot_hbm.1, s32[8,32]{1,0:T(8,128)} %bitcast.22, bf16[8,32]{1,0:T(8,128)(2,1)} %bitcast.23, s32[4]{0:T(128)} %hot_hbm, s32[4]{0:T(128)} %extra_hbm.1), custom_call_target="tpu_custom_call" | custom-call | flops 134217728 | bytes 2097152 | tf_op jit(solution)/shard_map/dispatch/pallas_call | solution.py:251
  3.6 0.0 copy-start.1
  3.6 0.0 copy-start.2
  3.6 0.0 copy-start.3
  3.6 70.7 %all_to_all.22 = bf16[128,8,1024]{2,1,0:T(8,128)(2,1)S(1)} all-to-all(bf16[128,8,1024]{2,1,0:T(8,128)(2,1)} %bitcast.18), channel_id=1, replica_groups=mesh['dp'=4,'expert'=128] {'expert'}, dimensions={0} | all-to-all | bytes 4194304 | tf_op jit(solution)/shard_map/all_to_all | solution.py:275
  74.4 7.2 %expert.1 = (bf16[1024,512]{1,0:T(8,128)(2,1)}, bf16[128,1024]{1,0:T(8,128)(2,1)S(1)}, bf16[256,1024]{1,0:T(8,128)(2,1)}, bf16[256,1536]{1,0:T(8,128)(2,1)S(1)}, bf16[256,1536]{1,0:T(8,128)(2,1)S(1)}) custom-call(s32[1]{0:T(128)} %bitcast.2.me, bf16[1024,1024]{1,0:T(8,128)(2,1)S(1)} %bitcast.14, bf16[1024,384]{1,0:T(8,128)(2,1)S(1)} %bitcast.15, ...), custom_call_target="tpu_custom_call" | custom-call | flops 3221225472 | bytes 8912896 | tf_op jit(solution)/shard_map/expert/pallas_call | solution.py:282
  81.6 4.4 %collective-permute-start.2 = (bf16[256,1024]{1,0:T(8,128)(2,1)}, bf16[256,1024]{1,0:T(8,128)(2,1)}, u32[]{:S(2)}, u32[]{:S(2)}) collective-permute-start(bf16[256,1024]{1,0:T(8,128)(2,1)} %get-tuple-element.26.kept), channel_id=1, source_target_pairs={{0,384},{128,256},{256,128},{384,0},{1,385},{129,257},{257,129},{3... | collective-permute-start | bytes 1572872 | tf_op jit(solution)/shard_map/ppermute | solution.py:314
  86.0 1.9 %collective-permute-start = (bf16[256,1536]{1,0:T(8,128)(2,1)S(1)}, bf16[256,1536]{1,0:T(8,128)(2,1)S(1)}, u32[]{:S(2)}, u32[]{:S(2)}) collective-permute-start(bf16[256,1536]{1,0:T(8,128)(2,1)S(1)} %get-tuple-element.22), channel_id=1, source_target_pairs={{0,128},{128,0},{256,384},{384,256},{1,129},{129,1},{257,385},{385... | collective-permute-start | bytes 2359304 | tf_op jit(solution)/shard_map/ppermute | solution.py:311
  87.9 8.3 %all-to-all-start.1 = ((bf16[128,8,512]{2,1,0:T(8,128)(2,1)}), bf16[128,8,512]{2,1,0:T(8,128)(2,1)S(1)}, u32[]{:S(2)}, u32[]{:S(2)}) async-start(bf16[128,8,512]{2,1,0:T(8,128)(2,1)} %bitcast.8), calls=%async_computation.1 | async-start | bytes 2097152 | tf_op jit(solution)/shard_map/all_to_all | solution.py:308
  96.2 3.4 %collective-permute-start.3 = (bf16[128,1024]{1,0:T(8,128)(2,1)}, bf16[128,1024]{1,0:T(8,128)(2,1)S(1)}, u32[]{:S(2)}, u32[]{:S(2)}) collective-permute-start(bf16[128,1024]{1,0:T(8,128)(2,1)} %copy-done.4), channel_id=1, source_target_pairs={{0,128},{128,0},{256,384},{384,256},{1,129},{129,1},{257,385},{385... | collective-permute-start | bytes 786440 | tf_op jit(solution)/shard_map/ppermute | solution.py:311
  99.7 1.3 %down_b.1.sum_b = bf16[256,1024]{1,0:T(8,128)(2,1)S(1)} custom-call(bf16[256,1024]{1,0:T(8,128)(2,1)} %get-tuple-element.26.kept, bf16[256,1024]{1,0:T(8,128)(2,1)} %collective-permute-done.2.received), custom_call_target="tpu_custom_call" | custom-call | flops 5000000000 | bytes 1572864 | tf_op jit(solution)/shard_map/down_b/pallas_call | solution.py:318
  101.0 1.9 %collective-permute-start.5 = (bf16[256,1024]{1,0:T(8,128)(2,1)S(1)}, bf16[256,1024]{1,0:T(8,128)(2,1)S(1)}, u32[]{:S(2)}, u32[]{:S(2)}) collective-permute-start(bf16[256,1024]{1,0:T(8,128)(2,1)S(1)} %down_b.1.sum_b), channel_id=1, source_target_pairs={{0,128},{128,0},{256,384},{384,256},{1,129},{129,1},{257,385},{385... | collective-permute-start | bytes 1572872 | tf_op jit(solution)/shard_map/ppermute | solution.py:311
  102.9 3.1 %collective-permute-done.received.first = bf16[256,1536]{1,0:T(8,128)(2,1)S(1)} collective-permute-done((bf16[256,1536]{1,0:T(8,128)(2,1)S(1)}, bf16[256,1536]{1,0:T(8,128)(2,1)S(1)}, u32[]{:S(2)}, u32[]{:S(2)}) %collective-permute-start) | collective-permute-done | bytes 786464 | tf_op jit(solution)/shard_map/ppermute | solution.py:311
  106.0 0.1 pair_sum.1
  106.1 2.1 %collective-permute-start.1 = (bf16[256,768]{1,0:T(8,128)(2,1)S(1)}, bf16[256,768]{1,0:T(8,128)(2,1)S(1)}, u32[]{:S(2)}, u32[]{:S(2)}) collective-permute-start(bf16[256,768]{1,0:T(8,128)(2,1)S(1)} %pair_sum.1), channel_id=1, source_target_pairs={{0,384},{128,256},{256,128},{384,0},{1,385},{129,257},{257,129},{3... | collective-permute-start | bytes 1179656 | tf_op jit(solution)/shard_map/ppermute | solution.py:314
  108.2 3.4 %collective-permute-done.3.received = bf16[128,1024]{1,0:T(8,128)(2,1)S(1)} collective-permute-done((bf16[128,1024]{1,0:T(8,128)(2,1)}, bf16[128,1024]{1,0:T(8,128)(2,1)S(1)}, u32[]{:S(2)}, u32[]{:S(2)}) %collective-permute-start.3) | collective-permute-done | bytes 262176 | tf_op jit(solution)/shard_map/ppermute | solution.py:311
  111.6 0.1 down_a.1.sum_a
  111.7 2.2 %collective-permute-start.4 = (bf16[128,1024]{1,0:T(8,128)(2,1)S(1)}, bf16[128,1024]{1,0:T(8,128)(2,1)S(1)}, u32[]{:S(2)}, u32[]{:S(2)}) collective-permute-start(bf16[128,1024]{1,0:T(8,128)(2,1)S(1)} %down_a.1.sum_a), channel_id=1, source_target_pairs={{0,384},{128,256},{256,128},{384,0},{1,385},{129,257},{257,129},{3... | collective-permute-start | bytes 786440 | tf_op jit(solution)/shard_map/ppermute | solution.py:314
  113.9 8.9 %collective-permute-done.5.next_b = bf16[256,1024]{1,0:T(8,128)(2,1)S(1)} collective-permute-done((bf16[256,1024]{1,0:T(8,128)(2,1)S(1)}, bf16[256,1024]{1,0:T(8,128)(2,1)S(1)}, u32[]{:S(2)}, u32[]{:S(2)}) %collective-permute-start.5) | collective-permute-done | bytes 524320 | tf_op jit(solution)/shard_map/ppermute | solution.py:311
  122.8 0.5 collective-permute-done.4.next_a
  123.3 1.1 down.1
  124.4 0.8 pair.1
  125.2 1.5 %all-to-all-done.1 = bf16[128,8,512]{2,1,0:T(8,128)(2,1)S(1)} async-done(((bf16[128,8,512]{2,1,0:T(8,128)(2,1)}), bf16[128,8,512]{2,1,0:T(8,128)(2,1)S(1)}, u32[]{:S(2)}, u32[]{:S(2)}) %all-to-all-start.1) | async-done | bytes 1048608 | tf_op jit(solution)/shard_map/all_to_all | solution.py:308
  126.7 0.9 token_grad.1
  (11 shorter events, 0.0 us)
Async XLA Ops:
  3.6 70.7 %copy-start.1 = (bf16[1,1024,384]{2,1,0:T(8,128)(2,1)S(1)}, bf16[1,1024,384]{2,1,0:T(8,128)(2,1)}, u32[]{:S(2)}) copy-start(bf16[1,1024,384]{2,1,0:T(8,128)(2,1)} %param.15) | copy-start | bytes 2359300
  3.6 70.7 %copy-start.2 = (bf16[1,1024,384]{2,1,0:T(8,128)(2,1)S(1)}, bf16[1,1024,384]{2,1,0:T(8,128)(2,1)}, u32[]{:S(2)}) copy-start(bf16[1,1024,384]{2,1,0:T(8,128)(2,1)} %param.16) | copy-start | bytes 2359300
  3.6 70.7 %copy-start.3 = (bf16[1,384,1024]{2,1,0:T(8,128)(2,1)S(1)}, bf16[1,384,1024]{2,1,0:T(8,128)(2,1)}, u32[]{:S(2)}) copy-start(bf16[1,384,1024]{2,1,0:T(8,128)(2,1)} %param.17) | copy-start | bytes 2359300
  81.6 6.3 %copy-start.4 = (bf16[128,1024]{1,0:T(8,128)(2,1)}, bf16[128,1024]{1,0:T(8,128)(2,1)S(1)}, u32[]{:S(2)}) copy-start(bf16[128,1024]{1,0:T(8,128)(2,1)S(1)} %get-tuple-element.27.kept) | copy-start | bytes 786436
  81.6 18.1 %collective-permute-start.2 = (bf16[256,1024]{1,0:T(8,128)(2,1)}, bf16[256,1024]{1,0:T(8,128)(2,1)}, u32[]{:S(2)}, u32[]{:S(2)}) collective-permute-start(bf16[256,1024]{1,0:T(8,128)(2,1)} %get-tuple-element.26.kept), channel_id=1, source_target_pairs={{0,384},{128,256},{256,128},{384,0},{1,385},{129,257},{257,129},{3... | collective-permute-start | bytes 1572872 | tf_op jit(solution)/shard_map/ppermute | solution.py:314
  86.0 20.0 %collective-permute-start = (bf16[256,1536]{1,0:T(8,128)(2,1)S(1)}, bf16[256,1536]{1,0:T(8,128)(2,1)S(1)}, u32[]{:S(2)}, u32[]{:S(2)}) collective-permute-start(bf16[256,1536]{1,0:T(8,128)(2,1)S(1)} %get-tuple-element.22), channel_id=1, source_target_pairs={{0,128},{128,0},{256,384},{384,256},{1,129},{129,1},{257,385},{385... | collective-permute-start | bytes 2359304 | tf_op jit(solution)/shard_map/ppermute | solution.py:311
  87.9 38.7 %all-to-all-start.1 = ((bf16[128,8,512]{2,1,0:T(8,128)(2,1)}), bf16[128,8,512]{2,1,0:T(8,128)(2,1)S(1)}, u32[]{:S(2)}, u32[]{:S(2)}) async-start(bf16[128,8,512]{2,1,0:T(8,128)(2,1)} %bitcast.8), calls=%async_computation.1 | async-start | bytes 2097152 | tf_op jit(solution)/shard_map/all_to_all | solution.py:308
  96.2 15.4 %collective-permute-start.3 = (bf16[128,1024]{1,0:T(8,128)(2,1)}, bf16[128,1024]{1,0:T(8,128)(2,1)S(1)}, u32[]{:S(2)}, u32[]{:S(2)}) collective-permute-start(bf16[128,1024]{1,0:T(8,128)(2,1)} %copy-done.4), channel_id=1, source_target_pairs={{0,128},{128,0},{256,384},{384,256},{1,129},{129,1},{257,385},{385... | collective-permute-start | bytes 786440 | tf_op jit(solution)/shard_map/ppermute | solution.py:311
  101.0 21.8 %collective-permute-start.5 = (bf16[256,1024]{1,0:T(8,128)(2,1)S(1)}, bf16[256,1024]{1,0:T(8,128)(2,1)S(1)}, u32[]{:S(2)}, u32[]{:S(2)}) collective-permute-start(bf16[256,1024]{1,0:T(8,128)(2,1)S(1)} %down_b.1.sum_b), channel_id=1, source_target_pairs={{0,128},{128,0},{256,384},{384,256},{1,129},{129,1},{257,385},{385... | collective-permute-start | bytes 1572872 | tf_op jit(solution)/shard_map/ppermute | solution.py:311
  106.0 5.6 %copy-start.5 = (bf16[128,1024]{1,0:T(8,128)(2,1)S(1)}, bf16[128,1024]{1,0:T(8,128)(2,1)}, u32[]{:S(2)}) copy-start(bf16[128,1024]{1,0:T(8,128)(2,1)} %copy-done.4) | copy-start | bytes 786436
  106.1 18.3 %collective-permute-start.1 = (bf16[256,768]{1,0:T(8,128)(2,1)S(1)}, bf16[256,768]{1,0:T(8,128)(2,1)S(1)}, u32[]{:S(2)}, u32[]{:S(2)}) collective-permute-start(bf16[256,768]{1,0:T(8,128)(2,1)S(1)} %pair_sum.1), channel_id=1, source_target_pairs={{0,384},{128,256},{256,128},{384,0},{1,385},{129,257},{257,129},{3... | collective-permute-start | bytes 1179656 | tf_op jit(solution)/shard_map/ppermute | solution.py:314
  111.7 15.0 %copy-start = (bf16[64,1024]{1,0:T(8,128)(2,1)S(1)}, bf16[64,1024]{1,0:T(8,128)(2,1)}, u32[]{:S(2)}) copy-start(bf16[64,1024]{1,0:T(8,128)(2,1)} %get-tuple-element.17.pick_t) | copy-start | bytes 393220
  111.7 11.6 %collective-permute-start.4 = (bf16[128,1024]{1,0:T(8,128)(2,1)S(1)}, bf16[128,1024]{1,0:T(8,128)(2,1)S(1)}, u32[]{:S(2)}, u32[]{:S(2)}) collective-permute-start(bf16[128,1024]{1,0:T(8,128)(2,1)S(1)} %down_a.1.sum_a), channel_id=1, source_target_pairs={{0,384},{128,256},{256,128},{384,0},{1,385},{129,257},{257,129},{3... | collective-permute-start | bytes 786440 | tf_op jit(solution)/shard_map/ppermute | solution.py:314

commit v10 on v8

--- a/solution.py
+++ b/solution.py
@@ -13,6 +13,7 @@
 LANES = 128
 CHUNKS = 4
 EARLY = 3 * 10**10
+
 F32 = jnp.float32
 BF16 = jnp.bfloat16
 VMEM = pl.BlockSpec(memory_space=pltpu.VMEM)
@@ -20,15 +21,12 @@
 SMEM = pl.BlockSpec(memory_space=pltpu.SMEM)
 MIB = 1024 * 1024
 
-
 NN = (((1,), (0,)), ((), ()))
 NT = (((1,), (1,)), ((), ()))
 TN = (((0,), (0,)), ((), ()))
 
-
 def dot(a, b, dims):
     return lax.dot_general(a, b, dims, preferred_element_type=F32)
-
 
 def call(
     body, name, out_shape, in_specs, scratch=(), flops=0, bytes_accessed=0, vmem=16 * MIB, out=VMEM
@@ -46,11 +44,9 @@
         ),
     )
 
-
 def identity(n):
     rows = lax.broadcasted_iota(jnp.int32, (n, n), 0)
     return jnp.where(rows == lax.broadcasted_iota(jnp.int32, (n, n), 1), 1.0, 0.0).astype(BF16)
-
 
 def dispatch_body(
     experts, tok_hbm, cot_hbm, routes_hbm, combine_hbm, hot_hbm, extra_hbm,
@@ -117,28 +113,24 @@
     departures += start_all([pltpu.make_async_copy(pick_t, pick_hbm, out_sems.at[CHUNKS])])
     wait_all(departures)
 
-
 def token_body(pick_t, returned, out):
     count, half = out.shape[0], returned.shape[1]
     both = dot(pick_t[...], returned[...], NN)
     out[:, :half] = both[:count].astype(BF16)
     out[:, half:] = both[count:].astype(BF16)
 
-
 def start_all(copies):
     for copy in copies:
         copy.start()
     return copies
 
-
 def wait_all(copies):
     for copy in copies:
         copy.wait()
 
-
 def expert_body(
     ranks, me, recv_hbm, w_gate_hbm, w_up_hbm, w_down_hbm,
-    back_hbm, down_a_hbm, down_b_hbm, send_hbm, keep_hbm, back, down_a, down_b, send, keep,
+    back_hbm, down_out_hbm, send_hbm, keep_hbm, back, down_out, send, keep,
     recv, w_in, w_down, wide, narrow, tok, og, pre, grad, in_rows, hid, total, in_sems, out_sems,
 ):
     rows_in, features = recv.shape
@@ -217,36 +209,22 @@
     keep[:, : 2 * hidden] = part_of(ranks - 1 - me[0])
     keep[:, 2 * hidden :] = part_of(me[0])
     send_out(keep, keep_hbm)
-    down = dot(hid[...], og[...], TN).astype(BF16)
-    cut = down_a.shape[0]
-    down_a[...] = down[:cut]
-    send_out(down_a, down_a_hbm)
-    down_b[...] = down[cut:]
-    send_out(down_b, down_b_hbm)
+    down_out[...] = dot(hid[...], og[...], TN).astype(BF16)
+    send_out(down_out, down_out_hbm)
     wait_all(departures)
-
 
 def add(kept, received):
     return kept.astype(F32) + received.astype(F32)
-
 
 def sum_body(kept, received, out):
     width = out.shape[1]
     out[...] = add(kept[:, :width], received[:, :width]).astype(BF16)
-
-
-def down_body(sum_a, next_a, sum_b, next_b, out):
-    cut = sum_a.shape[0]
-    out[:cut, :] = add(sum_a[...], next_a[...]).astype(BF16)
-    out[cut:, :] = add(sum_b[...], next_b[...]).astype(BF16)
-
 
 def pair_body(keep, first, second, grad_gate, grad_up):
     hidden = grad_gate.shape[1]
     own = add(keep[:, 2 * hidden :], first[:, 2 * hidden :]) + second[...].astype(F32)
     grad_gate[...] = own[:, :hidden].astype(BF16)
     grad_up[...] = own[:, hidden:].astype(BF16)
-
 
 def shards(tokens, cotangent, routes, combine, hot_experts, extra_slots, w_gate, w_up, w_down):
     experts = lax.axis_size("expert")
@@ -283,12 +261,11 @@
     )(tokens, cotangent, routes.T, combine.T, hot_experts, extra_slots)
     recv = lax.all_to_all(send, "expert", split_axis=0, concat_axis=0, tiled=True)
     piece = features // ranks
-    cut = hidden // 3
     shape = jax.ShapeDtypeStruct
     out = [shape((total, features // 2), BF16)]
-    parts = [shape((cut, features), BF16), shape((hidden - cut, features), BF16)]
-    out += parts + [shape((piece, 4 * hidden), BF16)] * 2
-    back, down_a, down_b, send, keep = call(
+    whole_down = shape((hidden, features), BF16)
+    out += [whole_down] + [shape((piece, 4 * hidden), BF16)] * 2
+    back, down, send, keep = call(
         functools.partial(expert_body, ranks),
         "expert",
         out,
@@ -331,19 +308,13 @@
 
     one_piece = shape((piece, hidden), BF16)
     first = even(send)
-    first_b = mirror(down_b)
-    first_a = even(down_a)
+    first_down = mirror(down)
     both_pieces = shape((piece, 2 * hidden), BF16)
-    sum_b = small(sum_body, "down_b", parts[1], down_b, first_b)
-    next_b = even(sum_b)
+    sum_down = small(sum_body, "down_sum", whole_down, down, first_down)
+    next_down = even(sum_down)
     pair_sum = small(sum_body, "pair_sum", both_pieces, keep, first, work=EARLY)
     second = mirror(pair_sum)
-    kept_a, _, _ = lax.optimization_barrier((down_a, sum_b, pair_sum))
-    sum_a = small(sum_body, "down_a", parts[0], kept_a, first_a)
-    next_a = mirror(sum_a)
-    grad_down = small(
-        down_body, "down", shape((hidden, features), BF16), sum_a, next_a, sum_b, next_b
-    )
+    grad_down = small(sum_body, "down", whole_down, sum_down, next_down)
     grad_gate, grad_up = small(pair_body, "pair", [one_piece, one_piece], keep, first, second)
     token_grads = call(
         token_body,
@@ -356,7 +327,6 @@
     )(pick_t, returned)
     return token_grads, grad_gate[None], grad_up[None], grad_down[None]
 
-
 def solution(mesh):
     in_specs = (
         P(("dp", "expert"), None),

time: 128 us -> 127 us (level)
  starting transfers between devices: 27.6 us -> 21 us
  waiting for transfers between devices: 14.8 us -> 20.7 us
    ppermute x3 -> x2, waiting for transfers between devices: 3.51 us -> 14.5 us  [mirror(): return lax.ppermute(value, 'dp', [(i, ranks - 1 - i) for i in range(ranks)])]
    ppermute x3 -> x2, starting transfers between devices: 7.26 us -> 3.84 us  [even(): return lax.ppermute(value, 'dp', [(i, i ^ 1) for i in range(ranks)])]
    ppermute x3 -> x2, starting transfers between devices: 12 us -> 8.9 us  [mirror(): return lax.ppermute(value, 'dp', [(i, ranks - 1 - i) for i in range(ranks)])]
    all_to_all x1, waiting for transfers between devices: 4.27 us -> 1.67 us  [shards(): lax.all_to_all(back, 'expert', split_axis=0, concat_axis=0, tiled=True)]
    ppermute x3 -> x2, waiting for transfers between devices: 7.02 us -> 4.49 us  [even(): return lax.ppermute(value, 'dp', [(i, i ^ 1) for i in range(ranks)])]
    pallas_call x5 -> x4, Pallas kernels: 3.2 us -> 3.29 us  [small(): call(body, name, out, [VMEM] * len(operands), flops=work, bytes_accessed=...]
  transfers between devices with their start and end apart: 7 -> 5, of which waited for: 5 -> 4; matrix products, arithmetic and copies ran while one was open for 0% -> 0% of each run, Pallas kernels for 3% -> 3%
where the time goes in v10:
time: 127 us
  blocking collectives  70.7 us (56%)
  starting transfers between devices  21 us (17%)
  waiting for transfers between devices  20.7 us (16%)
  Pallas kernels  13.6 us (11%)
    all_to_all x1, blocking collectives, shards(): lax.all_to_all(send, 'expert', split_axis=0, concat_axis=0, tiled=True)  70.7 us
    ppermute x2, waiting for transfers between devices, mirror(): return lax.ppermute(value, 'dp', [(i, ranks - 1 - i) for i in range(ranks)])  14.5 us
    ppermute x2, starting transfers between devices, mirror(): return lax.ppermute(value, 'dp', [(i, ranks - 1 - i) for i in range(ranks)])  8.9 us
    all_to_all x1, starting transfers between devices, shards(): lax.all_to_all(back, 'expert', split_axis=0, concat_axis=0, tiled=True)  8.3 us
    pallas_call x1, Pallas kernels, shards(): call(functools.partial(expert_body, ranks), 'expert', out, [SMEM] + [ANY]...  6.39 us
    ppermute x2, waiting for transfers between devices, even(): return lax.ppermute(value, 'dp', [(i, i ^ 1) for i in range(ranks)])  4.49 us
    ppermute x2, starting transfers between devices, even(): return lax.ppermute(value, 'dp', [(i, i ^ 1) for i in range(ranks)])  3.84 us
    pallas_call x4, Pallas kernels, small(): call(body, name, out, [VMEM] * len(operands), flops=work, bytes_accessed=...  3.29 us
  transfers between devices with their start and end apart: 5, of which 4 were waited for; matrix products, arithmetic and copies ran while one was open for 0% of the time, Pallas kernels for 3%

profile of v10, /device:TPU:1, one launch (start us, length us, event | category | flops | bytes accessed | tf_op | source)
XLA Modules:
  0.0 126.8 jit_solution(17720322644490459844)
XLA Ops:
  0.6 3.0 %dispatch.1 = (bf16[1024,1024]{1,0:T(8,128)(2,1)}, bf16[64,1024]{1,0:T(8,128)(2,1)}) custom-call(bf16[32,1024]{1,0:T(8,128)(2,1)} %tok_hbm.1, bf16[32,1024]{1,0:T(8,128)(2,1)} %cot_hbm.1, s32[8,32]{1,0:T(8,128)} %bitcast.22, bf16[8,32]{1,0:T(8,128)(2,1)} %bitcast.23, s32[4]{0:T(128)} %hot_hbm, s32[4]{0:T(128)} %extra_hbm.1), custom_call_target="tpu_custom_call" | custom-call | flops 134217728 | bytes 2097152 | tf_op jit(solution)/shard_map/dispatch/pallas_call | solution.py:238
  3.6 0.0 copy-start.1
  3.6 0.0 copy-start.2
  3.6 0.0 copy-start.3
  3.6 70.7 %all_to_all.22 = bf16[128,8,1024]{2,1,0:T(8,128)(2,1)S(1)} all-to-all(bf16[128,8,1024]{2,1,0:T(8,128)(2,1)} %bitcast.18), channel_id=1, replica_groups=mesh['dp'=4,'expert'=128] {'expert'}, dimensions={0} | all-to-all | bytes 4194304 | tf_op jit(solution)/shard_map/all_to_all | solution.py:262
  74.3 0.0 copy-done.1
  74.4 0.0 copy-done.3
  74.4 6.4 %expert.1 = (bf16[1024,512]{1,0:T(8,128)(2,1)}, bf16[384,1024]{1,0:T(8,128)(2,1)S(1)}, bf16[256,1536]{1,0:T(8,128)(2,1)}, bf16[256,1536]{1,0:T(8,128)(2,1)S(1)}) custom-call(s32[1]{0:T(128)} %bitcast.2.me, bf16[1024,1024]{1,0:T(8,128)(2,1)S(1)} %bitcast.14, bf16[1024,384]{1,0:T(8,128)(2,1)S(1)} %bitcast.15, bf16[1024,384]{1,0:T(8,128)(2,1)S(1)} %bitcast.16, ...), custom_call_target="tpu_custom_call" | custom-call | flops 3221225472 | bytes 8912896 | tf_op jit(solution)/shard_map/expert/pallas_call | solution.py:268
  80.8 4.4 %collective-permute-start.2 = (bf16[384,1024]{1,0:T(8,128)(2,1)S(1)}, bf16[384,1024]{1,0:T(8,128)(2,1)}, u32[]{:S(2)}, u32[]{:S(2)}) collective-permute-start(bf16[384,1024]{1,0:T(8,128)(2,1)S(1)} %get-tuple-element.23.kept), channel_id=1, source_target_pairs={{0,384},{128,256},{256,128},{384,0},{1,385},{129,257},{257,129},{3... | collective-permute-start | bytes 2359304 | tf_op jit(solution)/shard_map/ppermute | solution.py:301
  85.1 1.9 %collective-permute-start = (bf16[256,1536]{1,0:T(8,128)(2,1)}, bf16[256,1536]{1,0:T(8,128)(2,1)S(1)}, u32[]{:S(2)}, u32[]{:S(2)}) collective-permute-start(bf16[256,1536]{1,0:T(8,128)(2,1)} %get-tuple-element.20), channel_id=1, source_target_pairs={{0,128},{128,0},{256,384},{384,256},{1,129},{129,1},{257,385},{385... | collective-permute-start | bytes 2359304 | tf_op jit(solution)/shard_map/ppermute | solution.py:298
  87.1 8.3 %all-to-all-start.1 = ((bf16[128,8,512]{2,1,0:T(8,128)(2,1)}), bf16[128,8,512]{2,1,0:T(8,128)(2,1)S(1)}, u32[]{:S(2)}, u32[]{:S(2)}) async-start(bf16[128,8,512]{2,1,0:T(8,128)(2,1)} %bitcast.8), calls=%async_computation.1 | async-start | bytes 2097152 | tf_op jit(solution)/shard_map/all_to_all | solution.py:295
  95.4 7.0 %collective-permute-done.2.received = bf16[384,1024]{1,0:T(8,128)(2,1)} collective-permute-done((bf16[384,1024]{1,0:T(8,128)(2,1)S(1)}, bf16[384,1024]{1,0:T(8,128)(2,1)}, u32[]{:S(2)}, u32[]{:S(2)}) %collective-permute-start.2) | collective-permute-done | bytes 786464 | tf_op jit(solution)/shard_map/ppermute | solution.py:301
  102.4 1.3 %down_sum.1.kept = bf16[384,1024]{1,0:T(8,128)(2,1)S(1)} custom-call(bf16[384,1024]{1,0:T(8,128)(2,1)S(1)} %get-tuple-element.23.kept, bf16[384,1024]{1,0:T(8,128)(2,1)} %collective-permute-done.2.received), custom_call_target="tpu_custom_call" | custom-call | bytes 2359296 | tf_op jit(solution)/shard_map/down_sum/pallas_call | solution.py:305
  103.7 1.9 %collective-permute-start.3 = (bf16[384,1024]{1,0:T(8,128)(2,1)S(1)}, bf16[384,1024]{1,0:T(8,128)(2,1)S(1)}, u32[]{:S(2)}, u32[]{:S(2)}) collective-permute-start(bf16[384,1024]{1,0:T(8,128)(2,1)S(1)} %down_sum.1.kept), channel_id=1, source_target_pairs={{0,128},{128,0},{256,384},{384,256},{1,129},{129,1},{257,385},{385... | collective-permute-start | bytes 2359304 | tf_op jit(solution)/shard_map/ppermute | solution.py:298
  105.6 0.0 collective-permute-done.received.first
  105.6 0.1 pair_sum.1
  105.7 0.0 copy-start
  105.8 4.5 %collective-permute-start.1 = (bf16[256,768]{1,0:T(8,128)(2,1)S(1)}, bf16[256,768]{1,0:T(8,128)(2,1)S(1)}, u32[]{:S(2)}, u32[]{:S(2)}) collective-permute-start(bf16[256,768]{1,0:T(8,128)(2,1)S(1)} %pair_sum.1), channel_id=1, source_target_pairs={{0,384},{128,256},{256,128},{384,0},{1,385},{129,257},{257,129},{3... | collective-permute-start | bytes 1179656 | tf_op jit(solution)/shard_map/ppermute | solution.py:301
  110.3 7.5 %collective-permute-done.1.second = bf16[256,768]{1,0:T(8,128)(2,1)S(1)} collective-permute-done((bf16[256,768]{1,0:T(8,128)(2,1)S(1)}, bf16[256,768]{1,0:T(8,128)(2,1)S(1)}, u32[]{:S(2)}, u32[]{:S(2)}) %collective-permute-start.1) | collective-permute-done | bytes 393248 | tf_op jit(solution)/shard_map/ppermute | solution.py:301
  117.8 0.8 pair.1
  118.6 4.5 %collective-permute-done.3.received = bf16[384,1024]{1,0:T(8,128)(2,1)S(1)} collective-permute-done((bf16[384,1024]{1,0:T(8,128)(2,1)S(1)}, bf16[384,1024]{1,0:T(8,128)(2,1)S(1)}, u32[]{:S(2)}, u32[]{:S(2)}) %collective-permute-start.3) | collective-permute-done | bytes 786464 | tf_op jit(solution)/shard_map/ppermute | solution.py:298
  123.1 1.1 down.1
  124.2 1.7 %all-to-all-done.1 = bf16[128,8,512]{2,1,0:T(8,128)(2,1)S(1)} async-done(((bf16[128,8,512]{2,1,0:T(8,128)(2,1)}), bf16[128,8,512]{2,1,0:T(8,128)(2,1)S(1)}, u32[]{:S(2)}, u32[]{:S(2)}) %all-to-all-start.1) | async-done | bytes 1048608 | tf_op jit(solution)/shard_map/all_to_all | solution.py:295
  125.8 0.9 token_grad.1
  (2 shorter events, 0.0 us)
Async XLA Ops:
  3.6 70.7 %copy-start.1 = (bf16[1,1024,384]{2,1,0:T(8,128)(2,1)S(1)}, bf16[1,1024,384]{2,1,0:T(8,128)(2,1)}, u32[]{:S(2)}) copy-start(bf16[1,1024,384]{2,1,0:T(8,128)(2,1)} %param.15) | copy-start | bytes 2359300
  3.6 70.7 %copy-start.2 = (bf16[1,1024,384]{2,1,0:T(8,128)(2,1)S(1)}, bf16[1,1024,384]{2,1,0:T(8,128)(2,1)}, u32[]{:S(2)}) copy-start(bf16[1,1024,384]{2,1,0:T(8,128)(2,1)} %param.16) | copy-start | bytes 2359300
  3.6 70.7 %copy-start.3 = (bf16[1,384,1024]{2,1,0:T(8,128)(2,1)S(1)}, bf16[1,384,1024]{2,1,0:T(8,128)(2,1)}, u32[]{:S(2)}) copy-start(bf16[1,384,1024]{2,1,0:T(8,128)(2,1)} %param.17) | copy-start | bytes 2359300
  80.8 21.6 %collective-permute-start.2 = (bf16[384,1024]{1,0:T(8,128)(2,1)S(1)}, bf16[384,1024]{1,0:T(8,128)(2,1)}, u32[]{:S(2)}, u32[]{:S(2)}) collective-permute-start(bf16[384,1024]{1,0:T(8,128)(2,1)S(1)} %get-tuple-element.23.kept), channel_id=1, source_target_pairs={{0,384},{128,256},{256,128},{384,0},{1,385},{129,257},{257,129},{3... | collective-permute-start | bytes 2359304 | tf_op jit(solution)/shard_map/ppermute | solution.py:301
  85.1 20.5 %collective-permute-start = (bf16[256,1536]{1,0:T(8,128)(2,1)}, bf16[256,1536]{1,0:T(8,128)(2,1)S(1)}, u32[]{:S(2)}, u32[]{:S(2)}) collective-permute-start(bf16[256,1536]{1,0:T(8,128)(2,1)} %get-tuple-element.20), channel_id=1, source_target_pairs={{0,128},{128,0},{256,384},{384,256},{1,129},{129,1},{257,385},{385... | collective-permute-start | bytes 2359304 | tf_op jit(solution)/shard_map/ppermute | solution.py:298
  87.1 38.7 %all-to-all-start.1 = ((bf16[128,8,512]{2,1,0:T(8,128)(2,1)}), bf16[128,8,512]{2,1,0:T(8,128)(2,1)S(1)}, u32[]{:S(2)}, u32[]{:S(2)}) async-start(bf16[128,8,512]{2,1,0:T(8,128)(2,1)} %bitcast.8), calls=%async_computation.1 | async-start | bytes 2097152 | tf_op jit(solution)/shard_map/all_to_all | solution.py:295
  103.7 19.4 %collective-permute-start.3 = (bf16[384,1024]{1,0:T(8,128)(2,1)S(1)}, bf16[384,1024]{1,0:T(8,128)(2,1)S(1)}, u32[]{:S(2)}, u32[]{:S(2)}) collective-permute-start(bf16[384,1024]{1,0:T(8,128)(2,1)S(1)} %down_sum.1.kept), channel_id=1, source_target_pairs={{0,128},{128,0},{256,384},{384,256},{1,129},{129,1},{257,385},{385... | collective-permute-start | bytes 2359304 | tf_op jit(solution)/shard_map/ppermute | solution.py:298
  105.7 20.1 %copy-start = (bf16[64,1024]{1,0:T(8,128)(2,1)S(1)}, bf16[64,1024]{1,0:T(8,128)(2,1)}, u32[]{:S(2)}) copy-start(bf16[64,1024]{1,0:T(8,128)(2,1)} %get-tuple-element.15.pick_t) | copy-start | bytes 393220
  105.8 12.0 %collective-permute-start.1 = (bf16[256,768]{1,0:T(8,128)(2,1)S(1)}, bf16[256,768]{1,0:T(8,128)(2,1)S(1)}, u32[]{:S(2)}, u32[]{:S(2)}) collective-permute-start(bf16[256,768]{1,0:T(8,128)(2,1)S(1)} %pair_sum.1), channel_id=1, source_target_pairs={{0,384},{128,256},{256,128},{384,0},{1,385},{129,257},{257,129},{3... | collective-permute-start | bytes 1179656 | tf_op jit(solution)/shard_map/ppermute | solution.py:301

commit v11 on v10

--- a/solution.py
+++ b/solution.py
@@ -36,7 +36,7 @@
         name=name,
         out_shape=out_shape,
         in_specs=in_specs,
-        out_specs=jax.tree.map(lambda _: out, out_shape),
+        out_specs=out if isinstance(out, list) else jax.tree.map(lambda _: out, out_shape),
         scratch_shapes=list(scratch),
         compiler_params=pltpu.CompilerParams(vmem_limit_bytes=vmem),
         cost_estimate=pl.CostEstimate(
@@ -99,18 +99,17 @@
     hit = jnp.broadcast_to(place[:, None, :], (experts, MSG, lanes)) == slot
     scaled = jnp.where(hit, jnp.broadcast_to(weight[:, None, :], hit.shape), 0.0)
     scaled = scaled.reshape(experts * MSG, lanes).astype(BF16)
+    pick = jnp.where(hit, 1.0, 0.0).reshape(experts * MSG, lanes).astype(BF16)
+    pick_t[...] = dot(identity(lanes), pick, NT).astype(BF16)
+    departures = start_all([pltpu.make_async_copy(pick_t, pick_hbm, out_sems.at[CHUNKS])])
     for copy in copies[4:]:
         copy.wait()
     part = send.shape[0] // CHUNKS
-    departures = []
     for n in range(CHUNKS):
         at = pl.ds(n * part, part)
         block = dot(scaled[n * part : (n + 1) * part, :], both[...], NN)
         send[at, :] = block.astype(BF16)
         departures += start_all([pltpu.make_async_copy(send.at[at], send_hbm.at[at], out_sems.at[n])])
-    pick = jnp.where(hit, 1.0, 0.0).reshape(experts * MSG, lanes).astype(BF16)
-    pick_t[...] = dot(identity(lanes), pick, NT).astype(BF16)
-    departures += start_all([pltpu.make_async_copy(pick_t, pick_hbm, out_sems.at[CHUNKS])])
     wait_all(departures)
 
 def token_body(pick_t, returned, out):
@@ -129,25 +128,17 @@
         copy.wait()
 
 def expert_body(
-    ranks, me, recv_hbm, w_gate_hbm, w_up_hbm, w_down_hbm,
-    back_hbm, down_out_hbm, send_hbm, keep_hbm, back, down_out, send, keep,
-    recv, w_in, w_down, wide, narrow, tok, og, pre, grad, in_rows, hid, total, in_sems, out_sems,
+    ranks, me, recv, w_gate_hbm, w_up_hbm, w_down_hbm,
+    back_hbm, down_out, send, keep, back,
+    w_in, w_down, wide, narrow, tok, og, pre, grad, in_rows, hid, total, in_sems, out_sem,
 ):
     rows_in, features = recv.shape
     hidden = w_down.shape[0]
     peers = rows_in // MSG
     half = features // 2
-    step = rows_in // CHUNKS
-    chunks = [pl.ds(n * step, step) for n in range(CHUNKS)]
-    arrivals = start_all(
-        [
-            pltpu.make_async_copy(recv_hbm.at[at], recv.at[at], in_sems.at[n])
-            for n, at in enumerate(chunks)
-        ]
-    )
     weights = start_all(
         [
-            pltpu.make_async_copy(source, target, in_sems.at[CHUNKS + n])
+            pltpu.make_async_copy(source, target, in_sems.at[n])
             for n, (source, target) in enumerate(
                 [
                     (w_gate_hbm, w_in.at[:, pl.ds(0, hidden)]),
@@ -157,16 +148,8 @@
             )
         ]
     )
-    departures = []
-
-    def send_out(source, target):
-        copy = pltpu.make_async_copy(source, target, out_sems.at[len(departures)])
-        departures.extend(start_all([copy]))
-
-    for copy, at in zip(arrivals, chunks):
-        copy.wait()
-        for c in range(features // LANES):
-            wide[c, at, :] = recv[at, c * LANES : (c + 1) * LANES].astype(F32)
+    for c in range(features // LANES):
+        wide[c] = recv[:, c * LANES : (c + 1) * LANES].astype(F32)
     for s in range(SLOTS):
         at = pl.ds(s * peers, peers)
         for c in range(features // LANES):
@@ -195,7 +178,7 @@
             narrow[c, pl.ds(s + SLOTS, peers, MSG), :] = high
     for c in range(half // LANES):
         back[:, c * LANES : (c + 1) * LANES] = narrow[c].astype(BF16)
-    send_out(back, back_hbm)
+    departures = start_all([pltpu.make_async_copy(back, back_hbm, out_sem)])
     total[...] = dot(tok[...], in_rows[...], TN)
     piece = features // ranks
     even = me[0] + 1 - 2 * lax.rem(me[0], 2)
@@ -205,12 +188,9 @@
 
     send[:, : 2 * hidden] = part_of(ranks - 1 - even)
     send[:, 2 * hidden :] = part_of(even)
-    send_out(send, send_hbm)
     keep[:, : 2 * hidden] = part_of(ranks - 1 - me[0])
     keep[:, 2 * hidden :] = part_of(me[0])
-    send_out(keep, keep_hbm)
     down_out[...] = dot(hid[...], og[...], TN).astype(BF16)
-    send_out(down_out, down_out_hbm)
     wait_all(departures)
 
 def add(kept, received):
@@ -269,10 +249,9 @@
         functools.partial(expert_body, ranks),
         "expert",
         out,
-        [SMEM] + [ANY] * 4,
-        [pltpu.VMEM(a.shape, a.dtype) for a in out]
+        [SMEM, VMEM] + [ANY] * 3,
+        [pltpu.VMEM(out[0].shape, BF16)]
         + [
-            pltpu.VMEM((total, features), BF16),
             pltpu.VMEM((features, 2 * hidden), BF16),
             pltpu.VMEM((hidden, features), BF16),
             pltpu.VMEM((features // LANES, total, LANES), F32),
@@ -284,13 +263,13 @@
             pltpu.VMEM((rows, 2 * hidden), BF16),
             pltpu.VMEM((rows, hidden), BF16),
             pltpu.VMEM((features, 2 * hidden), F32),
-            pltpu.SemaphoreType.DMA((CHUNKS + 3,)),
-            pltpu.SemaphoreType.DMA((len(out),)),
+            pltpu.SemaphoreType.DMA((3,)),
+            pltpu.SemaphoreType.DMA(()),
         ],
         16 * rows * features * hidden,
         2 * (total * features * 2 + 6 * features * hidden),
         44 * MIB,
-        ANY,
+        [ANY] + [VMEM] * 3,
     )(me, recv, w_gate[0], w_up[0], w_down[0])
     returned = lax.all_to_all(back, "expert", split_axis=0, concat_axis=0, tiled=True)
 

time: 127 us -> 128 us (level)
  no operation moved by 1% of the time
where the time goes in v11:
time: 128 us
  blocking collectives  70.7 us (55%)
  starting transfers between devices  21.1 us (16%)
  waiting for transfers between devices  20.7 us (16%)
  Pallas kernels  14.5 us (11%)
    all_to_all x1, blocking collectives, shards(): lax.all_to_all(send, 'expert', split_axis=0, concat_axis=0, tiled=True)  70.7 us
    ppermute x2, waiting for transfers between devices, mirror(): return lax.ppermute(value, 'dp', [(i, ranks - 1 - i) for i in range(ranks)])  14.5 us
    ppermute x2, starting transfers between devices, mirror(): return lax.ppermute(value, 'dp', [(i, ranks - 1 - i) for i in range(ranks)])  8.91 us
    all_to_all x1, starting transfers between devices, shards(): lax.all_to_all(back, 'expert', split_axis=0, concat_axis=0, tiled=True)  8.3 us
    pallas_call x1, Pallas kernels, shards(): call(functools.partial(expert_body, ranks), 'expert', out, [SMEM, VMEM] +...  7.25 us
    ppermute x2, waiting for transfers between devices, even(): return lax.ppermute(value, 'dp', [(i, i ^ 1) for i in range(ranks)])  4.49 us
    ppermute x2, starting transfers between devices, even(): return lax.ppermute(value, 'dp', [(i, i ^ 1) for i in range(ranks)])  3.84 us
    pallas_call x4, Pallas kernels, small(): call(body, name, out, [VMEM] * len(operands), flops=work, bytes_accessed=...  3.29 us
  transfers between devices with their start and end apart: 5, of which 4 were waited for; matrix products, arithmetic and copies ran while one was open for 0% of the time, Pallas kernels for 3%

profile of v11, /device:TPU:1, one launch (start us, length us, event | category | flops | bytes accessed | tf_op | source)
XLA Modules:
  0.0 127.7 jit_solution(14661896761030016209)
XLA Ops:
  0.6 3.1 %dispatch.1 = (bf16[1024,1024]{1,0:T(8,128)(2,1)}, bf16[64,1024]{1,0:T(8,128)(2,1)}) custom-call(bf16[32,1024]{1,0:T(8,128)(2,1)} %tok_hbm.1, bf16[32,1024]{1,0:T(8,128)(2,1)} %cot_hbm.1, s32[8,32]{1,0:T(8,128)} %bitcast.22, bf16[8,32]{1,0:T(8,128)(2,1)} %bitcast.23, s32[4]{0:T(128)} %hot_hbm, s32[4]{0:T(128)} %extra_hbm.1), custom_call_target="tpu_custom_call" | custom-call | flops 134217728 | bytes 2097152 | tf_op jit(solution)/shard_map/dispatch/pallas_call | solution.py:218
  3.7 0.0 copy-start.1
  3.7 0.0 copy-start.2
  3.7 0.0 copy-start.3
  3.8 70.7 %all_to_all.22 = bf16[128,8,1024]{2,1,0:T(8,128)(2,1)S(1)} all-to-all(bf16[128,8,1024]{2,1,0:T(8,128)(2,1)} %bitcast.18), channel_id=1, replica_groups=mesh['dp'=4,'expert'=128] {'expert'}, dimensions={0} | all-to-all | bytes 4194304 | tf_op jit(solution)/shard_map/all_to_all | solution.py:242
  74.5 0.0 copy-done.1
  74.5 0.0 copy-done.2
  74.5 0.0 copy-done.3
  74.5 7.2 %expert.1 = (bf16[1024,512]{1,0:T(8,128)(2,1)}, bf16[384,1024]{1,0:T(8,128)(2,1)S(1)}, bf16[256,1536]{1,0:T(8,128)(2,1)}, bf16[256,1536]{1,0:T(8,128)(2,1)S(1)}) custom-call(s32[1]{0:T(128)} %bitcast.2.me, bf16[1024,1024]{1,0:T(8,128)(2,1)S(1)} %bitcast.14, bf16[1024,384]{1,0:T(8,128)(2,1)S(1)} %bitcast.15, bf16[1024,384]{1,0:T(8,128)(2,1)S(1)} %bitcast.16, ...), custom_call_target="tpu_custom_call" | custom-call | flops 3221225472 | bytes 8912896 | tf_op jit(solution)/shard_map/expert/pallas_call | solution.py:248
  81.7 4.4 %collective-permute-start.2 = (bf16[384,1024]{1,0:T(8,128)(2,1)S(1)}, bf16[384,1024]{1,0:T(8,128)(2,1)}, u32[]{:S(2)}, u32[]{:S(2)}) collective-permute-start(bf16[384,1024]{1,0:T(8,128)(2,1)S(1)} %get-tuple-element.23.kept), channel_id=1, source_target_pairs={{0,384},{128,256},{256,128},{384,0},{1,385},{129,257},{257,129},{3... | collective-permute-start | bytes 2359304 | tf_op jit(solution)/shard_map/ppermute | solution.py:280
  86.1 1.9 %collective-permute-start = (bf16[256,1536]{1,0:T(8,128)(2,1)}, bf16[256,1536]{1,0:T(8,128)(2,1)S(1)}, u32[]{:S(2)}, u32[]{:S(2)}) collective-permute-start(bf16[256,1536]{1,0:T(8,128)(2,1)} %get-tuple-element.20), channel_id=1, source_target_pairs={{0,128},{128,0},{256,384},{384,256},{1,129},{129,1},{257,385},{385... | collective-permute-start | bytes 2359304 | tf_op jit(solution)/shard_map/ppermute | solution.py:277
  88.0 8.3 %all-to-all-start.1 = ((bf16[128,8,512]{2,1,0:T(8,128)(2,1)}), bf16[128,8,512]{2,1,0:T(8,128)(2,1)S(1)}, u32[]{:S(2)}, u32[]{:S(2)}) async-start(bf16[128,8,512]{2,1,0:T(8,128)(2,1)} %bitcast.8), calls=%async_computation.1 | async-start | bytes 2097152 | tf_op jit(solution)/shard_map/all_to_all | solution.py:274
  96.4 7.0 %collective-permute-done.2.received = bf16[384,1024]{1,0:T(8,128)(2,1)} collective-permute-done((bf16[384,1024]{1,0:T(8,128)(2,1)S(1)}, bf16[384,1024]{1,0:T(8,128)(2,1)}, u32[]{:S(2)}, u32[]{:S(2)}) %collective-permute-start.2) | collective-permute-done | bytes 786464 | tf_op jit(solution)/shard_map/ppermute | solution.py:280
  103.4 1.3 %down_sum.1.kept = bf16[384,1024]{1,0:T(8,128)(2,1)S(1)} custom-call(bf16[384,1024]{1,0:T(8,128)(2,1)S(1)} %get-tuple-element.23.kept, bf16[384,1024]{1,0:T(8,128)(2,1)} %collective-permute-done.2.received), custom_call_target="tpu_custom_call" | custom-call | bytes 2359296 | tf_op jit(solution)/shard_map/down_sum/pallas_call | solution.py:284
  104.7 1.9 %collective-permute-start.3 = (bf16[384,1024]{1,0:T(8,128)(2,1)S(1)}, bf16[384,1024]{1,0:T(8,128)(2,1)S(1)}, u32[]{:S(2)}, u32[]{:S(2)}) collective-permute-start(bf16[384,1024]{1,0:T(8,128)(2,1)S(1)} %down_sum.1.kept), channel_id=1, source_target_pairs={{0,128},{128,0},{256,384},{384,256},{1,129},{129,1},{257,385},{385... | collective-permute-start | bytes 2359304 | tf_op jit(solution)/shard_map/ppermute | solution.py:277
  106.6 0.0 collective-permute-done.received.first
  106.6 0.1 pair_sum.1
  106.7 4.5 %collective-permute-start.1 = (bf16[256,768]{1,0:T(8,128)(2,1)S(1)}, bf16[256,768]{1,0:T(8,128)(2,1)S(1)}, u32[]{:S(2)}, u32[]{:S(2)}) collective-permute-start(bf16[256,768]{1,0:T(8,128)(2,1)S(1)} %pair_sum.1), channel_id=1, source_target_pairs={{0,384},{128,256},{256,128},{384,0},{1,385},{129,257},{257,129},{3... | collective-permute-start | bytes 1179656 | tf_op jit(solution)/shard_map/ppermute | solution.py:280
  111.2 7.5 %collective-permute-done.1.second = bf16[256,768]{1,0:T(8,128)(2,1)S(1)} collective-permute-done((bf16[256,768]{1,0:T(8,128)(2,1)S(1)}, bf16[256,768]{1,0:T(8,128)(2,1)S(1)}, u32[]{:S(2)}, u32[]{:S(2)}) %collective-permute-start.1) | collective-permute-done | bytes 393248 | tf_op jit(solution)/shard_map/ppermute | solution.py:280
  118.8 0.8 pair.1
  119.6 4.5 %collective-permute-done.3.received = bf16[384,1024]{1,0:T(8,128)(2,1)S(1)} collective-permute-done((bf16[384,1024]{1,0:T(8,128)(2,1)S(1)}, bf16[384,1024]{1,0:T(8,128)(2,1)S(1)}, u32[]{:S(2)}, u32[]{:S(2)}) %collective-permute-start.3) | collective-permute-done | bytes 786464 | tf_op jit(solution)/shard_map/ppermute | solution.py:277
  124.1 1.1 down.1
  125.1 1.7 %all-to-all-done.1 = bf16[128,8,512]{2,1,0:T(8,128)(2,1)S(1)} async-done(((bf16[128,8,512]{2,1,0:T(8,128)(2,1)}), bf16[128,8,512]{2,1,0:T(8,128)(2,1)S(1)}, u32[]{:S(2)}, u32[]{:S(2)}) %all-to-all-start.1) | async-done | bytes 1048608 | tf_op jit(solution)/shard_map/all_to_all | solution.py:274
  126.8 0.9 token_grad.1
  (2 shorter events, 0.0 us)
Async XLA Ops:
  3.7 70.7 %copy-start.1 = (bf16[1,1024,384]{2,1,0:T(8,128)(2,1)S(1)}, bf16[1,1024,384]{2,1,0:T(8,128)(2,1)}, u32[]{:S(2)}) copy-start(bf16[1,1024,384]{2,1,0:T(8,128)(2,1)} %param.15) | copy-start | bytes 2359300
  3.7 70.7 %copy-start.2 = (bf16[1,1024,384]{2,1,0:T(8,128)(2,1)S(1)}, bf16[1,1024,384]{2,1,0:T(8,128)(2,1)}, u32[]{:S(2)}) copy-start(bf16[1,1024,384]{2,1,0:T(8,128)(2,1)} %param.16) | copy-start | bytes 2359300
  3.7 70.7 %copy-start.3 = (bf16[1,384,1024]{2,1,0:T(8,128)(2,1)S(1)}, bf16[1,384,1024]{2,1,0:T(8,128)(2,1)}, u32[]{:S(2)}) copy-start(bf16[1,384,1024]{2,1,0:T(8,128)(2,1)} %param.17) | copy-start | bytes 2359300
  81.7 21.6 %collective-permute-start.2 = (bf16[384,1024]{1,0:T(8,128)(2,1)S(1)}, bf16[384,1024]{1,0:T(8,128)(2,1)}, u32[]{:S(2)}, u32[]{:S(2)}) collective-permute-start(bf16[384,1024]{1,0:T(8,128)(2,1)S(1)} %get-tuple-element.23.kept), channel_id=1, source_target_pairs={{0,384},{128,256},{256,128},{384,0},{1,385},{129,257},{257,129},{3... | collective-permute-start | bytes 2359304 | tf_op jit(solution)/shard_map/ppermute | solution.py:280
  86.1 20.5 %collective-permute-start = (bf16[256,1536]{1,0:T(8,128)(2,1)}, bf16[256,1536]{1,0:T(8,128)(2,1)S(1)}, u32[]{:S(2)}, u32[]{:S(2)}) collective-permute-start(bf16[256,1536]{1,0:T(8,128)(2,1)} %get-tuple-element.20), channel_id=1, source_target_pairs={{0,128},{128,0},{256,384},{384,256},{1,129},{129,1},{257,385},{385... | collective-permute-start | bytes 2359304 | tf_op jit(solution)/shard_map/ppermute | solution.py:277
  88.0 38.7 %all-to-all-start.1 = ((bf16[128,8,512]{2,1,0:T(8,128)(2,1)}), bf16[128,8,512]{2,1,0:T(8,128)(2,1)S(1)}, u32[]{:S(2)}, u32[]{:S(2)}) async-start(bf16[128,8,512]{2,1,0:T(8,128)(2,1)} %bitcast.8), calls=%async_computation.1 | async-start | bytes 2097152 | tf_op jit(solution)/shard_map/all_to_all | solution.py:274
  104.7 19.4 %collective-permute-start.3 = (bf16[384,1024]{1,0:T(8,128)(2,1)S(1)}, bf16[384,1024]{1,0:T(8,128)(2,1)S(1)}, u32[]{:S(2)}, u32[]{:S(2)}) collective-permute-start(bf16[384,1024]{1,0:T(8,128)(2,1)S(1)} %down_sum.1.kept), channel_id=1, source_target_pairs={{0,128},{128,0},{256,384},{384,256},{1,129},{129,1},{257,385},{385... | collective-permute-start | bytes 2359304 | tf_op jit(solution)/shard_map/ppermute | solution.py:277
  106.7 20.1 %copy-start = (bf16[64,1024]{1,0:T(8,128)(2,1)S(1)}, bf16[64,1024]{1,0:T(8,128)(2,1)}, u32[]{:S(2)}) copy-start(bf16[64,1024]{1,0:T(8,128)(2,1)} %get-tuple-element.15.pick_t) | copy-start | bytes 393220
  106.7 12.0 %collective-permute-start.1 = (bf16[256,768]{1,0:T(8,128)(2,1)S(1)}, bf16[256,768]{1,0:T(8,128)(2,1)S(1)}, u32[]{:S(2)}, u32[]{:S(2)}) collective-permute-start(bf16[256,768]{1,0:T(8,128)(2,1)S(1)} %pair_sum.1), channel_id=1, source_target_pairs={{0,384},{128,256},{256,128},{384,0},{1,385},{129,257},{257,129},{3... | collective-permute-start | bytes 1179656 | tf_op jit(solution)/shard_map/ppermute | solution.py:280
